TPU v7x, 32 devices: a whole 2x2x4 slice. The times are simulated.
32 devices in a mesh: groups: 2 (over y), corpus: 4 (over z), layer: 4 (over x, core).
Axes of the slice: x: 2, y: 2, z: 4, core: 2. Of those that a mesh axis runs over, the one named last changes fastest.
Arguments:
- query_acts: bfloat16 [64, 4, 16, 4096], P(('groups', 'corpus'), 'layer'), parts along dimension 0, may hold values from -6 to 6
- query_outgrads: bfloat16 [64, 4, 16, 4096], P(('groups', 'corpus'), 'layer'), parts along dimension 0, may hold values from -6 to 6
- in_project: bfloat16 [4, 64, 4096], P('layer', None, 'corpus'), may hold values from -0.09375 to 0.09375
- out_project: bfloat16 [4, 64, 4096], P('layer', None, 'corpus'), may hold values from -0.09375 to 0.09375
- in_basis: float32 [4, 64, 64], P('layer'), may hold values from -0.75 to 0.75
- out_basis: float32 [4, 64, 64], P('layer'), may hold values from -0.75 to 0.75
- eig_values: float32 [4, 4096], P('layer'), may hold values from 0.05 to 5
- train_grads: bfloat16 [2560, 4, 4096], P(('groups', 'corpus'), 'layer'), parts along dimension 0, may hold values from -0.099609375 to 0.099609375
Outputs:
- scores: float32 [2560, 32], P(('groups', 'corpus', 'layer')), parts along dimension 0
There are 2 independent parts, one for each index of `groups`. A program takes and returns all parts, laid end to end along the dimension named above; an argument that names none is the same for every part. Nothing has to cross between parts.
All inputs are finite; a program needn't handle non-finite values.
Results may differ from a plain program's by a relative error of at most 0.0059.
Values may be sent and summed in bfloat16 or wider, within the bound.
No kernel may reach another device: no remote copies, remote signals or barrier semaphores. Data moves between devices by JAX's collectives and lax.ppermute only.
A program may use at most 64 MiB of HBM per device.

v0:
```python
import jax
import jax.numpy as jnp
from jax import lax
from jax.sharding import PartitionSpec as P

damping = 0.1


def condition(grads, out_basis, in_basis, inverse):
    count, layers, width = grads.shape
    rank = out_basis.shape[-1]
    highest = lax.Precision.HIGHEST
    square = grads.astype(jnp.float32).reshape(count, layers, rank, rank)
    turned = jnp.einsum("lab,nlad->nlbd", out_basis, square, precision=highest)
    turned = jnp.einsum("nlbd,ldc->nlbc", turned, in_basis, precision=highest)
    scaled = turned * inverse.reshape(1, layers, rank, rank)
    back = jnp.einsum("lab,nlbc->nlac", out_basis, scaled, precision=highest)
    back = jnp.einsum("nlac,ldc->nlad", back, in_basis, precision=highest)
    return back.reshape(count, layers, width).astype(jnp.bfloat16)


def body(
    query_acts,
    query_outgrads,
    in_project,
    out_project,
    in_basis,
    out_basis,
    eig_values,
    train_grads,
):
    queries_here, layers_here, token_count, _ = query_acts.shape
    rank = in_project.shape[1]
    in_total = jnp.einsum(
        "qlsd,lrd->qlsr",
        query_acts,
        lax.all_gather(in_project, "corpus", axis=2, tiled=True),
        preferred_element_type=jnp.float32,
    )
    out_total = jnp.einsum(
        "qlsd,lrd->qlsr",
        query_outgrads,
        lax.all_gather(out_project, "corpus", axis=2, tiled=True),
        preferred_element_type=jnp.float32,
    )
    in_side = in_total.astype(jnp.bfloat16)
    out_side = out_total.astype(jnp.bfloat16)
    projected = (
        jnp.einsum("qlsa,qlsc->qlac", out_side, in_side, preferred_element_type=jnp.float32)
        / token_count
    )
    projected = projected.astype(jnp.bfloat16).reshape(queries_here, layers_here, rank * rank)
    inverse = 1.0 / (eig_values + damping)
    outgoing = condition(projected, out_basis, in_basis, inverse)
    partial_scores = jnp.einsum(
        "nlf,qlf->nq",
        train_grads,
        lax.all_gather(outgoing, "corpus", axis=0, tiled=True),
        preferred_element_type=jnp.float32,
    )
    return lax.psum_scatter(partial_scores, "layer", scatter_dimension=0, tiled=True)


def solution(mesh):
    placed = (
        P(("groups", "corpus"), "layer", None, None),
        P(("groups", "corpus"), "layer", None, None),
        P("layer", None, "corpus"),
        P("layer", None, "corpus"),
        P("layer", None, None),
        P("layer", None, None),
        P("layer", None),
        P(("groups", "corpus"), "layer", None),
    )
    return jax.shard_map(
        body,
        mesh=mesh,
        in_specs=placed,
        out_specs=P(("groups", "corpus", "layer"), None),
        check_vma=False,
    )
```

profile of v0, /device:TPU:0, one launch (start us, length us, event | category | flops | bytes accessed | tf_op | source)
XLA Modules:
  0.0 92.4 jit_solution(9037907821232982887)
XLA Ops:
  6.5 0.0 copy-start
  6.5 0.0 copy-start.1
  6.5 0.0 reduce-scatter.4.cloned.1.call-start
  6.5 17.7 %all_gather.9 = bf16[1,64,4096]{2,1,0:T(8,128)(2,1)S(1)} all-gather(bf16[1,64,1024]{2,1,0:T(8,128)(2,1)} %param.11), channel_id=1, replica_groups=mesh['groups'=2,'corpus'=4,'layer'=4] {'corpus'}, dimensions={2}, use_global_device_ids=true | all-gather | bytes 655360 | tf_op jit(solution)/shard_map/all_gather | solution.py:43
  24.2 0.0 copy-start.2
  24.2 17.8 %all_gather.10 = bf16[1,64,4096]{2,1,0:T(8,128)(2,1)} all-gather(bf16[1,64,1024]{2,1,0:T(8,128)(2,1)} %param.10), channel_id=1, replica_groups=mesh['groups'=2,'corpus'=4,'layer'=4] {'corpus'}, dimensions={2}, use_global_device_ids=true | all-gather | bytes 655360 | tf_op jit(solution)/shard_map/all_gather | solution.py:37
  42.1 0.8 divide_reduce_fusion
  42.8 0.1 mul.10
  42.9 1.6 %fusion.9 = bf16[8,16,64]{2,1,0:T(8,128)(2,1)S(1)} fusion(bf16[8,1,16,4096]{3,2,1,0:T(8,128)(2,1)} %param.9, bf16[1,64,4096]{2,1,0:T(8,128)(2,1)S(1)} %all_gather.9), kind=kOutput, calls=%fused_computation.14 | convolution fusion | flops 67117056 | bytes 1589248 | tf_op jit(solution)/shard_map/qlsd,lrd->qlsr/dot_general | solution.py:40
  44.6 2.1 %fusion.4 = bf16[8,64,64]{1,2,0:T(8,128)(2,1)S(1)} fusion(bf16[8,16,64]{2,1,0:T(8,128)(2,1)S(1)} %fusion.9, bf16[8,1,16,4096]{3,2,1,0:T(8,128)(2,1)} %param.8, bf16[1,64,4096]{2,1,0:T(8,128)(2,1)} %all_gather.10), kind=kOutput, calls=%fused_computation.8 | convolution fusion | flops 68231168 | bytes 1654784 | tf_op jit(solution)/shard_map/qlsa,qlsc->qlac/dot_general | solution.py:49
  46.6 0.0 copy-done.1
  46.6 0.2 convolution_bitcast_fusion.2
  46.9 0.0 copy-done.2
  46.9 0.6 fusion.3
  47.5 0.6 convolution_bitcast_fusion
  48.1 0.6 fusion.5
  48.7 0.2 convert_element_type.57
  48.9 13.8 %all_gather.11 = bf16[32,1,4096]{2,0,1:T(8,128)(2,1)S(1)} all-gather(bf16[8,1,4096]{2,0,1:T(8,128)(2,1)S(1)} %convert_element_type.57), channel_id=1, replica_groups=mesh['groups'=2,'corpus'=4,'layer'=4] {'corpus'}, dimensions={0}, use_global_device_ids=true | all-gather | bytes 327680 | tf_op jit(solution)/shard_map/all_gather | solution.py:58
  62.7 0.0 copy-done
  62.7 0.8 fusion.6
  63.5 0.8 copy.18
  64.3 0.0 reduce-scatter.4.cloned.1.call-update
  64.3 19.8 %reduce-scatter.4.cloned.1.call-done = f32[80,32]{1,0:T(8,128)} async-done(((f32[320,32]{1,0:T(8,128)}), f32[80,32]{1,0:T(8,128)}) %reduce-scatter.4.cloned.1.call-update) | async-done | bytes 10256
  84.1 1.5 %copy.19 = f32[80,32]{0,1:T(8,128)} copy(f32[80,32]{1,0:T(8,128)} %reduce-scatter.4.cloned.1.call-done) | data formatting | bytes 20480
Async XLA Ops:
  6.5 56.1 %copy-start = (bf16[320,1,4096]{2,0,1:T(8,128)(2,1)S(1)}, bf16[320,1,4096]{2,0,1:T(8,128)(2,1)}, u32[]{:S(2)}) copy-start(bf16[320,1,4096]{2,0,1:T(8,128)(2,1)} %param.15) | copy-start | bytes 7864324
  6.5 40.1 %copy-start.1 = (f32[1,64,64]{2,1,0:T(8,128)S(1)}, f32[1,64,64]{2,1,0:T(8,128)}, u32[]{:S(2)}) copy-start(f32[1,64,64]{2,1,0:T(8,128)} %param.13) | copy-start | bytes 49156
  6.5 77.5 %reduce-scatter.4.cloned.1.call-start = ((), (), s32[]{:S(2)}) async-start(), calls=%async_computation.1 | async-start | bytes 204800
  24.2 22.7 %copy-start.2 = (f32[1,64,64]{2,1,0:T(8,128)S(1)}, f32[1,64,64]{2,1,0:T(8,128)}, u32[]{:S(2)}) copy-start(f32[1,64,64]{2,1,0:T(8,128)} %param.12) | copy-start | bytes 49156
Sparse Core Ops, SparseCore 0:
  64.4 19.5 reduce-scatter.3
where the time goes:
time: 92.8 us; the launch traced here: 92.4 us
  blocking collectives  49.3 us (53%)
  waiting for transfers between devices  19.8 us (21%)
  between operations  13.5 us (15%)
  matrix products  6.55 us (7%)
  local copies, waits for them, and re-layouts  2.51 us (3%)
    unnamed x2, waiting for transfers between devices  19.8 us
    all_gather x1, blocking collectives, body(): lax.all_gather(in_project, 'corpus', axis=2, tiled=True)  17.8 us
    all_gather x1, blocking collectives, body(): lax.all_gather(out_project, 'corpus', axis=2, tiled=True)  17.7 us
    all_gather x1, blocking collectives, body(): lax.all_gather(outgoing, 'corpus', axis=0, tiled=True)  13.8 us
    unnamed x8, local copies, waits for them, and re-layouts  2.27 us
    dot_general x1, matrix products, body(): jnp.einsum('qlsa,qlsc->qlac', out_side, in_side, preferred_element_type=j...  2.07 us
  transfers between devices with their start and end apart: 1, of which 1 were waited for; matrix products, arithmetic and copies ran while one was open for 0% of the time, Pallas kernels for 0%

commit v1 on v0

v1 whole, which is shorter than its diff:
```python
import functools

import jax
import jax.numpy as jnp
from jax import lax
from jax.experimental import pallas as pl
from jax.experimental.pallas import tpu as pltpu
from jax.sharding import PartitionSpec as P

damping = 0.1
f32 = jnp.float32
bf16 = jnp.bfloat16
lanes = 256
nt = (((1,), (1,)), ((), ()))
tn = (((0,), (0,)), ((), ()))
vmem = pl.BlockSpec(memory_space=pltpu.VMEM)


def dot(a, b, dims=(((1,), (0,)), ((), ()))):
    return lax.dot_general(a, b, dims, preferred_element_type=f32)


def split(x):
    high = x.astype(bf16)
    return high, (x - high.astype(f32)).astype(bf16)


def tiled_diagonal(x, blocks):
    n = x.shape[0]
    wide = jnp.concatenate([x] * blocks, axis=1)
    tall = jnp.concatenate([wide] * blocks, axis=0)
    row = lax.broadcasted_iota(jnp.int32, tall.shape, 0) // n
    column = lax.broadcasted_iota(jnp.int32, tall.shape, 1) // n
    return jnp.where(row == column, tall, 0.0)


def product3(x, high, low):
    x_high, x_low = split(x)
    return dot(x_high, high) + (dot(x_low, high) + dot(x_high, low))


def sides_kernel(steps, acts, outgrads, *refs):
    group = lax.axis_index("groups")
    place = lax.axis_index("corpus")
    pieces, sides = refs[:-1], refs[-1]
    rank = pieces[0].shape[0]
    width = pieces[0].shape[1]
    in_total = jnp.zeros((acts.shape[0], rank), f32)
    out_total = jnp.zeros((acts.shape[0], rank), f32)
    for at, (shift, swapped) in enumerate(steps):
        first, second = pieces[2 * at][...], pieces[2 * at + 1][...]
        if swapped:
            first, second = jnp.where(group == 0, first, second), jnp.where(group == 0, second, first)
        if width == acts.shape[1]:
            columns = slice(None)
        else:
            columns = pl.ds(pl.multiple_of((place ^ shift) * width, 128), width)
        in_total += dot(acts[:, columns], first, nt)
        out_total += dot(outgrads[:, columns], second, nt)
    sides[...] = jnp.concatenate([out_total, in_total], axis=1).astype(bf16)


def scores_kernel(sources, tokens, in_basis, out_basis, eigen, train, *refs):
    blocks, outs, (scratch, rows) = refs[:sources], refs[sources:-2], refs[-2:]
    rank = in_basis.shape[0]
    across = lanes // rank
    here = blocks[0].shape[0] // tokens
    queries = here * sources
    groups = queries // across
    u_in, u_out = in_basis[...], out_basis[...]
    inverse = 1.0 / (eigen[...] + damping)
    inverse = jnp.concatenate([inverse] * across, axis=1)
    out_high, out_low = split(u_out)
    turn = jnp.concatenate([out_high, out_low], axis=0)
    back = jnp.concatenate([out_high, out_low, out_high], axis=1)
    in_high, in_low = split(tiled_diagonal(u_in, across))
    tin_high, tin_low = split(tiled_diagonal(u_in.T, across))
    mask = (
        lax.broadcasted_iota(jnp.int32, (across * tokens, lanes), 0) // tokens
        == lax.broadcasted_iota(jnp.int32, (across * tokens, lanes), 1) // rank
    )
    parts = [[] for _ in range(groups)]
    for group in range(groups):
        for j in range(across):
            query = j * groups + group
            start = query % here * tokens
            parts[group].append(blocks[query // here][start : start + tokens, :])
    turned = []
    for group in range(groups):
        both = jnp.concatenate(parts[group], axis=0)
        out_side = both[:, :rank]
        in_side = jnp.concatenate([both[:, rank:]] * across, axis=1)
        in_side = jnp.where(mask, in_side, jnp.zeros_like(in_side))
        gradient = (dot(out_side, in_side, tn) * (1.0 / tokens)).astype(bf16)
        turned.append(dot(turn, jnp.concatenate([gradient, gradient], axis=0), tn))
    turned = jnp.concatenate(turned, axis=0)
    turned = product3(turned, in_high, in_low)
    scaled = []
    for group in range(groups):
        part = turned[group * rank : (group + 1) * rank] * inverse
        high, low = split(part)
        scaled.append(dot(back, jnp.concatenate([high, high, low], axis=0)))
    scaled = jnp.concatenate(scaled, axis=0)
    conditioned = product3(scaled, tin_high, tin_low)
    for part in range(lanes // 128):
        scratch[part] = conditioned[:, part * 128 : (part + 1) * 128]
    for pair in range(rank // 2):
        for part in range(lanes // 128):
            even = scratch[part, pl.ds(2 * pair, groups, stride=rank), :]
            odd = scratch[part, pl.ds(2 * pair + 1, groups, stride=rank), :]
            columns = slice(2 * pair * rank, 2 * (pair + 1) * rank)
            for half in range(2):
                j = 2 * part + half
                cut = slice(half * rank, (half + 1) * rank)
                rows[j * groups : (j + 1) * groups, columns] = jnp.concatenate(
                    [even[:, cut], odd[:, cut]], axis=1
                )
    result = dot(train[...], rows[...].astype(bf16), nt)
    scored = result.T
    for at, out in enumerate(outs):
        out[...] = scored


def body(
    query_acts,
    query_outgrads,
    in_project,
    out_project,
    in_basis,
    out_basis,
    eig_values,
    train_grads,
):
    queries_here, _, tokens, model = query_acts.shape
    rank, width = in_project.shape[1:]
    places = model // width
    layers = lax.axis_size("layer")
    acts = query_acts.reshape(queries_here * tokens, model)
    outgrads = query_outgrads.reshape(queries_here * tokens, model)
    in_own, out_own = in_project[0], out_project[0]

    def far(x, shift):
        return lax.ppermute(x, "corpus", [(i, i ^ shift) for i in range(places)])

    if places == 4 and lax.axis_size("groups") == 2:
        half = jnp.where(lax.axis_index("groups") == 0, in_own, out_own)
        steps, pieces = [(0, False)], [in_own, out_own]
        for shift in (3, 2):
            got = far(half, shift)
            other = lax.ppermute(got, "groups", [(0, 1), (1, 0)])
            steps.append((shift, True))
            pieces += [got, other]
        steps.append((1, False))
        pieces += [far(in_own, 1), far(out_own, 1)]
    else:
        steps = [(0, False)]
        pieces = [lax.all_gather(x, "corpus", axis=1, tiled=True) for x in (in_own, out_own)]
    sides = pl.pallas_call(
        functools.partial(sides_kernel, steps),
        out_shape=jax.ShapeDtypeStruct((queries_here * tokens, 2 * rank), bf16),
        in_specs=[vmem] * (2 + len(pieces)),
        out_specs=vmem,
        name="sides",
    )(acts, outgrads, *pieces)

    eigen = eig_values.reshape(rank, rank)
    train = train_grads.reshape(train_grads.shape[0], rank * rank)
    rows_here = train.shape[0]
    if places == 4:
        blocks = [sides] + [far(sides, shift) for shift in (1, 2, 3)]
        queries = 4 * queries_here
        scored = pl.pallas_call(
            functools.partial(scores_kernel, 4, tokens),
            out_shape=jax.ShapeDtypeStruct((queries, rows_here), f32),
            in_specs=[vmem] * 8,
            out_specs=vmem,
            scratch_shapes=[
                pltpu.VMEM((lanes // 128, queries * rank * rank // lanes, 128), f32),
                pltpu.VMEM((queries, rank * rank), f32),
            ],
            name="scores",
        )(in_basis[0], out_basis[0], eigen, train, *blocks)
        place = lax.axis_index("corpus")
        scored = scored.reshape(4, queries_here, rows_here)
        scored = jnp.concatenate(
            [lax.dynamic_slice_in_dim(scored, place ^ i, 1, 0) for i in range(4)], axis=0
        ).reshape(queries, rows_here)
    else:
        everything = lax.all_gather(sides, "corpus", axis=0, tiled=True)
        chunk = 32
        queries = everything.shape[0] // tokens
        scored = pl.pallas_call(
            functools.partial(scores_kernel, 1, tokens),
            out_shape=jax.ShapeDtypeStruct((queries, rows_here), f32),
            grid=(queries // chunk,),
            in_specs=[vmem] * 4 + [pl.BlockSpec((chunk * tokens, 2 * rank), lambda i: (i, 0))],
            out_specs=pl.BlockSpec((chunk, rows_here), lambda i: (i, 0)),
            scratch_shapes=[
                pltpu.VMEM((lanes // 128, chunk * rank * rank // lanes, 128), f32),
                pltpu.VMEM((chunk, rank * rank), f32),
            ],
            name="scores",
        )(in_basis[0], out_basis[0], eigen, train, everything)

    rows_out = rows_here // layers
    layer = lax.axis_index("layer")

    def slab(which):
        return lax.dynamic_slice_in_dim(scored, which * rows_out, rows_out, 1)

    total = slab(layer)
    for shift in range(1, layers):
        total += lax.ppermute(slab(layer ^ shift), "layer", [(i, i ^ shift) for i in range(layers)])
    return total.T


def solution(mesh):
    placed = (
        P(("groups", "corpus"), "layer", None, None),
        P(("groups", "corpus"), "layer", None, None),
        P("layer", None, "corpus"),
        P("layer", None, "corpus"),
        P("layer", None, None),
        P("layer", None, None),
        P("layer", None),
        P(("groups", "corpus"), "layer", None),
    )
    return jax.shard_map(
        body,
        mesh=mesh,
        in_specs=placed,
        out_specs=P(("groups", "corpus", "layer"), None),
        check_vma=False,
    )
```

time: 92.8 us -> 47.7 us (0.51)
  blocking collectives: 49.3 us -> 0 us
  starting transfers between devices: 0.01 us -> 17 us
  between operations: 13.5 us -> 0.09 us
  Pallas kernels: 0 us -> 8.74 us
  matrix products: 6.55 us -> 0 us
  waiting for transfers between devices: 19.8 us -> 16 us
  other arithmetic: 0.77 us -> 2.37 us
    all_gather x3 -> x0, blocking collectives: 49.3 us -> none  [the longest x1 17.8 us: body(): lax.all_gather(in_project, 'corpus', axis=2, tiled=True)]
    unnamed x2 -> x0, waiting for transfers between devices: 19.8 us -> none
    ppermute x0 -> x12, starting transfers between devices: none -> 17 us  [the longest x7 11.5 us: far(): return lax.ppermute(x, 'corpus', [(i, i ^ shift) for i in range(places)])]
    ppermute x0 -> x12, waiting for transfers between devices: none -> 16 us  [the longest x7 10.1 us: far(): return lax.ppermute(x, 'corpus', [(i, i ^ shift) for i in range(places)])]
    pallas_call x0 -> x2, Pallas kernels: none -> 8.74 us  [the longest x1 5.53 us: body(): pl.pallas_call(functools.partial(scores_kernel, 4, tokens), out_shape=jax...]
    dot_general x7 -> x0, matrix products: 6.55 us -> none  [the longest x1 2.07 us: body(): jnp.einsum('qlsa,qlsc->qlac', out_side, in_side, preferred_element_type=j...]
    select_n x0 -> x1, other arithmetic: none -> 1 us  [body(): half = jnp.where(lax.axis_index('groups') == 0, in_own, out_own)]
    unnamed x8 -> x21, local copies, waits for them, and re-layouts: 2.27 us -> 1.75 us
  transfers between devices with their start and end apart: 1 -> 12, of which waited for: 1 -> 6; matrix products, arithmetic and copies ran while one was open for 0% -> 4% of each run, Pallas kernels for 0% -> 0%
where the time goes in v1:
time: 47.7 us; the launch traced here: 47.5 us
  starting transfers between devices  17 us (36%)
  waiting for transfers between devices  16 us (34%)
  Pallas kernels  8.74 us (18%)
  local copies, waits for them, and re-layouts  3.3 us (7%)
  other arithmetic  2.37 us (5%)
    ppermute x7, starting transfers between devices, far(): return lax.ppermute(x, 'corpus', [(i, i ^ shift) for i in range(places)])  11.5 us
    ppermute x7, waiting for transfers between devices, far(): return lax.ppermute(x, 'corpus', [(i, i ^ shift) for i in range(places)])  10.1 us
    pallas_call x1, Pallas kernels, body(): pl.pallas_call(functools.partial(scores_kernel, 4, tokens), out_shape=jax...  5.53 us
    ppermute x2, waiting for transfers between devices, body(): other = lax.ppermute(got, 'groups', [(0, 1), (1, 0)])  3.41 us
    ppermute x2, starting transfers between devices, body(): other = lax.ppermute(got, 'groups', [(0, 1), (1, 0)])  3.24 us
    pallas_call x1, Pallas kernels, body(): pl.pallas_call(functools.partial(sides_kernel, steps), out_shape=jax.Shap...  3.21 us
    ppermute x3, waiting for transfers between devices, body(): lax.ppermute(slab(layer ^ shift), 'layer', [(i, i ^ shift) for i in range...  2.52 us
    ppermute x3, starting transfers between devices, body(): lax.ppermute(slab(layer ^ shift), 'layer', [(i, i ^ shift) for i in range...  2.21 us
  transfers between devices with their start and end apart: 12, of which 6 were waited for; matrix products, arithmetic and copies ran while one was open for 4% of the time, Pallas kernels for 0%

profile of v1, /device:TPU:0, one launch (start us, length us, event | category | flops | bytes accessed | tf_op | source)
XLA Modules:
  0.0 47.5 jit_solution(13599279796178017105)
XLA Ops:
  0.0 1.0 %broadcast_select_fusion = bf16[64,1024]{1,0:T(8,128)(2,1)S(1)} fusion(pred[]{:T(512)S(6)} %eq.3, bf16[1,64,1024]{2,1,0:T(8,128)(2,1)} %param.11, bf16[1,64,1024]{2,1,0:T(8,128)(2,1)} %param.10), kind=kLoop, calls=%fused_computation | loop fusion | flops 65536 | bytes 393217 | tf_op jit(solution)/shard_map/jit(_where)/select_n | solution.py:146
  1.0 5.1 %collective-permute-start = (bf16[64,1024]{1,0:T(8,128)(2,1)S(1)}, bf16[64,1024]{1,0:T(8,128)(2,1)S(1)}, u32[]{:S(2)}, u32[]{:S(2)}) collective-permute-start(bf16[64,1024]{1,0:T(8,128)(2,1)S(1)} %broadcast_select_fusion), channel_id=1, source_target_pairs={{0,12},{4,8},{8,4},{12,0},{1,13},{5,9},{9,5},{13,1},{2,14},{6,10},... | collective-permute-start | bytes 393224 | tf_op jit(solution)/shard_map/ppermute | solution.py:143
  6.1 0.6 %collective-permute-start.4 = (bf16[64,1024]{1,0:T(8,128)(2,1)}, bf16[64,1024]{1,0:T(8,128)(2,1)S(1)}, u32[]{:S(2)}, u32[]{:S(2)}) collective-permute-start(bf16[64,1024]{1,0:T(8,128)(2,1)} %bitcast.17), channel_id=1, source_target_pairs={{0,4},{4,0},{8,12},{12,8},{1,5},{5,1},{9,13},{13,9},{2,6},{6,2},{1... | collective-permute-start | bytes 393224 | tf_op jit(solution)/shard_map/ppermute | solution.py:143
  6.8 1.4 %collective-permute-start.5 = (bf16[64,1024]{1,0:T(8,128)(2,1)}, bf16[64,1024]{1,0:T(8,128)(2,1)S(1)}, u32[]{:S(2)}, u32[]{:S(2)}) collective-permute-start(bf16[64,1024]{1,0:T(8,128)(2,1)} %bitcast.19), channel_id=1, source_target_pairs={{0,4},{4,0},{8,12},{12,8},{1,5},{5,1},{9,13},{13,9},{2,6},{6,2},{1... | collective-permute-start | bytes 393224 | tf_op jit(solution)/shard_map/ppermute | solution.py:143
  8.1 2.4 %collective-permute-done.refs_2_ = bf16[64,1024]{1,0:T(8,128)(2,1)S(1)} collective-permute-done((bf16[64,1024]{1,0:T(8,128)(2,1)S(1)}, bf16[64,1024]{1,0:T(8,128)(2,1)S(1)}, u32[]{:S(2)}, u32[]{:S(2)}) %collective-permute-start) | collective-permute-done | bytes 131104 | tf_op jit(solution)/shard_map/ppermute | solution.py:143
  10.5 1.7 %collective-permute-start.1 = (bf16[64,1024]{1,0:T(8,128)(2,1)S(1)}, bf16[64,1024]{1,0:T(8,128)(2,1)S(1)}, u32[]{:S(2)}, u32[]{:S(2)}) collective-permute-start(bf16[64,1024]{1,0:T(8,128)(2,1)S(1)} %collective-permute-done.refs_2_), channel_id=1, source_target_pairs={{0,16},{16,0},{1,17},{17,1},{2,18},{18,2},{3,19},{19,3},{4,20},{20... | collective-permute-start | bytes 393224 | tf_op jit(solution)/shard_map/ppermute | solution.py:150
  12.3 5.0 %collective-permute-done.2.refs_4_ = bf16[64,1024]{1,0:T(8,128)(2,1)S(1)} collective-permute-done((bf16[64,1024]{1,0:T(8,128)(2,1)S(1)}, bf16[64,1024]{1,0:T(8,128)(2,1)S(1)}, u32[]{:S(2)}, u32[]{:S(2)}) %collective-permute-start.2) | collective-permute-done | bytes 131104 | tf_op jit(solution)/shard_map/ppermute | solution.py:143
  17.3 1.5 %collective-permute-start.3 = (bf16[64,1024]{1,0:T(8,128)(2,1)S(1)}, bf16[64,1024]{1,0:T(8,128)(2,1)S(1)}, u32[]{:S(2)}, u32[]{:S(2)}) collective-permute-start(bf16[64,1024]{1,0:T(8,128)(2,1)S(1)} %collective-permute-done.2.refs_4_), channel_id=1, source_target_pairs={{0,16},{16,0},{1,17},{17,1},{2,18},{18,2},{3,19},{19,3},{4,20},{20... | collective-permute-start | bytes 393224 | tf_op jit(solution)/shard_map/ppermute | solution.py:150
  18.9 3.4 %collective-permute-done.3.refs_5_ = bf16[64,1024]{1,0:T(8,128)(2,1)S(1)} collective-permute-done((bf16[64,1024]{1,0:T(8,128)(2,1)S(1)}, bf16[64,1024]{1,0:T(8,128)(2,1)S(1)}, u32[]{:S(2)}, u32[]{:S(2)}) %collective-permute-start.3) | collective-permute-done | bytes 131104 | tf_op jit(solution)/shard_map/ppermute | solution.py:150
  22.3 0.6 %copy-done.5 = bf16[64,1024]{1,0:T(8,128)(2,1)} copy-done((bf16[64,1024]{1,0:T(8,128)(2,1)}, bf16[64,1024]{1,0:T(8,128)(2,1)S(1)}, u32[]{:S(2)}) %copy-start.5) | copy-done | bytes 131096
  22.9 3.2 %sides.1.refs_0_ = bf16[128,128]{1,0:T(8,128)(2,1)} custom-call(bf16[128,4096]{1,0:T(8,128)(2,1)} %bitcast.15, bf16[128,4096]{1,0:T(8,128)(2,1)} %bitcast.16, bf16[64,1024]{1,0:T(8,128)(2,1)} %bitcast.18, bf16[64,1024]{1,0:T(8,128)(2,1)} %bitcast.20, bf16[64,1024]{1,0:T(8,128)(2,1)} %copy-done, bf16[64,1024]{1,0:T(8,128)(2,1)} %copy-done.4, ...), custom_call_target="tpu_custom_call" | custom-call | tf_op jit(solution)/shard_map/sides/pallas_call | solution.py:158
  26.5 2.7 %collective-permute-start.7 = (bf16[128,128]{1,0:T(8,128)(2,1)}, bf16[128,128]{1,0:T(8,128)(2,1)S(1)}, u32[]{:S(2)}, u32[]{:S(2)}) collective-permute-start(bf16[128,128]{1,0:T(8,128)(2,1)} %sides.1.refs_0_), channel_id=1, source_target_pairs={{0,8},{4,12},{8,0},{12,4},{1,9},{5,13},{9,1},{13,5},{2,10},{6,14},... | collective-permute-start | bytes 98312 | tf_op jit(solution)/shard_map/ppermute | solution.py:143
  29.1 1.4 %collective-permute-start.8 = (bf16[128,128]{1,0:T(8,128)(2,1)}, bf16[128,128]{1,0:T(8,128)(2,1)S(1)}, u32[]{:S(2)}, u32[]{:S(2)}) collective-permute-start(bf16[128,128]{1,0:T(8,128)(2,1)} %sides.1.refs_0_), channel_id=1, source_target_pairs={{0,12},{4,8},{8,4},{12,0},{1,13},{5,9},{9,5},{13,1},{2,14},{6,10},... | collective-permute-start | bytes 98312 | tf_op jit(solution)/shard_map/ppermute | solution.py:143
  31.0 0.7 %reduce.3 = f32[4096]{0:T(1024)S(1)} reduce(f32[1,4096]{1,0:T(1,128)S(1)} %copy-done.9, f32[]{:T(128)} %broadcast.3), dimensions={0}, to_apply=%param.14.reduce_sub_computation.3 | reduce | bytes 32772 | tf_op args[6]
  31.7 0.7 %reshape.18.eigen = f32[64,64]{1,0:T(8,128)} reshape(f32[4096]{0:T(1024)S(1)} %reduce.3) | data formatting | bytes 32768 | tf_op jit(solution)/shard_map/reshape | solution.py:166
  32.4 2.6 %collective-permute-done.8.refs_3_ = bf16[128,128]{1,0:T(8,128)(2,1)S(1)} collective-permute-done((bf16[128,128]{1,0:T(8,128)(2,1)}, bf16[128,128]{1,0:T(8,128)(2,1)S(1)}, u32[]{:S(2)}, u32[]{:S(2)}) %collective-permute-start.8) | collective-permute-done | bytes 32800 | tf_op jit(solution)/shard_map/ppermute | solution.py:143
  35.1 0.6 %copy-done.8 = bf16[128,128]{1,0:T(8,128)(2,1)} copy-done((bf16[128,128]{1,0:T(8,128)(2,1)}, bf16[128,128]{1,0:T(8,128)(2,1)S(1)}, u32[]{:S(2)}) %copy-start.8) | copy-done | bytes 32792
  35.7 5.5 %scores.1 = f32[32,320]{1,0:T(8,128)} custom-call(f32[64,64]{1,0:T(8,128)} %bitcast.22, f32[64,64]{1,0:T(8,128)} %bitcast.23, f32[64,64]{1,0:T(8,128)} %reshape.18.eigen, bf16[320,4096]{1,0:T(8,128)(2,1)} %bitcast.14, bf16[128,128]{1,0:T(8,128)(2,1)} %sides.1.refs_0_, bf16[128,128]{1,0:T(8,128)(2,1)} %copy-done.6, bf16[128,128]{1,0:T(8,128)(2,1)} %copy-done.7, ...), custom_call_target="tpu_custom_call" | custom-call | tf_op jit(solution)/shard_map/scores/pallas_call | solution.py:172
  41.2 0.8 %constant_dynamic-slice_fusion.6 = (f32[1,8,320]{2,1,0:T(8,128)S(1)}, f32[1,8,320]{2,1,0:T(8,128)S(1)}, f32[1,8,320]{2,1,0:T(8,128)S(1)}, f32[1,8,320]{2,1,0:T(8,128)S(1)}) fusion(f32[4,8,320]{2,1,0:T(8,128)} %bitcast.21, s32[]{:T(128)S(6)} %select_n.34, s32[]{:T(128)S(6)} %select_n.37, s32[]{:T(128)S(6)} %select_n.36, s32[]{:T(128)S(6)} %select_n.35), kind=kLoop, calls=%fused_computation.9 | loop fusion | bytes 81936 | tf_op jit(solution)/shard_map/dynamic_slice | solution.py:186
  42.1 1.6 %collective-permute-start.10 = (f32[32,80]{1,0:T(8,128)S(1)}, f32[32,80]{1,0:T(8,128)S(1)}, u32[]{:S(2)}, u32[]{:S(2)}) collective-permute-start(f32[32,80]{1,0:T(8,128)S(1)} %get-tuple-element.7), channel_id=1, source_target_pairs={{0,2},{1,3},{2,0},{3,1},{4,6},{5,7},{6,4},{7,5},{8,10},{9,11},{10,... | collective-permute-start | bytes 30728 | tf_op jit(solution)/shard_map/ppermute | solution.py:213
  43.6 0.6 %collective-permute-start.9 = (f32[32,80]{1,0:T(8,128)S(1)}, f32[32,80]{1,0:T(8,128)S(1)}, u32[]{:S(2)}, u32[]{:S(2)}) collective-permute-start(f32[32,80]{1,0:T(8,128)S(1)} %get-tuple-element.5), channel_id=1, source_target_pairs={{0,1},{1,0},{2,3},{3,2},{4,5},{5,4},{6,7},{7,6},{8,9},{9,8},{10,11... | collective-permute-start | bytes 30728 | tf_op jit(solution)/shard_map/ppermute | solution.py:213
  44.3 1.6 %collective-permute-done.10 = f32[32,80]{1,0:T(8,128)S(1)} collective-permute-done((f32[32,80]{1,0:T(8,128)S(1)}, f32[32,80]{1,0:T(8,128)S(1)}, u32[]{:S(2)}, u32[]{:S(2)}) %collective-permute-start.10) | collective-permute-done | bytes 10272 | tf_op jit(solution)/shard_map/ppermute | solution.py:213
  45.9 0.9 %collective-permute-done.11 = f32[32,80]{1,0:T(8,128)S(1)} collective-permute-done((f32[32,80]{1,0:T(8,128)S(1)}, f32[32,80]{1,0:T(8,128)S(1)}, u32[]{:S(2)}, u32[]{:S(2)}) %collective-permute-start.11) | collective-permute-done | bytes 10272 | tf_op jit(solution)/shard_map/ppermute | solution.py:213
  46.8 0.7 %add_bitcast_fusion = f32[80,32]{0,1:T(8,128)} fusion(f32[32,80]{1,0:T(8,128)S(1)} %collective-permute-done.11, f32[32,80]{1,0:T(8,128)S(1)} %collective-permute-done.10, f32[32,80]{1,0:T(8,128)S(1)} %collective-permute-done.9, f32[32,320]{1,0:T(8,128)S(1)} %maximum_bitcast_fusion, s32[]{:T(128)S(6)} %select_n.38), kind=kLoop, calls=%fused_computation.2 | loop fusion | flops 7680 | bytes 51204 | tf_op jit(solution)/shard_map/transpose | solution.py:214
  (30 shorter events, 1.0 us)
Async XLA Ops:
  0.0 31.0 %copy-start.9 = (f32[1,4096]{1,0:T(1,128)S(1)}, f32[1,4096]{1,0:T(1,128)}, u32[]{:S(2)}) copy-start(f32[1,4096]{1,0:T(1,128)} %param.14) | copy-start | bytes 49156
  1.0 9.5 %collective-permute-start = (bf16[64,1024]{1,0:T(8,128)(2,1)S(1)}, bf16[64,1024]{1,0:T(8,128)(2,1)S(1)}, u32[]{:S(2)}, u32[]{:S(2)}) collective-permute-start(bf16[64,1024]{1,0:T(8,128)(2,1)S(1)} %broadcast_select_fusion), channel_id=1, source_target_pairs={{0,12},{4,8},{8,4},{12,0},{1,13},{5,9},{9,5},{13,1},{2,14},{6,10},... | collective-permute-start | bytes 393224 | tf_op jit(solution)/shard_map/ppermute | solution.py:143
  6.1 11.2 %collective-permute-start.2 = (bf16[64,1024]{1,0:T(8,128)(2,1)S(1)}, bf16[64,1024]{1,0:T(8,128)(2,1)S(1)}, u32[]{:S(2)}, u32[]{:S(2)}) collective-permute-start(bf16[64,1024]{1,0:T(8,128)(2,1)S(1)} %broadcast_select_fusion), channel_id=1, source_target_pairs={{0,8},{4,12},{8,0},{12,4},{1,9},{5,13},{9,1},{13,5},{2,10},{6,14},... | collective-permute-start | bytes 393224 | tf_op jit(solution)/shard_map/ppermute | solution.py:143
  6.1 12.7 %collective-permute-start.4 = (bf16[64,1024]{1,0:T(8,128)(2,1)}, bf16[64,1024]{1,0:T(8,128)(2,1)S(1)}, u32[]{:S(2)}, u32[]{:S(2)}) collective-permute-start(bf16[64,1024]{1,0:T(8,128)(2,1)} %bitcast.17), channel_id=1, source_target_pairs={{0,4},{4,0},{8,12},{12,8},{1,5},{5,1},{9,13},{13,9},{2,6},{6,2},{1... | collective-permute-start | bytes 393224 | tf_op jit(solution)/shard_map/ppermute | solution.py:143
  6.8 12.1 %collective-permute-start.5 = (bf16[64,1024]{1,0:T(8,128)(2,1)}, bf16[64,1024]{1,0:T(8,128)(2,1)S(1)}, u32[]{:S(2)}, u32[]{:S(2)}) collective-permute-start(bf16[64,1024]{1,0:T(8,128)(2,1)} %bitcast.19), channel_id=1, source_target_pairs={{0,4},{4,0},{8,12},{12,8},{1,5},{5,1},{9,13},{13,9},{2,6},{6,2},{1... | collective-permute-start | bytes 393224 | tf_op jit(solution)/shard_map/ppermute | solution.py:143
  10.5 11.7 %copy-start = (bf16[64,1024]{1,0:T(8,128)(2,1)}, bf16[64,1024]{1,0:T(8,128)(2,1)S(1)}, u32[]{:S(2)}) copy-start(bf16[64,1024]{1,0:T(8,128)(2,1)S(1)} %collective-permute-done.refs_2_) | copy-start | bytes 393220
  10.5 8.3 %collective-permute-start.1 = (bf16[64,1024]{1,0:T(8,128)(2,1)S(1)}, bf16[64,1024]{1,0:T(8,128)(2,1)S(1)}, u32[]{:S(2)}, u32[]{:S(2)}) collective-permute-start(bf16[64,1024]{1,0:T(8,128)(2,1)S(1)} %collective-permute-done.refs_2_), channel_id=1, source_target_pairs={{0,16},{16,0},{1,17},{17,1},{2,18},{18,2},{3,19},{19,3},{4,20},{20... | collective-permute-start | bytes 393224 | tf_op jit(solution)/shard_map/ppermute | solution.py:150
  17.3 5.0 %copy-start.1 = (bf16[64,1024]{1,0:T(8,128)(2,1)}, bf16[64,1024]{1,0:T(8,128)(2,1)S(1)}, u32[]{:S(2)}) copy-start(bf16[64,1024]{1,0:T(8,128)(2,1)S(1)} %collective-permute-done.2.refs_4_) | copy-start | bytes 393220
  17.3 5.0 %collective-permute-start.3 = (bf16[64,1024]{1,0:T(8,128)(2,1)S(1)}, bf16[64,1024]{1,0:T(8,128)(2,1)S(1)}, u32[]{:S(2)}, u32[]{:S(2)}) collective-permute-start(bf16[64,1024]{1,0:T(8,128)(2,1)S(1)} %collective-permute-done.2.refs_4_), channel_id=1, source_target_pairs={{0,16},{16,0},{1,17},{17,1},{2,18},{18,2},{3,19},{19,3},{4,20},{20... | collective-permute-start | bytes 393224 | tf_op jit(solution)/shard_map/ppermute | solution.py:150
  18.8 3.5 %copy-start.2 = (bf16[64,1024]{1,0:T(8,128)(2,1)}, bf16[64,1024]{1,0:T(8,128)(2,1)S(1)}, u32[]{:S(2)}) copy-start(bf16[64,1024]{1,0:T(8,128)(2,1)S(1)} %collective-permute-done.4.refs_6_) | copy-start | bytes 393220
  18.8 3.5 %copy-start.3 = (bf16[64,1024]{1,0:T(8,128)(2,1)}, bf16[64,1024]{1,0:T(8,128)(2,1)S(1)}, u32[]{:S(2)}) copy-start(bf16[64,1024]{1,0:T(8,128)(2,1)S(1)} %collective-permute-done.5.refs_7_) | copy-start | bytes 393220
  18.8 3.4 %copy-start.4 = (bf16[64,1024]{1,0:T(8,128)(2,1)}, bf16[64,1024]{1,0:T(8,128)(2,1)S(1)}, u32[]{:S(2)}) copy-start(bf16[64,1024]{1,0:T(8,128)(2,1)S(1)} %collective-permute-done.1.refs_3_) | copy-start | bytes 393220
  22.3 0.6 %copy-start.5 = (bf16[64,1024]{1,0:T(8,128)(2,1)}, bf16[64,1024]{1,0:T(8,128)(2,1)S(1)}, u32[]{:S(2)}) copy-start(bf16[64,1024]{1,0:T(8,128)(2,1)S(1)} %collective-permute-done.3.refs_5_) | copy-start | bytes 393220
  26.1 6.3 %collective-permute-start.6 = (bf16[128,128]{1,0:T(8,128)(2,1)}, bf16[128,128]{1,0:T(8,128)(2,1)S(1)}, u32[]{:S(2)}, u32[]{:S(2)}) collective-permute-start(bf16[128,128]{1,0:T(8,128)(2,1)} %sides.1.refs_0_), channel_id=1, source_target_pairs={{0,4},{4,0},{8,12},{12,8},{1,5},{5,1},{9,13},{13,9},{2,6},{6,2},{1... | collective-permute-start | bytes 98312 | tf_op jit(solution)/shard_map/ppermute | solution.py:143
  26.5 5.9 %collective-permute-start.7 = (bf16[128,128]{1,0:T(8,128)(2,1)}, bf16[128,128]{1,0:T(8,128)(2,1)S(1)}, u32[]{:S(2)}, u32[]{:S(2)}) collective-permute-start(bf16[128,128]{1,0:T(8,128)(2,1)} %sides.1.refs_0_), channel_id=1, source_target_pairs={{0,8},{4,12},{8,0},{12,4},{1,9},{5,13},{9,1},{13,5},{2,10},{6,14},... | collective-permute-start | bytes 98312 | tf_op jit(solution)/shard_map/ppermute | solution.py:143
  29.1 5.9 %collective-permute-start.8 = (bf16[128,128]{1,0:T(8,128)(2,1)}, bf16[128,128]{1,0:T(8,128)(2,1)S(1)}, u32[]{:S(2)}, u32[]{:S(2)}) collective-permute-start(bf16[128,128]{1,0:T(8,128)(2,1)} %sides.1.refs_0_), channel_id=1, source_target_pairs={{0,12},{4,8},{8,4},{12,0},{1,13},{5,9},{9,5},{13,1},{2,14},{6,10},... | collective-permute-start | bytes 98312 | tf_op jit(solution)/shard_map/ppermute | solution.py:143
  32.4 2.7 %copy-start.6 = (bf16[128,128]{1,0:T(8,128)(2,1)}, bf16[128,128]{1,0:T(8,128)(2,1)S(1)}, u32[]{:S(2)}) copy-start(bf16[128,128]{1,0:T(8,128)(2,1)S(1)} %collective-permute-done.6.refs_1_) | copy-start | bytes 98308
  32.4 2.7 %copy-start.7 = (bf16[128,128]{1,0:T(8,128)(2,1)}, bf16[128,128]{1,0:T(8,128)(2,1)S(1)}, u32[]{:S(2)}) copy-start(bf16[128,128]{1,0:T(8,128)(2,1)S(1)} %collective-permute-done.7.refs_2_) | copy-start | bytes 98308
  35.1 0.6 %copy-start.8 = (bf16[128,128]{1,0:T(8,128)(2,1)}, bf16[128,128]{1,0:T(8,128)(2,1)S(1)}, u32[]{:S(2)}) copy-start(bf16[128,128]{1,0:T(8,128)(2,1)S(1)} %collective-permute-done.8.refs_3_) | copy-start | bytes 98308
  42.1 3.8 %collective-permute-start.10 = (f32[32,80]{1,0:T(8,128)S(1)}, f32[32,80]{1,0:T(8,128)S(1)}, u32[]{:S(2)}, u32[]{:S(2)}) collective-permute-start(f32[32,80]{1,0:T(8,128)S(1)} %get-tuple-element.7), channel_id=1, source_target_pairs={{0,2},{1,3},{2,0},{3,1},{4,6},{5,7},{6,4},{7,5},{8,10},{9,11},{10,... | collective-permute-start | bytes 30728 | tf_op jit(solution)/shard_map/ppermute | solution.py:213
  43.6 3.2 %collective-permute-start.11 = (f32[32,80]{1,0:T(8,128)S(1)}, f32[32,80]{1,0:T(8,128)S(1)}, u32[]{:S(2)}, u32[]{:S(2)}) collective-permute-start(f32[32,80]{1,0:T(8,128)S(1)} %get-tuple-element.6), channel_id=1, source_target_pairs={{0,3},{1,2},{2,1},{3,0},{4,7},{5,6},{6,5},{7,4},{8,11},{9,10},{10,... | collective-permute-start | bytes 30728 | tf_op jit(solution)/shard_map/ppermute | solution.py:213
  43.6 3.2 %collective-permute-start.9 = (f32[32,80]{1,0:T(8,128)S(1)}, f32[32,80]{1,0:T(8,128)S(1)}, u32[]{:S(2)}, u32[]{:S(2)}) collective-permute-start(f32[32,80]{1,0:T(8,128)S(1)} %get-tuple-element.5), channel_id=1, source_target_pairs={{0,1},{1,0},{2,3},{3,2},{4,5},{5,4},{6,7},{7,6},{8,9},{9,8},{10,11... | collective-permute-start | bytes 30728 | tf_op jit(solution)/shard_map/ppermute | solution.py:213

commit v2 on v1

v2 whole, which is shorter than its diff:
```python
import functools

import jax
import jax.numpy as jnp
from jax import lax
from jax.experimental import pallas as pl
from jax.experimental.pallas import tpu as pltpu
from jax.sharding import PartitionSpec as P

damping = 0.1
f32 = jnp.float32
bf16 = jnp.bfloat16
lanes = 256
nt = (((1,), (1,)), ((), ()))
tn = (((0,), (0,)), ((), ()))
vmem = pl.BlockSpec(memory_space=pltpu.VMEM)
params = pltpu.CompilerParams(vmem_limit_bytes=16 << 20)


def dot(a, b, dims=(((1,), (0,)), ((), ()))):
    return lax.dot_general(a, b, dims, preferred_element_type=f32)


def split(x):
    high = x.astype(bf16)
    return high, (x - high.astype(f32)).astype(bf16)


def tiled_diagonal(x, blocks):
    n = x.shape[0]
    wide = jnp.concatenate([x] * blocks, axis=1)
    tall = jnp.concatenate([wide] * blocks, axis=0)
    row = lax.broadcasted_iota(jnp.int32, tall.shape, 0) // n
    column = lax.broadcasted_iota(jnp.int32, tall.shape, 1) // n
    return jnp.where(row == column, tall, 0.0)


def product3(x, high, low):
    x_high, x_low = split(x)
    return dot(x_high, high) + (dot(x_low, high) + dot(x_high, low))


def sides_kernel(plan, acts, outgrads, *refs):
    total, sides = refs[len(plan) : -1], refs[-1]
    group, place = lax.axis_index("groups"), lax.axis_index("corpus")
    sums = [jnp.zeros((acts.shape[0], sides.shape[1] // 2), f32)] * 2
    for (side, first), piece in zip(plan, refs):
        width = piece.shape[1]
        columns = pl.ds(pl.multiple_of(first(group, place), 128), width)
        inputs = acts if side else outgrads
        sums[side] += dot(inputs[:, columns], piece[...], nt)
    result = jnp.concatenate(sums, axis=1)
    if total:
        result += total[0][...]
    sides[...] = result.astype(sides.dtype)


def scores_kernel(sources, shifts, tokens, in_basis, out_basis, eigen, train, *refs):
    blocks, (scratch, rows, tall) = refs[:sources], refs[-3:]
    layers = lax.axis_size("layer")
    given = refs[sources : -3 - layers]
    outs = refs[-3 - layers : -3]
    rank = in_basis.shape[0]
    across = lanes // rank
    here = blocks[0].shape[0] // tokens
    queries = here * sources
    groups = queries // across
    u_in, u_out = in_basis[...], out_basis[...]
    inverse = 1.0 / (eigen[...] + damping)
    inverse = jnp.concatenate([inverse] * across, axis=1)
    out_high, out_low = split(u_out)
    turn = jnp.concatenate([out_high, out_low], axis=0)
    back = jnp.concatenate([out_high, out_low, out_high], axis=1)
    in_high, in_low = split(tiled_diagonal(u_in, across))
    tin_high, tin_low = split(tiled_diagonal(u_in.T, across))
    mask = (
        lax.broadcasted_iota(jnp.int32, (across * tokens, lanes), 0) // tokens
        == lax.broadcasted_iota(jnp.int32, (across * tokens, lanes), 1) // rank
    )
    parts = [[] for _ in range(groups)]
    for group in range(groups):
        for j in range(across):
            query = j * groups + group
            start = query % here * tokens
            parts[group].append(blocks[query // here][start : start + tokens, :])
    turned = []
    for group in range(groups):
        both = jnp.concatenate(parts[group], axis=0)
        out_side = both[:, :rank]
        in_side = jnp.concatenate([both[:, rank:]] * across, axis=1)
        in_side = jnp.where(mask, in_side, jnp.zeros_like(in_side))
        gradient = (dot(out_side, in_side, tn) * (1.0 / tokens)).astype(bf16)
        turned.append(dot(turn, jnp.concatenate([gradient, gradient], axis=0), tn))
    turned = jnp.concatenate(turned, axis=0)
    turned = product3(turned, in_high, in_low)
    scaled = []
    for group in range(groups):
        part = turned[group * rank : (group + 1) * rank] * inverse
        high, low = split(part)
        scaled.append(dot(back, jnp.concatenate([high, high, low], axis=0)))
    scaled = jnp.concatenate(scaled, axis=0)
    conditioned = product3(scaled, tin_high, tin_low)
    for part in range(lanes // 128):
        scratch[part] = conditioned[:, part * 128 : (part + 1) * 128]
    for pair in range(rank // 2):
        for part in range(lanes // 128):
            even = scratch[part, pl.ds(2 * pair, groups, stride=rank), :]
            odd = scratch[part, pl.ds(2 * pair + 1, groups, stride=rank), :]
            columns = slice(2 * pair * rank, 2 * (pair + 1) * rank)
            for half in range(2):
                j = 2 * part + half
                cut = slice(half * rank, (half + 1) * rank)
                rows[j * groups : (j + 1) * groups, columns] = jnp.concatenate(
                    [even[:, cut], odd[:, cut]], axis=1
                )
    tall[...] = dot(train[...], rows[...].astype(bf16), nt)
    layer, place = lax.axis_index("layer"), lax.axis_index("corpus")
    slab_rows = train.shape[0] // layers
    for shift, out in enumerate(outs):
        slab = tall[pl.ds(pl.multiple_of((layer ^ shift) * slab_rows, 8), slab_rows), :].T
        if shifts is None:
            out[...] = slab
            continue
        out[pl.ds(pl.multiple_of(place * here, 8), here), :] = given[shift][...]
        for at, far in enumerate(shifts):
            to = pl.ds(pl.multiple_of((place ^ far) * here, 8), here)
            out[to, :] = slab[at * here : (at + 1) * here]


def body(
    query_acts,
    query_outgrads,
    in_project,
    out_project,
    in_basis,
    out_basis,
    eig_values,
    train_grads,
):
    queries_here, _, tokens, model = query_acts.shape
    rank, width = in_project.shape[1:]
    places = model // width
    layers = lax.axis_size("layer")
    acts = query_acts.reshape(queries_here * tokens, model)
    outgrads = query_outgrads.reshape(queries_here * tokens, model)
    in_own, out_own = in_project[0], out_project[0]

    def far(x, shift):
        return lax.ppermute(x, "corpus", [(i, i ^ shift) for i in range(places)])

    def mixed(x, shifts):
        pairs = [(g * places + i, g * places + (i ^ shifts[g])) for g in range(2) for i in range(places)]
        return lax.ppermute(x, ("groups", "corpus"), pairs)

    def swapped(x):
        return lax.ppermute(x, "groups", [(0, 1), (1, 0)])

    def sides_call(plan, pieces, total, dtype):
        return pl.pallas_call(
            functools.partial(sides_kernel, plan),
            out_shape=jax.ShapeDtypeStruct((queries_here * tokens, 2 * rank), dtype),
            in_specs=[vmem] * (2 + len(pieces) + len(total)),
            out_specs=vmem,
            compiler_params=params,
            name="sides",
        )(acts, outgrads, *pieces, *total)

    eigen = eig_values.reshape(rank, rank)
    train = train_grads.reshape(train_grads.shape[0], rank * rank)
    rows_out = train.shape[0] // layers

    def scores_call(shifts, blocks, given, chunk):
        queries = sum(x.shape[0] for x in blocks) // tokens + (queries_here if given else 0)
        here = blocks[0].shape[0] // tokens // (chunk or 1)
        count = here * len(blocks)
        out_rows = queries // (chunk or 1)
        if chunk:
            specs = dict(
                grid=(chunk,),
                in_specs=[vmem] * 4 + [pl.BlockSpec((here * tokens, 2 * rank), lambda i: (i, 0))],
                out_specs=[pl.BlockSpec((out_rows, rows_out), lambda i: (i, 0))] * layers,
            )
        else:
            specs = dict(in_specs=[vmem] * (4 + len(blocks) + len(given)), out_specs=[vmem] * layers)
        return pl.pallas_call(
            functools.partial(scores_kernel, len(blocks), shifts, tokens),
            out_shape=[jax.ShapeDtypeStruct((queries, rows_out), f32)] * layers,
            scratch_shapes=[
                pltpu.VMEM((lanes // 128, count * rank * rank // lanes, 128), f32),
                pltpu.VMEM((count, rank * rank), f32),
                pltpu.VMEM((train.shape[0], count), f32),
            ],
            compiler_params=params,
            name="scores",
            **specs,
        )(in_basis[0], out_basis[0], eigen, train, *blocks, *given)

    if places == 4 and lax.axis_size("groups") == 2:
        part = width // 2
        near = mixed(in_own, (3, 1))
        near_out = mixed(out_own, (1, 3))
        cut = far(lax.dynamic_slice_in_dim(out_own, lax.axis_index("groups") * part, part, 1), 2)
        last = far(in_own, 2)
        direct = lambda g, p: (p ^ 2) * width
        first, second = (lambda g, p: (p ^ (3 - 2 * g)) * width), (lambda g, p: (p ^ (1 + 2 * g)) * width)
        mine = lambda g, p: (p ^ 2) * width + g * part
        other = lambda g, p: (p ^ 2) * width + (1 - g) * part
        total = sides_call([(1, lambda g, p: p * width), (0, lambda g, p: p * width)], [in_own, out_own], [], f32)
        near, total, eigen = lax.optimization_barrier((near, total, eigen))
        total = sides_call(
            [(1, first), (0, second), (0, mine), (1, direct)], [near, near_out, cut, last], [total], f32
        )
        sides = sides_call(
            [(1, second), (0, first), (0, other)],
            [swapped(near), swapped(near_out), swapped(cut)],
            [total],
            bf16,
        )
        arrived = [far(sides, shift) for shift in (3, 2, 1)]
        own = scores_call(None, [sides], [], None)
        slabs = scores_call((3, 2, 1), arrived, own, None)
    else:
        pieces = [lax.all_gather(x, "corpus", axis=1, tiled=True) for x in (in_own, out_own)]
        sides = sides_call([(1, lambda g, p: 0), (0, lambda g, p: 0)], pieces, [], bf16)
        everything = lax.all_gather(sides, "corpus", axis=0, tiled=True)
        slabs = scores_call(None, [everything], [], everything.shape[0] // tokens // 32)

    total = slabs[0]
    for shift in range(1, layers):
        total += lax.ppermute(slabs[shift], "layer", [(i, i ^ shift) for i in range(layers)])
    return total.T


def solution(mesh):
    placed = (
        P(("groups", "corpus"), "layer", None, None),
        P(("groups", "corpus"), "layer", None, None),
        P("layer", None, "corpus"),
        P("layer", None, "corpus"),
        P("layer", None, None),
        P("layer", None, None),
        P("layer", None),
        P(("groups", "corpus"), "layer", None),
    )
    return jax.shard_map(
        body,
        mesh=mesh,
        in_specs=placed,
        out_specs=P(("groups", "corpus", "layer"), None),
        check_vma=False,
    )
```

time: 47.7 us -> 40.5 us (0.85)
  waiting for transfers between devices: 16 us -> 7.48 us
  Pallas kernels: 8.74 us -> 5.78 us
  local copies, waits for them, and re-layouts: 3.3 us -> 5.7 us
  starting transfers between devices: 17 us -> 19.1 us
    ppermute x7 -> x5, waiting for transfers between devices: 10.1 us -> 2.7 us  [far(): return lax.ppermute(x, 'corpus', [(i, i ^ shift) for i in range(places)])]
    ppermute x5 -> x8, starting transfers between devices: 5.45 us -> 11.8 us  [the longest x2 5.05 us: mixed(): return lax.ppermute(x, ('groups', 'corpus'), pairs)]
    ppermute x7 -> x5, starting transfers between devices: 11.5 us -> 7.38 us  [far(): return lax.ppermute(x, 'corpus', [(i, i ^ shift) for i in range(places)])]
    unnamed x21 -> x15, local copies, waits for them, and re-layouts: 1.75 us -> 4.79 us
    pallas_call x2 -> x5, Pallas kernels: 8.74 us -> 5.78 us  [the longest x2 4.64 us: scores_call(): pl.pallas_call(functools.partial(scores_kernel, len(blocks), shifts, toke...]
    ppermute x5 -> x8, waiting for transfers between devices: 5.93 us -> 4.78 us  [the longest x3 2.86 us: body(): lax.ppermute(slabs[shift], 'layer', [(i, i ^ shift) for i in range(layers)])]
    select_n x1 -> x0, other arithmetic: 1 us -> none  [body(): half = jnp.where(lax.axis_index('groups') == 0, in_own, out_own)]
    unnamed x1, other arithmetic: 0.68 us -> 1.4 us
  transfers between devices with their start and end apart: 12 -> 13, of which waited for: 6 -> 5; matrix products, arithmetic and copies ran while one was open for 4% -> 7% of each run, Pallas kernels for 0% -> 7%
where the time goes in v2:
time: 40.5 us; the launch traced here: 40.2 us
  starting transfers between devices  19.1 us (47%)
  waiting for transfers between devices  7.48 us (18%)
  Pallas kernels  5.78 us (14%)
  local copies, waits for them, and re-layouts  5.7 us (14%)
  other arithmetic  2.01 us (5%)
    ppermute x5, starting transfers between devices, far(): return lax.ppermute(x, 'corpus', [(i, i ^ shift) for i in range(places)])  7.38 us
    ppermute x2, starting transfers between devices, mixed(): return lax.ppermute(x, ('groups', 'corpus'), pairs)  5.05 us
    unnamed x15, local copies, waits for them, and re-layouts  4.79 us
    ppermute x3, starting transfers between devices, swapped(): return lax.ppermute(x, 'groups', [(0, 1), (1, 0)])  4.77 us
    pallas_call x2, Pallas kernels, scores_call(): pl.pallas_call(functools.partial(scores_kernel, len(blocks), shifts, toke...  4.64 us
    ppermute x3, waiting for transfers between devices, body(): lax.ppermute(slabs[shift], 'layer', [(i, i ^ shift) for i in range(layers)])  2.86 us
    ppermute x5, waiting for transfers between devices, far(): return lax.ppermute(x, 'corpus', [(i, i ^ shift) for i in range(places)])  2.7 us
    ppermute x3, starting transfers between devices, body(): lax.ppermute(slabs[shift], 'layer', [(i, i ^ shift) for i in range(layers)])  1.93 us
  transfers between devices with their start and end apart: 13, of which 5 were waited for; matrix products, arithmetic and copies ran while one was open for 7% of the time, Pallas kernels for 7%

profile of v2, /device:TPU:0, one launch (start us, length us, event | category | flops | bytes accessed | tf_op | source)
XLA Modules:
  0.0 40.2 jit_solution(15003849822413492651)
XLA Ops:
  0.0 5.0 %collective-permute-start = (bf16[64,1024]{1,0:T(8,128)(2,1)}, bf16[64,1024]{1,0:T(8,128)(2,1)S(1)}, u32[]{:S(2)}, u32[]{:S(2)}) collective-permute-start(bf16[64,1024]{1,0:T(8,128)(2,1)} %bitcast.25), channel_id=1, source_target_pairs={{0,12},{4,8},{8,4},{12,0},{16,20},{20,16},{24,28},{28,24},{1,13},{... | collective-permute-start | bytes 393224 | tf_op jit(solution)/shard_map/ppermute | solution.py:153
  5.1 0.6 %collective-permute-start.6 = (bf16[64,1024]{1,0:T(8,128)(2,1)}, bf16[64,1024]{1,0:T(8,128)(2,1)S(1)}, u32[]{:S(2)}, u32[]{:S(2)}) collective-permute-start(bf16[64,1024]{1,0:T(8,128)(2,1)} %bitcast.26), channel_id=1, source_target_pairs={{0,8},{4,12},{8,0},{12,4},{1,9},{5,13},{9,1},{13,5},{2,10},{6,14},... | collective-permute-start | bytes 393224 | tf_op jit(solution)/shard_map/ppermute | solution.py:149
  5.6 0.8 %dynamic-slice_bitcast_fusion = bf16[64,512]{1,0:T(8,128)(2,1)S(1)} fusion(bf16[1,64,1024]{2,1,0:T(8,128)(2,1)} %param.11, s32[]{:T(128)S(6)} %select_n.3), kind=kLoop, calls=%fused_computation | loop fusion | bytes 131076 | tf_op jit(solution)/shard_map/dynamic_slice | solution.py:202
  6.5 2.4 %collective-permute-start.4 = (bf16[64,512]{1,0:T(8,128)(2,1)S(1)}, bf16[64,512]{1,0:T(8,128)(2,1)S(1)}, u32[]{:S(2)}, u32[]{:S(2)}) collective-permute-start(bf16[64,512]{1,0:T(8,128)(2,1)S(1)} %dynamic-slice_bitcast_fusion), channel_id=1, source_target_pairs={{0,8},{4,12},{8,0},{12,4},{1,9},{5,13},{9,1},{13,5},{2,10},{6,14},... | collective-permute-start | bytes 196616 | tf_op jit(solution)/shard_map/ppermute | solution.py:149
  8.8 0.5 %broadcast.3 = f32[]{:T(128)} broadcast(f32[]{:T(128)} %constant.24), dimensions={} | broadcast | bytes 8 | tf_op args[6]
  9.3 1.4 %reduce.3 = f32[4096]{0:T(1024)S(1)} reduce(f32[1,4096]{1,0:T(1,128)} %param.14, f32[]{:T(128)} %broadcast.3), dimensions={0}, to_apply=%param.14.reduce_sub_computation.3 | reduce | bytes 32772 | tf_op args[6]
  10.8 1.2 %copy-done.1 = bf16[8,1,16,4096]{3,2,1,0:T(8,128)(2,1)S(1)} copy-done((bf16[8,1,16,4096]{3,2,1,0:T(8,128)(2,1)S(1)}, bf16[8,1,16,4096]{3,2,1,0:T(8,128)(2,1)}, u32[]{:S(2)}) %copy-start.1) | copy-done | bytes 1048600
  12.0 1.2 %copy-done.2 = bf16[8,1,16,4096]{3,2,1,0:T(8,128)(2,1)S(1)} copy-done((bf16[8,1,16,4096]{3,2,1,0:T(8,128)(2,1)S(1)}, bf16[8,1,16,4096]{3,2,1,0:T(8,128)(2,1)}, u32[]{:S(2)}) %copy-start.2) | copy-done | bytes 1048600
  13.3 0.9 %copy-done.3 = bf16[1,64,1024]{2,1,0:T(8,128)(2,1)S(1)} copy-done((bf16[1,64,1024]{2,1,0:T(8,128)(2,1)S(1)}, bf16[1,64,1024]{2,1,0:T(8,128)(2,1)}, u32[]{:S(2)}) %copy-start.3) | copy-done | bytes 131096
  14.2 0.9 %copy-done.6 = bf16[1,64,1024]{2,1,0:T(8,128)(2,1)S(1)} copy-done((bf16[1,64,1024]{2,1,0:T(8,128)(2,1)S(1)}, bf16[1,64,1024]{2,1,0:T(8,128)(2,1)}, u32[]{:S(2)}) %copy-start.6) | copy-done | bytes 131096
  15.5 2.0 %collective-permute-start.1 = (bf16[64,1024]{1,0:T(8,128)(2,1)S(1)}, bf16[64,1024]{1,0:T(8,128)(2,1)S(1)}, u32[]{:S(2)}, u32[]{:S(2)}) collective-permute-start(bf16[64,1024]{1,0:T(8,128)(2,1)S(1)} %collective-permute-done.refs_0_), channel_id=1, source_target_pairs={{0,16},{16,0},{1,17},{17,1},{2,18},{18,2},{3,19},{19,3},{4,20},{20... | collective-permute-start | bytes 393224 | tf_op jit(solution)/shard_map/ppermute | solution.py:156
  17.6 1.6 %collective-permute-done.4.refs_2_ = bf16[64,512]{1,0:T(8,128)(2,1)S(1)} collective-permute-done((bf16[64,512]{1,0:T(8,128)(2,1)S(1)}, bf16[64,512]{1,0:T(8,128)(2,1)S(1)}, u32[]{:S(2)}, u32[]{:S(2)}) %collective-permute-start.4) | collective-permute-done | bytes 65568 | tf_op jit(solution)/shard_map/ppermute | solution.py:149
  19.1 2.6 %collective-permute-start.5 = (bf16[64,512]{1,0:T(8,128)(2,1)S(1)}, bf16[64,512]{1,0:T(8,128)(2,1)S(1)}, u32[]{:S(2)}, u32[]{:S(2)}) collective-permute-start(bf16[64,512]{1,0:T(8,128)(2,1)S(1)} %collective-permute-done.4.refs_2_), channel_id=1, source_target_pairs={{0,16},{16,0},{1,17},{17,1},{2,18},{18,2},{3,19},{19,3},{4,20},{20... | collective-permute-start | bytes 196616 | tf_op jit(solution)/shard_map/ppermute | solution.py:156
  22.3 1.9 %collective-permute-done.5.refs_2_ = bf16[64,512]{1,0:T(8,128)(2,1)S(1)} collective-permute-done((bf16[64,512]{1,0:T(8,128)(2,1)S(1)}, bf16[64,512]{1,0:T(8,128)(2,1)S(1)}, u32[]{:S(2)}, u32[]{:S(2)}) %collective-permute-start.5) | collective-permute-done | bytes 65568 | tf_op jit(solution)/shard_map/ppermute | solution.py:156
  24.5 2.6 %collective-permute-start.7 = (bf16[128,128]{1,0:T(8,128)(2,1)S(1)}, bf16[128,128]{1,0:T(8,128)(2,1)S(1)}, u32[]{:S(2)}, u32[]{:S(2)}) collective-permute-start(bf16[128,128]{1,0:T(8,128)(2,1)S(1)} %sides.5.refs_0_), channel_id=1, source_target_pairs={{0,12},{4,8},{8,4},{12,0},{1,13},{5,9},{9,5},{13,1},{2,14},{6,10},... | collective-permute-start | bytes 98312 | tf_op jit(solution)/shard_map/ppermute | solution.py:149
  27.1 0.7 %collective-permute-start.8 = (bf16[128,128]{1,0:T(8,128)(2,1)S(1)}, bf16[128,128]{1,0:T(8,128)(2,1)S(1)}, u32[]{:S(2)}, u32[]{:S(2)}) collective-permute-start(bf16[128,128]{1,0:T(8,128)(2,1)S(1)} %sides.5.refs_0_), channel_id=1, source_target_pairs={{0,8},{4,12},{8,0},{12,4},{1,9},{5,13},{9,1},{13,5},{2,10},{6,14},... | collective-permute-start | bytes 98312 | tf_op jit(solution)/shard_map/ppermute | solution.py:149
  27.8 1.2 %collective-permute-start.9 = (bf16[128,128]{1,0:T(8,128)(2,1)S(1)}, bf16[128,128]{1,0:T(8,128)(2,1)S(1)}, u32[]{:S(2)}, u32[]{:S(2)}) collective-permute-start(bf16[128,128]{1,0:T(8,128)(2,1)S(1)} %sides.5.refs_0_), channel_id=1, source_target_pairs={{0,4},{4,0},{8,12},{12,8},{1,5},{5,1},{9,13},{13,9},{2,6},{6,2},{1... | collective-permute-start | bytes 98312 | tf_op jit(solution)/shard_map/ppermute | solution.py:149
  29.0 1.9 %scores.2 = (f32[8,80]{1,0:T(8,128)S(1)}, f32[8,80]{1,0:T(8,128)S(1)}, f32[8,80]{1,0:T(8,128)S(1)}, f32[8,80]{1,0:T(8,128)S(1)}) custom-call(f32[64,64]{1,0:T(8,128)S(1)} %bitcast.21, f32[64,64]{1,0:T(8,128)S(1)} %bitcast.23, f32[64,64]{1,0:T(8,128)S(1)} %reshape.15.eigen, bf16[320,4096]{1,0:T(8,128)(2,1)S(1)} %bitcast.11, bf16[128,128]{1,0:T(8,128)(2,1)S(1)} %sides.5.refs_0_), custom_call_target="tpu_custom_call" | custom-call | tf_op jit(solution)/shard_map/scores/pallas_call | solution.py:185
  30.9 1.1 %collective-permute-done.8.refs_1_ = bf16[128,128]{1,0:T(8,128)(2,1)S(1)} collective-permute-done((bf16[128,128]{1,0:T(8,128)(2,1)S(1)}, bf16[128,128]{1,0:T(8,128)(2,1)S(1)}, u32[]{:S(2)}, u32[]{:S(2)}) %collective-permute-start.8) | collective-permute-done | bytes 32800 | tf_op jit(solution)/shard_map/ppermute | solution.py:149
  32.0 2.7 %scores.3 = (f32[32,80]{1,0:T(8,128)S(1)}, f32[32,80]{1,0:T(8,128)S(1)}, f32[32,80]{1,0:T(8,128)S(1)}, f32[32,80]{1,0:T(8,128)S(1)}) custom-call(f32[64,64]{1,0:T(8,128)S(1)} %bitcast.22, f32[64,64]{1,0:T(8,128)S(1)} %bitcast.24, f32[64,64]{1,0:T(8,128)S(1)} %reshape.15.eigen, bf16[320,4096]{1,0:T(8,128)(2,1)S(1)} %bitcast.12, ...), custom_call_target="tpu_custom_call" | custom-call | tf_op jit(solution)/shard_map/scores/pallas_call | solution.py:185
  34.9 1.6 %collective-permute-start.11 = (f32[32,80]{1,0:T(8,128)S(1)}, f32[32,80]{1,0:T(8,128)S(1)}, u32[]{:S(2)}, u32[]{:S(2)}) collective-permute-start(f32[32,80]{1,0:T(8,128)S(1)} %get-tuple-element.25), channel_id=1, source_target_pairs={{0,2},{1,3},{2,0},{3,1},{4,6},{5,7},{6,4},{7,5},{8,10},{9,11},{10,... | collective-permute-start | bytes 30728 | tf_op jit(solution)/shard_map/ppermute | solution.py:230
  36.7 1.9 %collective-permute-done.11 = f32[32,80]{1,0:T(8,128)S(1)} collective-permute-done((f32[32,80]{1,0:T(8,128)S(1)}, f32[32,80]{1,0:T(8,128)S(1)}, u32[]{:S(2)}, u32[]{:S(2)}) %collective-permute-start.11) | collective-permute-done | bytes 10272 | tf_op jit(solution)/shard_map/ppermute | solution.py:230
  38.7 0.9 %collective-permute-done.12 = f32[32,80]{1,0:T(8,128)S(1)} collective-permute-done((f32[32,80]{1,0:T(8,128)S(1)}, f32[32,80]{1,0:T(8,128)S(1)}, u32[]{:S(2)}, u32[]{:S(2)}) %collective-permute-start.12) | collective-permute-done | bytes 10272 | tf_op jit(solution)/shard_map/ppermute | solution.py:230
  39.6 0.6 %add_bitcast_fusion = f32[80,32]{0,1:T(8,128)} fusion(f32[32,80]{1,0:T(8,128)S(1)} %collective-permute-done.12, f32[32,80]{1,0:T(8,128)S(1)} %collective-permute-done.11, f32[32,80]{1,0:T(8,128)S(1)} %get-tuple-element.23, f32[32,80]{1,0:T(8,128)S(1)} %collective-permute-done.10), kind=kLoop, calls=%fused_computation.1 | loop fusion | flops 7680 | bytes 51200 | tf_op jit(solution)/shard_map/transpose | solution.py:231
  (26 shorter events, 1.7 us)
Async XLA Ops:
  0.0 15.5 %collective-permute-start = (bf16[64,1024]{1,0:T(8,128)(2,1)}, bf16[64,1024]{1,0:T(8,128)(2,1)S(1)}, u32[]{:S(2)}, u32[]{:S(2)}) collective-permute-start(bf16[64,1024]{1,0:T(8,128)(2,1)} %bitcast.25), channel_id=1, source_target_pairs={{0,12},{4,8},{8,4},{12,0},{16,20},{20,16},{24,28},{28,24},{1,13},{... | collective-permute-start | bytes 393224 | tf_op jit(solution)/shard_map/ppermute | solution.py:153
  5.0 12.5 %collective-permute-start.2 = (bf16[64,1024]{1,0:T(8,128)(2,1)}, bf16[64,1024]{1,0:T(8,128)(2,1)S(1)}, u32[]{:S(2)}, u32[]{:S(2)}) collective-permute-start(bf16[64,1024]{1,0:T(8,128)(2,1)} %bitcast.19), channel_id=1, source_target_pairs={{0,4},{4,0},{8,12},{12,8},{16,28},{20,24},{24,20},{28,16},{1,5},{5... | collective-permute-start | bytes 393224 | tf_op jit(solution)/shard_map/ppermute | solution.py:153
  5.1 16.7 %collective-permute-start.6 = (bf16[64,1024]{1,0:T(8,128)(2,1)}, bf16[64,1024]{1,0:T(8,128)(2,1)S(1)}, u32[]{:S(2)}, u32[]{:S(2)}) collective-permute-start(bf16[64,1024]{1,0:T(8,128)(2,1)} %bitcast.26), channel_id=1, source_target_pairs={{0,8},{4,12},{8,0},{12,4},{1,9},{5,13},{9,1},{13,5},{2,10},{6,14},... | collective-permute-start | bytes 393224 | tf_op jit(solution)/shard_map/ppermute | solution.py:149
  6.5 12.7 %collective-permute-start.4 = (bf16[64,512]{1,0:T(8,128)(2,1)S(1)}, bf16[64,512]{1,0:T(8,128)(2,1)S(1)}, u32[]{:S(2)}, u32[]{:S(2)}) collective-permute-start(bf16[64,512]{1,0:T(8,128)(2,1)S(1)} %dynamic-slice_bitcast_fusion), channel_id=1, source_target_pairs={{0,8},{4,12},{8,0},{12,4},{1,9},{5,13},{9,1},{13,5},{2,10},{6,14},... | collective-permute-start | bytes 196616 | tf_op jit(solution)/shard_map/ppermute | solution.py:149
  10.8 1.2 %copy-start.1 = (bf16[8,1,16,4096]{3,2,1,0:T(8,128)(2,1)S(1)}, bf16[8,1,16,4096]{3,2,1,0:T(8,128)(2,1)}, u32[]{:S(2)}) copy-start(bf16[8,1,16,4096]{3,2,1,0:T(8,128)(2,1)} %param.8) | copy-start | bytes 3145732
  12.0 1.2 %copy-start.2 = (bf16[8,1,16,4096]{3,2,1,0:T(8,128)(2,1)S(1)}, bf16[8,1,16,4096]{3,2,1,0:T(8,128)(2,1)}, u32[]{:S(2)}) copy-start(bf16[8,1,16,4096]{3,2,1,0:T(8,128)(2,1)} %param.9) | copy-start | bytes 3145732
  13.3 0.9 %copy-start.3 = (bf16[1,64,1024]{2,1,0:T(8,128)(2,1)S(1)}, bf16[1,64,1024]{2,1,0:T(8,128)(2,1)}, u32[]{:S(2)}) copy-start(bf16[1,64,1024]{2,1,0:T(8,128)(2,1)} %param.11) | copy-start | bytes 393220
  14.2 0.9 %copy-start.6 = (bf16[1,64,1024]{2,1,0:T(8,128)(2,1)S(1)}, bf16[1,64,1024]{2,1,0:T(8,128)(2,1)}, u32[]{:S(2)}) copy-start(bf16[1,64,1024]{2,1,0:T(8,128)(2,1)} %param.10) | copy-start | bytes 393220
  15.4 13.6 %copy-start = (bf16[320,1,4096]{2,0,1:T(8,128)(2,1)S(1)}, bf16[320,1,4096]{2,0,1:T(8,128)(2,1)}, u32[]{:S(2)}) copy-start(bf16[320,1,4096]{2,0,1:T(8,128)(2,1)} %param.15) | copy-start | bytes 7864324
  15.4 13.6 %copy-start.4 = (f32[1,64,64]{2,1,0:T(8,128)S(1)}, f32[1,64,64]{2,1,0:T(8,128)}, u32[]{:S(2)}) copy-start(f32[1,64,64]{2,1,0:T(8,128)} %param.12) | copy-start | bytes 49156
  15.4 13.6 %copy-start.5 = (f32[1,64,64]{2,1,0:T(8,128)S(1)}, f32[1,64,64]{2,1,0:T(8,128)}, u32[]{:S(2)}) copy-start(f32[1,64,64]{2,1,0:T(8,128)} %param.13) | copy-start | bytes 49156
  15.5 8.7 %collective-permute-start.1 = (bf16[64,1024]{1,0:T(8,128)(2,1)S(1)}, bf16[64,1024]{1,0:T(8,128)(2,1)S(1)}, u32[]{:S(2)}, u32[]{:S(2)}) collective-permute-start(bf16[64,1024]{1,0:T(8,128)(2,1)S(1)} %collective-permute-done.refs_0_), channel_id=1, source_target_pairs={{0,16},{16,0},{1,17},{17,1},{2,18},{18,2},{3,19},{19,3},{4,20},{20... | collective-permute-start | bytes 393224 | tf_op jit(solution)/shard_map/ppermute | solution.py:156
  17.5 6.7 %collective-permute-start.3 = (bf16[64,1024]{1,0:T(8,128)(2,1)S(1)}, bf16[64,1024]{1,0:T(8,128)(2,1)S(1)}, u32[]{:S(2)}, u32[]{:S(2)}) collective-permute-start(bf16[64,1024]{1,0:T(8,128)(2,1)S(1)} %collective-permute-done.2.refs_1_), channel_id=1, source_target_pairs={{0,16},{16,0},{1,17},{17,1},{2,18},{18,2},{3,19},{19,3},{4,20},{20... | collective-permute-start | bytes 393224 | tf_op jit(solution)/shard_map/ppermute | solution.py:156
  19.1 5.0 %collective-permute-start.5 = (bf16[64,512]{1,0:T(8,128)(2,1)S(1)}, bf16[64,512]{1,0:T(8,128)(2,1)S(1)}, u32[]{:S(2)}, u32[]{:S(2)}) collective-permute-start(bf16[64,512]{1,0:T(8,128)(2,1)S(1)} %collective-permute-done.4.refs_2_), channel_id=1, source_target_pairs={{0,16},{16,0},{1,17},{17,1},{2,18},{18,2},{3,19},{19,3},{4,20},{20... | collective-permute-start | bytes 196616 | tf_op jit(solution)/shard_map/ppermute | solution.py:156
  24.5 6.4 %collective-permute-start.7 = (bf16[128,128]{1,0:T(8,128)(2,1)S(1)}, bf16[128,128]{1,0:T(8,128)(2,1)S(1)}, u32[]{:S(2)}, u32[]{:S(2)}) collective-permute-start(bf16[128,128]{1,0:T(8,128)(2,1)S(1)} %sides.5.refs_0_), channel_id=1, source_target_pairs={{0,12},{4,8},{8,4},{12,0},{1,13},{5,9},{9,5},{13,1},{2,14},{6,10},... | collective-permute-start | bytes 98312 | tf_op jit(solution)/shard_map/ppermute | solution.py:149
  27.1 4.9 %collective-permute-start.8 = (bf16[128,128]{1,0:T(8,128)(2,1)S(1)}, bf16[128,128]{1,0:T(8,128)(2,1)S(1)}, u32[]{:S(2)}, u32[]{:S(2)}) collective-permute-start(bf16[128,128]{1,0:T(8,128)(2,1)S(1)} %sides.5.refs_0_), channel_id=1, source_target_pairs={{0,8},{4,12},{8,0},{12,4},{1,9},{5,13},{9,1},{13,5},{2,10},{6,14},... | collective-permute-start | bytes 98312 | tf_op jit(solution)/shard_map/ppermute | solution.py:149
  27.8 4.3 %collective-permute-start.9 = (bf16[128,128]{1,0:T(8,128)(2,1)S(1)}, bf16[128,128]{1,0:T(8,128)(2,1)S(1)}, u32[]{:S(2)}, u32[]{:S(2)}) collective-permute-start(bf16[128,128]{1,0:T(8,128)(2,1)S(1)} %sides.5.refs_0_), channel_id=1, source_target_pairs={{0,4},{4,0},{8,12},{12,8},{1,5},{5,1},{9,13},{13,9},{2,6},{6,2},{1... | collective-permute-start | bytes 98312 | tf_op jit(solution)/shard_map/ppermute | solution.py:149
  34.8 1.9 %collective-permute-start.10 = (f32[32,80]{1,0:T(8,128)S(1)}, f32[32,80]{1,0:T(8,128)S(1)}, u32[]{:S(2)}, u32[]{:S(2)}) collective-permute-start(f32[32,80]{1,0:T(8,128)S(1)} %get-tuple-element.24), channel_id=1, source_target_pairs={{0,1},{1,0},{2,3},{3,2},{4,5},{5,4},{6,7},{7,6},{8,9},{9,8},{10,11... | collective-permute-start | bytes 30728 | tf_op jit(solution)/shard_map/ppermute | solution.py:230
  34.9 3.8 %collective-permute-start.11 = (f32[32,80]{1,0:T(8,128)S(1)}, f32[32,80]{1,0:T(8,128)S(1)}, u32[]{:S(2)}, u32[]{:S(2)}) collective-permute-start(f32[32,80]{1,0:T(8,128)S(1)} %get-tuple-element.25), channel_id=1, source_target_pairs={{0,2},{1,3},{2,0},{3,1},{4,6},{5,7},{6,4},{7,5},{8,10},{9,11},{10,... | collective-permute-start | bytes 30728 | tf_op jit(solution)/shard_map/ppermute | solution.py:230
  36.4 3.2 %collective-permute-start.12 = (f32[32,80]{1,0:T(8,128)S(1)}, f32[32,80]{1,0:T(8,128)S(1)}, u32[]{:S(2)}, u32[]{:S(2)}) collective-permute-start(f32[32,80]{1,0:T(8,128)S(1)} %get-tuple-element.26), channel_id=1, source_target_pairs={{0,3},{1,2},{2,1},{3,0},{4,7},{5,6},{6,5},{7,4},{8,11},{9,10},{10,... | collective-permute-start | bytes 30728 | tf_op jit(solution)/shard_map/ppermute | solution.py:230

commit v3 on v2

--- a/solution.py
+++ b/solution.py
@@ -55,51 +55,87 @@
     sides[...] = result.astype(sides.dtype)
 
 
-def scores_kernel(sources, shifts, tokens, in_basis, out_basis, eigen, train, *refs):
+def prepare_kernel(in_own, out_own, acts, outgrads, in_basis, out_basis, eigen, *refs):
+    total, acts_here, outgrads_here, turn, back, turns, inverse = refs[:7]
+    in_here, out_here, u_in, u_out, values, spread, sems = refs[7:]
+    width = in_own.shape[1]
+    pairs = [(in_basis, u_in), (out_basis, u_out), (eigen, values)]
+    pairs += [(in_own, in_here), (out_own, out_here), (acts, acts_here), (outgrads, outgrads_here)]
+    copies = [pltpu.make_async_copy(a, b, sems.at[i]) for i, (a, b) in enumerate(pairs)]
+    for copy in copies:
+        copy.start()
+    for copy in copies[:3]:
+        copy.wait()
+    lay_out(u_in, u_out, values, turn, back, turns, inverse, spread)
+    for copy in copies[3:]:
+        copy.wait()
+    columns = pl.ds(pl.multiple_of(lax.axis_index("corpus") * width, 128), width)
+    total[...] = jnp.concatenate(
+        [dot(outgrads_here[:, columns], out_here[...], nt), dot(acts_here[:, columns], in_here[...], nt)], axis=1
+    )
+
+
+def lay_out(in_basis, out_basis, eigen, turn, back, turns, inverse, spread):
+    rank = in_basis.shape[0]
+    across = lanes // rank
+    for at in range(rank):
+        spread[at : at + 1, :] = eigen[:, at * rank : (at + 1) * rank]
+    inverse[...] = jnp.concatenate([1.0 / (spread[...] + damping)] * across, axis=1)
+    out_high, out_low = split(out_basis[...])
+    u_in = in_basis[...]
+    in_high, in_low = split(u_in)
+    for at, (of_out, of_in) in enumerate(((out_high, in_high), (out_low, in_low))):
+        zero = jnp.zeros_like(of_out)
+        top = jnp.concatenate([of_out, of_out, zero, zero], axis=1)
+        bottom = jnp.concatenate([zero, zero, of_in, of_in], axis=1)
+        turn[:, at * lanes : (at + 1) * lanes] = jnp.concatenate([top, bottom], axis=0)
+    back[...] = jnp.concatenate([out_high, out_low, out_high], axis=1)
+    for at, part in enumerate(split(tiled_diagonal(u_in.T, across))):
+        turns[at * lanes : (at + 1) * lanes, :] = part
+
+
+def scores_kernel(sources, shifts, tokens, turn, back, turns, inverse, train, *refs):
     blocks, (scratch, rows, tall) = refs[:sources], refs[-3:]
     layers = lax.axis_size("layer")
     given = refs[sources : -3 - layers]
     outs = refs[-3 - layers : -3]
-    rank = in_basis.shape[0]
+    rank = turn.shape[0] // 2
     across = lanes // rank
     here = blocks[0].shape[0] // tokens
     queries = here * sources
     groups = queries // across
-    u_in, u_out = in_basis[...], out_basis[...]
-    inverse = 1.0 / (eigen[...] + damping)
-    inverse = jnp.concatenate([inverse] * across, axis=1)
-    out_high, out_low = split(u_out)
-    turn = jnp.concatenate([out_high, out_low], axis=0)
-    back = jnp.concatenate([out_high, out_low, out_high], axis=1)
-    in_high, in_low = split(tiled_diagonal(u_in, across))
-    tin_high, tin_low = split(tiled_diagonal(u_in.T, across))
+    back, inverse = back[...], inverse[...] * (1.0 / tokens)
     mask = (
         lax.broadcasted_iota(jnp.int32, (across * tokens, lanes), 0) // tokens
         == lax.broadcasted_iota(jnp.int32, (across * tokens, lanes), 1) // rank
     )
-    parts = [[] for _ in range(groups)]
+    parts = []
+    for block in blocks:
+        both = dot(block[...], turn[...])
+        parts.append(split(both[:, :lanes] + both[:, lanes:]))
+    scaled = []
     for group in range(groups):
+        high, low = [], []
         for j in range(across):
             query = j * groups + group
             start = query % here * tokens
-            parts[group].append(blocks[query // here][start : start + tokens, :])
-    turned = []
-    for group in range(groups):
-        both = jnp.concatenate(parts[group], axis=0)
-        out_side = both[:, :rank]
-        in_side = jnp.concatenate([both[:, rank:]] * across, axis=1)
-        in_side = jnp.where(mask, in_side, jnp.zeros_like(in_side))
-        gradient = (dot(out_side, in_side, tn) * (1.0 / tokens)).astype(bf16)
-        turned.append(dot(turn, jnp.concatenate([gradient, gradient], axis=0), tn))
-    turned = jnp.concatenate(turned, axis=0)
-    turned = product3(turned, in_high, in_low)
-    scaled = []
-    for group in range(groups):
-        part = turned[group * rank : (group + 1) * rank] * inverse
-        high, low = split(part)
+            for kept, part in zip((high, low), parts[query // here]):
+                kept.append(part[start : start + tokens])
+        high, low = jnp.concatenate(high, axis=0), jnp.concatenate(low, axis=0)
+        out_high, out_low = high[:, :rank], low[:, :rank]
+        in_high, in_low = (
+            jnp.where(mask, jnp.concatenate([x[:, lanes // 2 :]] * 2, axis=1), jnp.zeros(mask.shape, bf16))
+            for x in (high, low)
+        )
+        gradient = dot(
+            jnp.concatenate([out_high, out_low, out_high], axis=0),
+            jnp.concatenate([in_high, in_high, in_low], axis=0),
+            tn,
+        )
+        high, low = split(gradient * inverse)
         scaled.append(dot(back, jnp.concatenate([high, high, low], axis=0)))
     scaled = jnp.concatenate(scaled, axis=0)
-    conditioned = product3(scaled, tin_high, tin_low)
+    conditioned = product3(scaled, turns[:lanes, :], turns[lanes:, :])
     for part in range(lanes // 128):
         scratch[part] = conditioned[:, part * 128 : (part + 1) * 128]
     for pair in range(rank // 2):
@@ -113,7 +149,10 @@
                 rows[j * groups : (j + 1) * groups, columns] = jnp.concatenate(
                     [even[:, cut], odd[:, cut]], axis=1
                 )
-    tall[...] = dot(train[...], rows[...].astype(bf16), nt)
+    conditioned = rows[...].astype(bf16)
+    middle = train.shape[0] // 32 * 16
+    tall[:middle] = dot(train[:middle], conditioned, nt)
+    tall[middle:] = dot(train[middle:], conditioned, nt)
     layer, place = lax.axis_index("layer"), lax.axis_index("corpus")
     slab_rows = train.shape[0] // layers
     for shift, out in enumerate(outs):
@@ -155,17 +194,44 @@
     def swapped(x):
         return lax.ppermute(x, "groups", [(0, 1), (1, 0)])
 
-    def sides_call(plan, pieces, total, dtype):
+    def sides_call(plan, pieces, totals, dtype):
         return pl.pallas_call(
             functools.partial(sides_kernel, plan),
             out_shape=jax.ShapeDtypeStruct((queries_here * tokens, 2 * rank), dtype),
-            in_specs=[vmem] * (2 + len(pieces) + len(total)),
+            in_specs=[vmem] * (2 + len(pieces) + len(totals)),
             out_specs=vmem,
             compiler_params=params,
             name="sides",
-        )(acts, outgrads, *pieces, *total)
-
-    eigen = eig_values.reshape(rank, rank)
+        )(acts, outgrads, *pieces, *totals)
+
+    stay = functools.partial(pltpu.with_memory_space_constraint, memory_space=pltpu.HBM)
+    hbm = pl.BlockSpec(memory_space=pltpu.HBM)
+    prepared = pl.pallas_call(
+        prepare_kernel,
+        out_shape=[
+            jax.ShapeDtypeStruct((queries_here * tokens, 2 * rank), f32),
+            jax.ShapeDtypeStruct(acts.shape, bf16),
+            jax.ShapeDtypeStruct(acts.shape, bf16),
+            jax.ShapeDtypeStruct((2 * rank, 2 * lanes), bf16),
+            jax.ShapeDtypeStruct((rank, 3 * rank), bf16),
+            jax.ShapeDtypeStruct((2 * lanes, lanes), bf16),
+            jax.ShapeDtypeStruct((rank, lanes), f32),
+        ],
+        in_specs=[hbm] * 7,
+        out_specs=[vmem] * 7,
+        scratch_shapes=[
+            pltpu.VMEM((rank, width), bf16),
+            pltpu.VMEM((rank, width), bf16),
+            pltpu.VMEM((rank, rank), f32),
+            pltpu.VMEM((rank, rank), f32),
+            pltpu.VMEM((1, rank * rank), f32),
+            pltpu.VMEM((rank, rank), f32),
+            pltpu.SemaphoreType.DMA((7,)),
+        ],
+        compiler_params=params,
+        name="prepare",
+    )(*(stay(x) for x in (in_own, out_own, acts, outgrads, in_basis[0], out_basis[0], eig_values)))
+    total, acts, outgrads = prepared[:3]
     train = train_grads.reshape(train_grads.shape[0], rank * rank)
     rows_out = train.shape[0] // layers
 
@@ -177,11 +243,11 @@
         if chunk:
             specs = dict(
                 grid=(chunk,),
-                in_specs=[vmem] * 4 + [pl.BlockSpec((here * tokens, 2 * rank), lambda i: (i, 0))],
+                in_specs=[vmem] * 5 + [pl.BlockSpec((here * tokens, 2 * rank), lambda i: (i, 0))],
                 out_specs=[pl.BlockSpec((out_rows, rows_out), lambda i: (i, 0))] * layers,
             )
         else:
-            specs = dict(in_specs=[vmem] * (4 + len(blocks) + len(given)), out_specs=[vmem] * layers)
+            specs = dict(in_specs=[vmem] * (5 + len(blocks) + len(given)), out_specs=[vmem] * layers)
         return pl.pallas_call(
             functools.partial(scores_kernel, len(blocks), shifts, tokens),
             out_shape=[jax.ShapeDtypeStruct((queries, rows_out), f32)] * layers,
@@ -193,29 +259,21 @@
             compiler_params=params,
             name="scores",
             **specs,
-        )(in_basis[0], out_basis[0], eigen, train, *blocks, *given)
+        )(*prepared[3:], train, *blocks, *given)
 
     if places == 4 and lax.axis_size("groups") == 2:
         part = width // 2
         near = mixed(in_own, (3, 1))
         near_out = mixed(out_own, (1, 3))
-        cut = far(lax.dynamic_slice_in_dim(out_own, lax.axis_index("groups") * part, part, 1), 2)
-        last = far(in_own, 2)
+        last, last_out = far(in_own, 2), far(out_own, 2)
+        near, total = lax.optimization_barrier((near, total))
         direct = lambda g, p: (p ^ 2) * width
-        first, second = (lambda g, p: (p ^ (3 - 2 * g)) * width), (lambda g, p: (p ^ (1 + 2 * g)) * width)
+        first = lambda g, p: (p ^ jnp.where(g == 0, 3, 1)) * width
+        second = lambda g, p: (p ^ jnp.where(g == 0, 1, 3)) * width
         mine = lambda g, p: (p ^ 2) * width + g * part
         other = lambda g, p: (p ^ 2) * width + (1 - g) * part
-        total = sides_call([(1, lambda g, p: p * width), (0, lambda g, p: p * width)], [in_own, out_own], [], f32)
-        near, total, eigen = lax.optimization_barrier((near, total, eigen))
-        total = sides_call(
-            [(1, first), (0, second), (0, mine), (1, direct)], [near, near_out, cut, last], [total], f32
-        )
-        sides = sides_call(
-            [(1, second), (0, first), (0, other)],
-            [swapped(near), swapped(near_out), swapped(cut)],
-            [total],
-            bf16,
-        )
+        total = sides_call([(1, first), (0, second)], [near, near_out], [total], f32)
+        sides = sides_call([(1, second), (0, first), (1, direct), (0, direct)], [swapped(near), swapped(near_out), last, last_out], [total], bf16)
         arrived = [far(sides, shift) for shift in (3, 2, 1)]
         own = scores_call(None, [sides], [], None)
         slabs = scores_call((3, 2, 1), arrived, own, None)

time: 40.5 us -> 37.5 us (0.926)
  local copies, waits for them, and re-layouts: 5.7 us -> 0.01 us
  waiting for transfers between devices: 7.48 us -> 11.1 us
  other arithmetic: 2.01 us -> 0.61 us
  Pallas kernels: 5.78 us -> 7.05 us
  starting transfers between devices: 19.1 us -> 18.5 us
    ppermute x5, waiting for transfers between devices: 2.7 us -> 8.09 us  [far(): return lax.ppermute(x, 'corpus', [(i, i ^ shift) for i in range(places)])]
    unnamed x15 -> x2, local copies, waits for them, and re-layouts: 4.79 us -> 0.01 us
    pallas_call x0 -> x1, Pallas kernels: none -> 2.14 us  [body(): pl.pallas_call(prepare_kernel, out_shape=[jax.ShapeDtypeStruct((queries_h...]
    ppermute x3 -> x2, waiting for transfers between devices: 1.92 us -> 0.01 us  [swapped(): return lax.ppermute(x, 'groups', [(0, 1), (1, 0)])]
    unnamed x1 -> x0, other arithmetic: 1.4 us -> none
    ppermute x3 -> x2, starting transfers between devices: 4.77 us -> 3.87 us  [swapped(): return lax.ppermute(x, 'groups', [(0, 1), (1, 0)])]
    dynamic_slice x1 -> x0, local copies, waits for them, and re-layouts: 0.84 us -> none  [body(): lax.dynamic_slice_in_dim(out_own, lax.axis_index('groups') * part, part, 1)]
    pallas_call x2, Pallas kernels: 4.64 us -> 4.08 us  [scores_call(): pl.pallas_call(functools.partial(scores_kernel, len(blocks), shifts, toke...]
  transfers between devices with their start and end apart: 13 -> 12, of which waited for: 5 -> 6; matrix products, arithmetic and copies ran while one was open for 7% -> 0% of each run, Pallas kernels for 7% -> 12%
where the time goes in v3:
time: 37.5 us; the launch traced here: 37.3 us
  starting transfers between devices  18.5 us (49%)
  waiting for transfers between devices  11.1 us (30%)
  Pallas kernels  7.05 us (19%)
  other arithmetic  0.61 us (2%)
    ppermute x5, waiting for transfers between devices, far(): return lax.ppermute(x, 'corpus', [(i, i ^ shift) for i in range(places)])  8.09 us
    ppermute x5, starting transfers between devices, far(): return lax.ppermute(x, 'corpus', [(i, i ^ shift) for i in range(places)])  7.38 us
    ppermute x2, starting transfers between devices, mixed(): return lax.ppermute(x, ('groups', 'corpus'), pairs)  5.05 us
    pallas_call x2, Pallas kernels, scores_call(): pl.pallas_call(functools.partial(scores_kernel, len(blocks), shifts, toke...  4.08 us
    ppermute x2, starting transfers between devices, swapped(): return lax.ppermute(x, 'groups', [(0, 1), (1, 0)])  3.87 us
    ppermute x3, waiting for transfers between devices, body(): lax.ppermute(slabs[shift], 'layer', [(i, i ^ shift) for i in range(layers)])  2.53 us
    ppermute x3, starting transfers between devices, body(): lax.ppermute(slabs[shift], 'layer', [(i, i ^ shift) for i in range(layers)])  2.21 us
    pallas_call x1, Pallas kernels, body(): pl.pallas_call(prepare_kernel, out_shape=[jax.ShapeDtypeStruct((queries_h...  2.14 us
  transfers between devices with their start and end apart: 12, of which 6 were waited for; matrix products, arithmetic and copies ran while one was open for 0% of the time, Pallas kernels for 12%

profile of v3, /device:TPU:0, one launch (start us, length us, event | category | flops | bytes accessed | tf_op | source)
XLA Modules:
  0.0 37.3 jit_solution(16607375690351317146)
XLA Ops:
  0.0 5.0 %collective-permute-start = (bf16[64,1024]{1,0:T(8,128)(2,1)}, bf16[64,1024]{1,0:T(8,128)(2,1)S(1)}, u32[]{:S(2)}, u32[]{:S(2)}) collective-permute-start(bf16[64,1024]{1,0:T(8,128)(2,1)} %bitcast.13), channel_id=1, source_target_pairs={{0,12},{4,8},{8,4},{12,0},{16,20},{20,16},{24,28},{28,24},{1,13},{... | collective-permute-start | bytes 393224 | tf_op jit(solution)/shard_map/ppermute | solution.py:192
  5.1 0.6 %collective-permute-start.4 = (bf16[64,1024]{1,0:T(8,128)(2,1)}, bf16[64,1024]{1,0:T(8,128)(2,1)S(1)}, u32[]{:S(2)}, u32[]{:S(2)}) collective-permute-start(bf16[64,1024]{1,0:T(8,128)(2,1)} %bitcast.14), channel_id=1, source_target_pairs={{0,8},{4,12},{8,0},{12,4},{1,9},{5,13},{9,1},{13,5},{2,10},{6,14},... | collective-permute-start | bytes 393224 | tf_op jit(solution)/shard_map/ppermute | solution.py:188
  5.6 2.4 %collective-permute-start.5 = (bf16[64,1024]{1,0:T(8,128)(2,1)}, bf16[64,1024]{1,0:T(8,128)(2,1)S(1)}, u32[]{:S(2)}, u32[]{:S(2)}) collective-permute-start(bf16[64,1024]{1,0:T(8,128)(2,1)} %bitcast.17), channel_id=1, source_target_pairs={{0,8},{4,12},{8,0},{12,4},{1,9},{5,13},{9,1},{13,5},{2,10},{6,14},... | collective-permute-start | bytes 393224 | tf_op jit(solution)/shard_map/ppermute | solution.py:188
  8.0 2.1 %prepare.1 = (f32[128,128]{1,0:T(8,128)S(1)}, bf16[128,4096]{1,0:T(8,128)(2,1)S(1)}, bf16[128,4096]{1,0:T(8,128)(2,1)S(1)}, bf16[128,512]{1,0:T(8,128)(2,1)S(1)}...) custom-call(bf16[64,1024]{1,0:T(8,128)(2,1)} %bitcast.15, ...), custom_call_target="tpu_custom_call" | custom-call | tf_op jit(solution)/shard_map/prepare/pallas_call | solution.py:209
  10.1 0.0 copy-start
  10.1 2.0 %collective-permute-start.1 = (bf16[64,1024]{1,0:T(8,128)(2,1)S(1)}, bf16[64,1024]{1,0:T(8,128)(2,1)S(1)}, u32[]{:S(2)}, u32[]{:S(2)}) collective-permute-start(bf16[64,1024]{1,0:T(8,128)(2,1)S(1)} %collective-permute-done.refs_0_), channel_id=1, source_target_pairs={{0,16},{16,0},{1,17},{17,1},{2,18},{18,2},{3,19},{19,3},{4,20},{20... | collective-permute-start | bytes 393224 | tf_op jit(solution)/shard_map/ppermute | solution.py:195
  12.2 0.5 %collective-permute-done.2.refs_1_ = bf16[64,1024]{1,0:T(8,128)(2,1)S(1)} collective-permute-done((bf16[64,1024]{1,0:T(8,128)(2,1)}, bf16[64,1024]{1,0:T(8,128)(2,1)S(1)}, u32[]{:S(2)}, u32[]{:S(2)}) %collective-permute-start.2) | collective-permute-done | bytes 131104 | tf_op jit(solution)/shard_map/ppermute | solution.py:192
  12.7 1.8 %collective-permute-start.3 = (bf16[64,1024]{1,0:T(8,128)(2,1)S(1)}, bf16[64,1024]{1,0:T(8,128)(2,1)S(1)}, u32[]{:S(2)}, u32[]{:S(2)}) collective-permute-start(bf16[64,1024]{1,0:T(8,128)(2,1)S(1)} %collective-permute-done.2.refs_1_), channel_id=1, source_target_pairs={{0,16},{16,0},{1,17},{17,1},{2,18},{18,2},{3,19},{19,3},{4,20},{20... | collective-permute-start | bytes 393224 | tf_op jit(solution)/shard_map/ppermute | solution.py:195
  14.5 0.3 sides.2.refs_4_
  14.9 5.2 %collective-permute-done.4.refs_2_ = bf16[64,1024]{1,0:T(8,128)(2,1)S(1)} collective-permute-done((bf16[64,1024]{1,0:T(8,128)(2,1)}, bf16[64,1024]{1,0:T(8,128)(2,1)S(1)}, u32[]{:S(2)}, u32[]{:S(2)}) %collective-permute-start.4) | collective-permute-done | bytes 131104 | tf_op jit(solution)/shard_map/ppermute | solution.py:188
  20.1 1.8 %collective-permute-done.5.refs_3_ = bf16[64,1024]{1,0:T(8,128)(2,1)S(1)} collective-permute-done((bf16[64,1024]{1,0:T(8,128)(2,1)}, bf16[64,1024]{1,0:T(8,128)(2,1)S(1)}, u32[]{:S(2)}, u32[]{:S(2)}) %collective-permute-start.5) | collective-permute-done | bytes 131104 | tf_op jit(solution)/shard_map/ppermute | solution.py:188
  22.0 0.0 collective-permute-done.1.refs_0_
  22.0 0.5 %sides.3.refs_0_ = bf16[128,128]{1,0:T(8,128)(2,1)S(1)} custom-call(bf16[128,4096]{1,0:T(8,128)(2,1)S(1)} %get-tuple-element.26.acts, bf16[128,4096]{1,0:T(8,128)(2,1)S(1)} %get-tuple-element.27.outgrads, bf16[64,1024]{1,0:T(8,128)(2,1)S(1)} %collective-permute-done.1.refs_0_, bf16[64,1024]{1,0:T(8,128)(2,1)S(1)} %collective-permute-done.3.refs_1_, ...), custom_call_target="tpu_custom_call" | custom-call | tf_op jit(solution)/shard_map/sides/pallas_call | solution.py:198
  22.5 2.5 %collective-permute-start.6 = (bf16[128,128]{1,0:T(8,128)(2,1)S(1)}, bf16[128,128]{1,0:T(8,128)(2,1)S(1)}, u32[]{:S(2)}, u32[]{:S(2)}) collective-permute-start(bf16[128,128]{1,0:T(8,128)(2,1)S(1)} %sides.3.refs_0_), channel_id=1, source_target_pairs={{0,12},{4,8},{8,4},{12,0},{1,13},{5,9},{9,5},{13,1},{2,14},{6,10},... | collective-permute-start | bytes 98312 | tf_op jit(solution)/shard_map/ppermute | solution.py:188
  25.0 0.5 %collective-permute-start.7 = (bf16[128,128]{1,0:T(8,128)(2,1)S(1)}, bf16[128,128]{1,0:T(8,128)(2,1)S(1)}, u32[]{:S(2)}, u32[]{:S(2)}) collective-permute-start(bf16[128,128]{1,0:T(8,128)(2,1)S(1)} %sides.3.refs_0_), channel_id=1, source_target_pairs={{0,8},{4,12},{8,0},{12,4},{1,9},{5,13},{9,1},{13,5},{2,10},{6,14},... | collective-permute-start | bytes 98312 | tf_op jit(solution)/shard_map/ppermute | solution.py:188
  25.5 1.4 %collective-permute-start.8 = (bf16[128,128]{1,0:T(8,128)(2,1)S(1)}, bf16[128,128]{1,0:T(8,128)(2,1)S(1)}, u32[]{:S(2)}, u32[]{:S(2)}) collective-permute-start(bf16[128,128]{1,0:T(8,128)(2,1)S(1)} %sides.3.refs_0_), channel_id=1, source_target_pairs={{0,4},{4,0},{8,12},{12,8},{1,5},{5,1},{9,13},{13,9},{2,6},{6,2},{1... | collective-permute-start | bytes 98312 | tf_op jit(solution)/shard_map/ppermute | solution.py:188
  26.9 1.9 %scores.2 = (f32[8,80]{1,0:T(8,128)S(1)}, f32[8,80]{1,0:T(8,128)S(1)}, f32[8,80]{1,0:T(8,128)S(1)}, f32[8,80]{1,0:T(8,128)S(1)}) custom-call(bf16[128,512]{1,0:T(8,128)(2,1)S(1)} %get-tuple-element.22.turn, bf16[64,192]{1,0:T(8,128)(2,1)S(1)} %get-tuple-element.23.back, bf16[512,256]{1,0:T(8,128)(2,1)S(1)} %get-tuple-element.24.turns, ...), custom_call_target="tpu_custom_call" | custom-call | tf_op jit(solution)/shard_map/scores/pallas_call | solution.py:251
  28.8 1.0 %collective-permute-done.7.refs_1_ = bf16[128,128]{1,0:T(8,128)(2,1)S(1)} collective-permute-done((bf16[128,128]{1,0:T(8,128)(2,1)S(1)}, bf16[128,128]{1,0:T(8,128)(2,1)S(1)}, u32[]{:S(2)}, u32[]{:S(2)}) %collective-permute-start.7) | collective-permute-done | bytes 32800 | tf_op jit(solution)/shard_map/ppermute | solution.py:188
  29.8 2.2 %scores.3 = (f32[32,80]{1,0:T(8,128)S(1)}, f32[32,80]{1,0:T(8,128)S(1)}, f32[32,80]{1,0:T(8,128)S(1)}, f32[32,80]{1,0:T(8,128)S(1)}) custom-call(bf16[128,512]{1,0:T(8,128)(2,1)S(1)} %get-tuple-element.22.turn, bf16[64,192]{1,0:T(8,128)(2,1)S(1)} %get-tuple-element.23.back, bf16[512,256]{1,0:T(8,128)(2,1)S(1)} %get-tuple-element.24.turns, ...), custom_call_target="tpu_custom_call" | custom-call | tf_op jit(solution)/shard_map/scores/pallas_call | solution.py:251
  32.0 1.6 %collective-permute-start.10 = (f32[32,80]{1,0:T(8,128)S(1)}, f32[32,80]{1,0:T(8,128)S(1)}, u32[]{:S(2)}, u32[]{:S(2)}) collective-permute-start(f32[32,80]{1,0:T(8,128)S(1)} %get-tuple-element.37), channel_id=1, source_target_pairs={{0,2},{1,3},{2,0},{3,1},{4,6},{5,7},{6,4},{7,5},{8,10},{9,11},{10,... | collective-permute-start | bytes 30728 | tf_op jit(solution)/shard_map/ppermute | solution.py:288
  33.6 0.6 %collective-permute-start.9 = (f32[32,80]{1,0:T(8,128)S(1)}, f32[32,80]{1,0:T(8,128)S(1)}, u32[]{:S(2)}, u32[]{:S(2)}) collective-permute-start(f32[32,80]{1,0:T(8,128)S(1)} %get-tuple-element.36), channel_id=1, source_target_pairs={{0,1},{1,0},{2,3},{3,2},{4,5},{5,4},{6,7},{7,6},{8,9},{9,8},{10,11... | collective-permute-start | bytes 30728 | tf_op jit(solution)/shard_map/ppermute | solution.py:288
  34.2 1.6 %collective-permute-done.10 = f32[32,80]{1,0:T(8,128)S(1)} collective-permute-done((f32[32,80]{1,0:T(8,128)S(1)}, f32[32,80]{1,0:T(8,128)S(1)}, u32[]{:S(2)}, u32[]{:S(2)}) %collective-permute-start.10) | collective-permute-done | bytes 10272 | tf_op jit(solution)/shard_map/ppermute | solution.py:288
  35.8 0.9 %collective-permute-done.11 = f32[32,80]{1,0:T(8,128)S(1)} collective-permute-done((f32[32,80]{1,0:T(8,128)S(1)}, f32[32,80]{1,0:T(8,128)S(1)}, u32[]{:S(2)}, u32[]{:S(2)}) %collective-permute-start.11) | collective-permute-done | bytes 10272 | tf_op jit(solution)/shard_map/ppermute | solution.py:288
  36.7 0.6 %add_bitcast_fusion = f32[80,32]{0,1:T(8,128)} fusion(f32[32,80]{1,0:T(8,128)S(1)} %collective-permute-done.11, f32[32,80]{1,0:T(8,128)S(1)} %collective-permute-done.10, f32[32,80]{1,0:T(8,128)S(1)} %get-tuple-element.35, f32[32,80]{1,0:T(8,128)S(1)} %collective-permute-done.9), kind=kLoop, calls=%fused_computation | loop fusion | flops 7680 | bytes 51200 | tf_op jit(solution)/shard_map/transpose | solution.py:289
  (8 shorter events, 0.0 us)
Async XLA Ops:
  0.0 10.1 %collective-permute-start = (bf16[64,1024]{1,0:T(8,128)(2,1)}, bf16[64,1024]{1,0:T(8,128)(2,1)S(1)}, u32[]{:S(2)}, u32[]{:S(2)}) collective-permute-start(bf16[64,1024]{1,0:T(8,128)(2,1)} %bitcast.13), channel_id=1, source_target_pairs={{0,12},{4,8},{8,4},{12,0},{16,20},{20,16},{24,28},{28,24},{1,13},{... | collective-permute-start | bytes 393224 | tf_op jit(solution)/shard_map/ppermute | solution.py:192
  5.0 7.6 %collective-permute-start.2 = (bf16[64,1024]{1,0:T(8,128)(2,1)}, bf16[64,1024]{1,0:T(8,128)(2,1)S(1)}, u32[]{:S(2)}, u32[]{:S(2)}) collective-permute-start(bf16[64,1024]{1,0:T(8,128)(2,1)} %bitcast.16), channel_id=1, source_target_pairs={{0,4},{4,0},{8,12},{12,8},{16,28},{20,24},{24,20},{28,16},{1,5},{5... | collective-permute-start | bytes 393224 | tf_op jit(solution)/shard_map/ppermute | solution.py:192
  5.1 15.1 %collective-permute-start.4 = (bf16[64,1024]{1,0:T(8,128)(2,1)}, bf16[64,1024]{1,0:T(8,128)(2,1)S(1)}, u32[]{:S(2)}, u32[]{:S(2)}) collective-permute-start(bf16[64,1024]{1,0:T(8,128)(2,1)} %bitcast.14), channel_id=1, source_target_pairs={{0,8},{4,12},{8,0},{12,4},{1,9},{5,13},{9,1},{13,5},{2,10},{6,14},... | collective-permute-start | bytes 393224 | tf_op jit(solution)/shard_map/ppermute | solution.py:188
  5.6 16.3 %collective-permute-start.5 = (bf16[64,1024]{1,0:T(8,128)(2,1)}, bf16[64,1024]{1,0:T(8,128)(2,1)S(1)}, u32[]{:S(2)}, u32[]{:S(2)}) collective-permute-start(bf16[64,1024]{1,0:T(8,128)(2,1)} %bitcast.17), channel_id=1, source_target_pairs={{0,8},{4,12},{8,0},{12,4},{1,9},{5,13},{9,1},{13,5},{2,10},{6,14},... | collective-permute-start | bytes 393224 | tf_op jit(solution)/shard_map/ppermute | solution.py:188
  10.1 16.8 %copy-start = (bf16[320,1,4096]{2,0,1:T(8,128)(2,1)S(1)}, bf16[320,1,4096]{2,0,1:T(8,128)(2,1)}, u32[]{:S(2)}) copy-start(bf16[320,1,4096]{2,0,1:T(8,128)(2,1)} %param.15) | copy-start | bytes 7864324
  10.1 11.8 %collective-permute-start.1 = (bf16[64,1024]{1,0:T(8,128)(2,1)S(1)}, bf16[64,1024]{1,0:T(8,128)(2,1)S(1)}, u32[]{:S(2)}, u32[]{:S(2)}) collective-permute-start(bf16[64,1024]{1,0:T(8,128)(2,1)S(1)} %collective-permute-done.refs_0_), channel_id=1, source_target_pairs={{0,16},{16,0},{1,17},{17,1},{2,18},{18,2},{3,19},{19,3},{4,20},{20... | collective-permute-start | bytes 393224 | tf_op jit(solution)/shard_map/ppermute | solution.py:195
  12.7 9.3 %collective-permute-start.3 = (bf16[64,1024]{1,0:T(8,128)(2,1)S(1)}, bf16[64,1024]{1,0:T(8,128)(2,1)S(1)}, u32[]{:S(2)}, u32[]{:S(2)}) collective-permute-start(bf16[64,1024]{1,0:T(8,128)(2,1)S(1)} %collective-permute-done.2.refs_1_), channel_id=1, source_target_pairs={{0,16},{16,0},{1,17},{17,1},{2,18},{18,2},{3,19},{19,3},{4,20},{20... | collective-permute-start | bytes 393224 | tf_op jit(solution)/shard_map/ppermute | solution.py:195
  22.5 6.4 %collective-permute-start.6 = (bf16[128,128]{1,0:T(8,128)(2,1)S(1)}, bf16[128,128]{1,0:T(8,128)(2,1)S(1)}, u32[]{:S(2)}, u32[]{:S(2)}) collective-permute-start(bf16[128,128]{1,0:T(8,128)(2,1)S(1)} %sides.3.refs_0_), channel_id=1, source_target_pairs={{0,12},{4,8},{8,4},{12,0},{1,13},{5,9},{9,5},{13,1},{2,14},{6,10},... | collective-permute-start | bytes 98312 | tf_op jit(solution)/shard_map/ppermute | solution.py:188
  25.0 4.8 %collective-permute-start.7 = (bf16[128,128]{1,0:T(8,128)(2,1)S(1)}, bf16[128,128]{1,0:T(8,128)(2,1)S(1)}, u32[]{:S(2)}, u32[]{:S(2)}) collective-permute-start(bf16[128,128]{1,0:T(8,128)(2,1)S(1)} %sides.3.refs_0_), channel_id=1, source_target_pairs={{0,8},{4,12},{8,0},{12,4},{1,9},{5,13},{9,1},{13,5},{2,10},{6,14},... | collective-permute-start | bytes 98312 | tf_op jit(solution)/shard_map/ppermute | solution.py:188
  25.5 4.3 %collective-permute-start.8 = (bf16[128,128]{1,0:T(8,128)(2,1)S(1)}, bf16[128,128]{1,0:T(8,128)(2,1)S(1)}, u32[]{:S(2)}, u32[]{:S(2)}) collective-permute-start(bf16[128,128]{1,0:T(8,128)(2,1)S(1)} %sides.3.refs_0_), channel_id=1, source_target_pairs={{0,4},{4,0},{8,12},{12,8},{1,5},{5,1},{9,13},{13,9},{2,6},{6,2},{1... | collective-permute-start | bytes 98312 | tf_op jit(solution)/shard_map/ppermute | solution.py:188
  32.0 3.8 %collective-permute-start.10 = (f32[32,80]{1,0:T(8,128)S(1)}, f32[32,80]{1,0:T(8,128)S(1)}, u32[]{:S(2)}, u32[]{:S(2)}) collective-permute-start(f32[32,80]{1,0:T(8,128)S(1)} %get-tuple-element.37), channel_id=1, source_target_pairs={{0,2},{1,3},{2,0},{3,1},{4,6},{5,7},{6,4},{7,5},{8,10},{9,11},{10,... | collective-permute-start | bytes 30728 | tf_op jit(solution)/shard_map/ppermute | solution.py:288
  33.5 3.2 %collective-permute-start.11 = (f32[32,80]{1,0:T(8,128)S(1)}, f32[32,80]{1,0:T(8,128)S(1)}, u32[]{:S(2)}, u32[]{:S(2)}) collective-permute-start(f32[32,80]{1,0:T(8,128)S(1)} %get-tuple-element.38), channel_id=1, source_target_pairs={{0,3},{1,2},{2,1},{3,0},{4,7},{5,6},{6,5},{7,4},{8,11},{9,10},{10,... | collective-permute-start | bytes 30728 | tf_op jit(solution)/shard_map/ppermute | solution.py:288
  33.6 3.2 %collective-permute-start.9 = (f32[32,80]{1,0:T(8,128)S(1)}, f32[32,80]{1,0:T(8,128)S(1)}, u32[]{:S(2)}, u32[]{:S(2)}) collective-permute-start(f32[32,80]{1,0:T(8,128)S(1)} %get-tuple-element.36), channel_id=1, source_target_pairs={{0,1},{1,0},{2,3},{3,2},{4,5},{5,4},{6,7},{7,6},{8,9},{9,8},{10,11... | collective-permute-start | bytes 30728 | tf_op jit(solution)/shard_map/ppermute | solution.py:288

commit v4 on v3

--- a/solution.py
+++ b/solution.py
@@ -94,11 +94,9 @@
         turns[at * lanes : (at + 1) * lanes, :] = part
 
 
-def scores_kernel(sources, shifts, tokens, turn, back, turns, inverse, train, *refs):
-    blocks, (scratch, rows, tall) = refs[:sources], refs[-3:]
-    layers = lax.axis_size("layer")
-    given = refs[sources : -3 - layers]
-    outs = refs[-3 - layers : -3]
+def scores_kernel(sources, far, tokens, which, turn, back, turns, inverse, train, *refs):
+    blocks, given = refs[:sources], refs[sources : sources + (len(which) if far else 0)]
+    outs, (rows, scratch) = refs[len(blocks) + len(given) : -2], refs[-2:]
     rank = turn.shape[0] // 2
     across = lanes // rank
     here = blocks[0].shape[0] // tokens
@@ -137,7 +135,7 @@
     scaled = jnp.concatenate(scaled, axis=0)
     conditioned = product3(scaled, turns[:lanes, :], turns[lanes:, :])
     for part in range(lanes // 128):
-        scratch[part] = conditioned[:, part * 128 : (part + 1) * 128]
+        scratch[part, : conditioned.shape[0], :] = conditioned[:, part * 128 : (part + 1) * 128]
     for pair in range(rank // 2):
         for part in range(lanes // 128):
             even = scratch[part, pl.ds(2 * pair, groups, stride=rank), :]
@@ -149,21 +147,29 @@
                 rows[j * groups : (j + 1) * groups, columns] = jnp.concatenate(
                     [even[:, cut], odd[:, cut]], axis=1
                 )
+    write_slabs(far, which, here, rows, train, given, outs)
+
+
+def slabs_kernel(far, which, here, rows, train, *refs):
+    write_slabs(far, which, here, rows, train, refs[: len(which)], refs[len(which) :])
+
+
+def write_slabs(far, which, here, rows, train, given, outs):
+    layer, place = lax.axis_index("layer"), lax.axis_index("corpus")
+    slab_rows = train.shape[0] // lax.axis_size("layer")
     conditioned = rows[...].astype(bf16)
-    middle = train.shape[0] // 32 * 16
-    tall[:middle] = dot(train[:middle], conditioned, nt)
-    tall[middle:] = dot(train[middle:], conditioned, nt)
-    layer, place = lax.axis_index("layer"), lax.axis_index("corpus")
-    slab_rows = train.shape[0] // layers
-    for shift, out in enumerate(outs):
-        slab = tall[pl.ds(pl.multiple_of((layer ^ shift) * slab_rows, 8), slab_rows), :].T
-        if shifts is None:
-            out[...] = slab
+    for at, shift in enumerate(which):
+        if outs[at].shape[1] > slab_rows:
+            outs[at][:, slab_rows:] = jnp.zeros((outs[at].shape[0], outs[at].shape[1] - slab_rows), f32)
+        first = pl.multiple_of((layer ^ shift) * slab_rows, 16)
+        slab = dot(train[pl.ds(first, slab_rows), :], conditioned, nt).T
+        if not far:
+            outs[at][...] = slab
             continue
-        out[pl.ds(pl.multiple_of(place * here, 8), here), :] = given[shift][...]
-        for at, far in enumerate(shifts):
-            to = pl.ds(pl.multiple_of((place ^ far) * here, 8), here)
-            out[to, :] = slab[at * here : (at + 1) * here]
+        outs[at][pl.ds(pl.multiple_of(place * here, 8), here), :slab_rows] = given[at][...]
+        for block, distance in enumerate(far):
+            to = pl.ds(pl.multiple_of((place ^ distance) * here, 8), here)
+            outs[at][to, :slab_rows] = slab[block * here : (block + 1) * here]
 
 
 def body(
@@ -235,27 +241,32 @@
     train = train_grads.reshape(train_grads.shape[0], rank * rank)
     rows_out = train.shape[0] // layers
 
-    def scores_call(shifts, blocks, given, chunk):
-        queries = sum(x.shape[0] for x in blocks) // tokens + (queries_here if given else 0)
-        here = blocks[0].shape[0] // tokens // (chunk or 1)
+    def slab_shapes(queries, count, wide=0):
+        return [jax.ShapeDtypeStruct((queries, rows_out + wide), f32)] * count
+
+    def scores_call(far, which, blocks, given, chunks):
+        here = blocks[0].shape[0] // tokens // chunks
         count = here * len(blocks)
-        out_rows = queries // (chunk or 1)
-        if chunk:
+        queries = count * chunks + (queries_here if far else 0)
+        scratch = pltpu.VMEM((lanes // 128, count * rank * rank // lanes + rank, 128), f32)
+        shapes, rows = slab_shapes(queries, len(which), -rows_out % 128 if far else 0), (count, rank * rank)
+        specs = dict(in_specs=[vmem] * (5 + len(blocks) + len(given)), out_specs=[vmem] * len(which))
+        if chunks > 1:
             specs = dict(
-                grid=(chunk,),
+                grid=(chunks,),
                 in_specs=[vmem] * 5 + [pl.BlockSpec((here * tokens, 2 * rank), lambda i: (i, 0))],
-                out_specs=[pl.BlockSpec((out_rows, rows_out), lambda i: (i, 0))] * layers,
+                out_specs=[pl.BlockSpec((here, rows_out), lambda i: (i, 0))] * len(which),
             )
+        if far:
+            shapes.append(jax.ShapeDtypeStruct(rows, f32))
+            specs["out_specs"].append(vmem)
+            scratches = [scratch]
         else:
-            specs = dict(in_specs=[vmem] * (5 + len(blocks) + len(given)), out_specs=[vmem] * layers)
+            scratches = [pltpu.VMEM(rows, f32), scratch]
         return pl.pallas_call(
-            functools.partial(scores_kernel, len(blocks), shifts, tokens),
-            out_shape=[jax.ShapeDtypeStruct((queries, rows_out), f32)] * layers,
-            scratch_shapes=[
-                pltpu.VMEM((lanes // 128, count * rank * rank // lanes, 128), f32),
-                pltpu.VMEM((count, rank * rank), f32),
-                pltpu.VMEM((train.shape[0], count), f32),
-            ],
+            functools.partial(scores_kernel, len(blocks), far, tokens, which),
+            out_shape=shapes,
+            scratch_shapes=scratches,
             compiler_params=params,
             name="scores",
             **specs,
@@ -275,17 +286,26 @@
         total = sides_call([(1, first), (0, second)], [near, near_out], [total], f32)
         sides = sides_call([(1, second), (0, first), (1, direct), (0, direct)], [swapped(near), swapped(near_out), last, last_out], [total], bf16)
         arrived = [far(sides, shift) for shift in (3, 2, 1)]
-        own = scores_call(None, [sides], [], None)
-        slabs = scores_call((3, 2, 1), arrived, own, None)
+        own = scores_call((), tuple(range(layers)), [sides], [], 1)
+        soon, later = tuple(range(layers // 2, layers)), tuple(range(layers // 2))
+        *slabs, rows = scores_call((3, 2, 1), soon, arrived, [own[i] for i in soon], 1)
+        slabs = pl.pallas_call(
+            functools.partial(slabs_kernel, (3, 2, 1), later, queries_here),
+            out_shape=slab_shapes(slabs[0].shape[0], len(later)),
+            in_specs=[vmem] * (2 + len(later)),
+            out_specs=[vmem] * len(later),
+            compiler_params=params,
+            name="slabs",
+        )(rows, train, *(own[i] for i in later)) + tuple(slabs)
     else:
         pieces = [lax.all_gather(x, "corpus", axis=1, tiled=True) for x in (in_own, out_own)]
         sides = sides_call([(1, lambda g, p: 0), (0, lambda g, p: 0)], pieces, [], bf16)
         everything = lax.all_gather(sides, "corpus", axis=0, tiled=True)
-        slabs = scores_call(None, [everything], [], everything.shape[0] // tokens // 32)
+        slabs = scores_call((), tuple(range(layers)), [everything], [], everything.shape[0] // tokens // 32)
 
     total = slabs[0]
     for shift in range(1, layers):
-        total += lax.ppermute(slabs[shift], "layer", [(i, i ^ shift) for i in range(layers)])
+        total += lax.ppermute(slabs[shift], "layer", [(i, i ^ shift) for i in range(layers)])[:, :rows_out]
     return total.T
 
 

time: 37.5 us -> 37.1 us (0.989)
  waiting for transfers between devices: 11.1 us -> 10.6 us
    ppermute x3, waiting for transfers between devices: 2.53 us -> 1.96 us  [body(): lax.ppermute(slabs[shift], 'layer', [(i, i ^ shift) for i in range(layers)])]
    pallas_call x2 -> x3, Pallas kernels: 4.08 us -> 4.19 us  [the longest x2 3.66 us: scores_call(): pl.pallas_call(functools.partial(scores_kernel, len(blocks), far, tokens,...]
  transfers between devices with their start and end apart: 12 -> 12, of which waited for: 6 -> 7; matrix products, arithmetic and copies ran while one was open for 0% -> 0% of each run, Pallas kernels for 12% -> 13%
where the time goes in v4:
time: 37.1 us; the launch traced here: 36.9 us
  starting transfers between devices  18.5 us (50%)
  waiting for transfers between devices  10.6 us (29%)
  Pallas kernels  7.18 us (19%)
  other arithmetic  0.61 us (2%)
    ppermute x5, waiting for transfers between devices, far(): return lax.ppermute(x, 'corpus', [(i, i ^ shift) for i in range(places)])  8.16 us
    ppermute x5, starting transfers between devices, far(): return lax.ppermute(x, 'corpus', [(i, i ^ shift) for i in range(places)])  7.38 us
    ppermute x2, starting transfers between devices, mixed(): return lax.ppermute(x, ('groups', 'corpus'), pairs)  5.05 us
    ppermute x2, starting transfers between devices, swapped(): return lax.ppermute(x, 'groups', [(0, 1), (1, 0)])  3.87 us
    pallas_call x2, Pallas kernels, scores_call(): pl.pallas_call(functools.partial(scores_kernel, len(blocks), far, tokens,...  3.66 us
    ppermute x3, starting transfers between devices, body(): lax.ppermute(slabs[shift], 'layer', [(i, i ^ shift) for i in range(layers)])  2.19 us
    pallas_call x1, Pallas kernels, body(): pl.pallas_call(prepare_kernel, out_shape=[jax.ShapeDtypeStruct((queries_h...  2.14 us
    ppermute x3, waiting for transfers between devices, body(): lax.ppermute(slabs[shift], 'layer', [(i, i ^ shift) for i in range(layers)])  1.96 us
  transfers between devices with their start and end apart: 12, of which 7 were waited for; matrix products, arithmetic and copies ran while one was open for 0% of the time, Pallas kernels for 13%

profile of v4, /device:TPU:0, one launch (start us, length us, event | category | flops | bytes accessed | tf_op | source)
XLA Modules:
  0.0 36.9 jit_solution(14263120210179727034)
XLA Ops:
  0.0 5.0 %collective-permute-start = (bf16[64,1024]{1,0:T(8,128)(2,1)}, bf16[64,1024]{1,0:T(8,128)(2,1)S(1)}, u32[]{:S(2)}, u32[]{:S(2)}) collective-permute-start(bf16[64,1024]{1,0:T(8,128)(2,1)} %bitcast.14), channel_id=1, source_target_pairs={{0,12},{4,8},{8,4},{12,0},{16,20},{20,16},{24,28},{28,24},{1,13},{... | collective-permute-start | bytes 393224 | tf_op jit(solution)/shard_map/ppermute | solution.py:198
  5.1 0.6 %collective-permute-start.4 = (bf16[64,1024]{1,0:T(8,128)(2,1)}, bf16[64,1024]{1,0:T(8,128)(2,1)S(1)}, u32[]{:S(2)}, u32[]{:S(2)}) collective-permute-start(bf16[64,1024]{1,0:T(8,128)(2,1)} %bitcast.15), channel_id=1, source_target_pairs={{0,8},{4,12},{8,0},{12,4},{1,9},{5,13},{9,1},{13,5},{2,10},{6,14},... | collective-permute-start | bytes 393224 | tf_op jit(solution)/shard_map/ppermute | solution.py:194
  5.6 2.4 %collective-permute-start.5 = (bf16[64,1024]{1,0:T(8,128)(2,1)}, bf16[64,1024]{1,0:T(8,128)(2,1)S(1)}, u32[]{:S(2)}, u32[]{:S(2)}) collective-permute-start(bf16[64,1024]{1,0:T(8,128)(2,1)} %bitcast.18), channel_id=1, source_target_pairs={{0,8},{4,12},{8,0},{12,4},{1,9},{5,13},{9,1},{13,5},{2,10},{6,14},... | collective-permute-start | bytes 393224 | tf_op jit(solution)/shard_map/ppermute | solution.py:194
  8.0 2.1 %prepare.1 = (f32[128,128]{1,0:T(8,128)S(1)}, bf16[128,4096]{1,0:T(8,128)(2,1)S(1)}, bf16[128,4096]{1,0:T(8,128)(2,1)S(1)}, bf16[128,512]{1,0:T(8,128)(2,1)S(1)}...) custom-call(bf16[64,1024]{1,0:T(8,128)(2,1)} %bitcast.16, ...), custom_call_target="tpu_custom_call" | custom-call | tf_op jit(solution)/shard_map/prepare/pallas_call | solution.py:215
  10.2 2.0 %collective-permute-start.1 = (bf16[64,1024]{1,0:T(8,128)(2,1)S(1)}, bf16[64,1024]{1,0:T(8,128)(2,1)S(1)}, u32[]{:S(2)}, u32[]{:S(2)}) collective-permute-start(bf16[64,1024]{1,0:T(8,128)(2,1)S(1)} %collective-permute-done.refs_0_), channel_id=1, source_target_pairs={{0,16},{16,0},{1,17},{17,1},{2,18},{18,2},{3,19},{19,3},{4,20},{20... | collective-permute-start | bytes 393224 | tf_op jit(solution)/shard_map/ppermute | solution.py:201
  12.2 0.5 %collective-permute-done.2.refs_1_ = bf16[64,1024]{1,0:T(8,128)(2,1)S(1)} collective-permute-done((bf16[64,1024]{1,0:T(8,128)(2,1)}, bf16[64,1024]{1,0:T(8,128)(2,1)S(1)}, u32[]{:S(2)}, u32[]{:S(2)}) %collective-permute-start.2) | collective-permute-done | bytes 131104 | tf_op jit(solution)/shard_map/ppermute | solution.py:198
  12.7 1.8 %collective-permute-start.3 = (bf16[64,1024]{1,0:T(8,128)(2,1)S(1)}, bf16[64,1024]{1,0:T(8,128)(2,1)S(1)}, u32[]{:S(2)}, u32[]{:S(2)}) collective-permute-start(bf16[64,1024]{1,0:T(8,128)(2,1)S(1)} %collective-permute-done.2.refs_1_), channel_id=1, source_target_pairs={{0,16},{16,0},{1,17},{17,1},{2,18},{18,2},{3,19},{19,3},{4,20},{20... | collective-permute-start | bytes 393224 | tf_op jit(solution)/shard_map/ppermute | solution.py:201
  14.5 0.4 sides.2.refs_4_
  14.9 5.2 %collective-permute-done.4.refs_2_ = bf16[64,1024]{1,0:T(8,128)(2,1)S(1)} collective-permute-done((bf16[64,1024]{1,0:T(8,128)(2,1)}, bf16[64,1024]{1,0:T(8,128)(2,1)S(1)}, u32[]{:S(2)}, u32[]{:S(2)}) %collective-permute-start.4) | collective-permute-done | bytes 131104 | tf_op jit(solution)/shard_map/ppermute | solution.py:194
  20.1 1.8 %collective-permute-done.5.refs_3_ = bf16[64,1024]{1,0:T(8,128)(2,1)S(1)} collective-permute-done((bf16[64,1024]{1,0:T(8,128)(2,1)}, bf16[64,1024]{1,0:T(8,128)(2,1)S(1)}, u32[]{:S(2)}, u32[]{:S(2)}) %collective-permute-start.5) | collective-permute-done | bytes 131104 | tf_op jit(solution)/shard_map/ppermute | solution.py:194
  22.0 0.5 %sides.3.refs_0_ = bf16[128,128]{1,0:T(8,128)(2,1)S(1)} custom-call(bf16[128,4096]{1,0:T(8,128)(2,1)S(1)} %get-tuple-element.27.acts, bf16[128,4096]{1,0:T(8,128)(2,1)S(1)} %get-tuple-element.28.outgrads, bf16[64,1024]{1,0:T(8,128)(2,1)S(1)} %collective-permute-done.1.refs_0_, bf16[64,1024]{1,0:T(8,128)(2,1)S(1)} %collective-permute-done.3.refs_1_, ...), custom_call_target="tpu_custom_call" | custom-call | tf_op jit(solution)/shard_map/sides/pallas_call | solution.py:204
  22.5 2.5 %collective-permute-start.6 = (bf16[128,128]{1,0:T(8,128)(2,1)S(1)}, bf16[128,128]{1,0:T(8,128)(2,1)S(1)}, u32[]{:S(2)}, u32[]{:S(2)}) collective-permute-start(bf16[128,128]{1,0:T(8,128)(2,1)S(1)} %sides.3.refs_0_), channel_id=1, source_target_pairs={{0,12},{4,8},{8,4},{12,0},{1,13},{5,9},{9,5},{13,1},{2,14},{6,10},... | collective-permute-start | bytes 98312 | tf_op jit(solution)/shard_map/ppermute | solution.py:194
  25.0 0.5 %collective-permute-start.7 = (bf16[128,128]{1,0:T(8,128)(2,1)S(1)}, bf16[128,128]{1,0:T(8,128)(2,1)S(1)}, u32[]{:S(2)}, u32[]{:S(2)}) collective-permute-start(bf16[128,128]{1,0:T(8,128)(2,1)S(1)} %sides.3.refs_0_), channel_id=1, source_target_pairs={{0,8},{4,12},{8,0},{12,4},{1,9},{5,13},{9,1},{13,5},{2,10},{6,14},... | collective-permute-start | bytes 98312 | tf_op jit(solution)/shard_map/ppermute | solution.py:194
  25.5 1.4 %collective-permute-start.8 = (bf16[128,128]{1,0:T(8,128)(2,1)S(1)}, bf16[128,128]{1,0:T(8,128)(2,1)S(1)}, u32[]{:S(2)}, u32[]{:S(2)}) collective-permute-start(bf16[128,128]{1,0:T(8,128)(2,1)S(1)} %sides.3.refs_0_), channel_id=1, source_target_pairs={{0,4},{4,0},{8,12},{12,8},{1,5},{5,1},{9,13},{13,9},{2,6},{6,2},{1... | collective-permute-start | bytes 98312 | tf_op jit(solution)/shard_map/ppermute | solution.py:194
  26.9 1.8 %scores.2 = (f32[8,80]{1,0:T(8,128)S(1)}, f32[8,80]{1,0:T(8,128)S(1)}, f32[8,80]{1,0:T(8,128)S(1)}, f32[8,80]{1,0:T(8,128)S(1)}) custom-call(bf16[128,512]{1,0:T(8,128)(2,1)S(1)} %get-tuple-element.23.turn, bf16[64,192]{1,0:T(8,128)(2,1)S(1)} %get-tuple-element.24.back, bf16[512,256]{1,0:T(8,128)(2,1)S(1)} %get-tuple-element.25.turns, ...), custom_call_target="tpu_custom_call" | custom-call | tf_op jit(solution)/shard_map/scores/pallas_call | solution.py:266
  28.8 1.1 %collective-permute-done.7.refs_1_ = bf16[128,128]{1,0:T(8,128)(2,1)S(1)} collective-permute-done((bf16[128,128]{1,0:T(8,128)(2,1)S(1)}, bf16[128,128]{1,0:T(8,128)(2,1)S(1)}, u32[]{:S(2)}, u32[]{:S(2)}) %collective-permute-start.7) | collective-permute-done | bytes 32800 | tf_op jit(solution)/shard_map/ppermute | solution.py:194
  29.8 1.8 %scores.3 = (f32[32,128]{1,0:T(8,128)S(1)}, f32[32,128]{1,0:T(8,128)S(1)}, f32[24,4096]{1,0:T(8,128)S(1)}) custom-call(bf16[128,512]{1,0:T(8,128)(2,1)S(1)} %get-tuple-element.23.turn, bf16[64,192]{1,0:T(8,128)(2,1)S(1)} %get-tuple-element.24.back, bf16[512,256]{1,0:T(8,128)(2,1)S(1)} %get-tuple-element.25.turns, f32[64,256]{1,0:T(8,128)S(1)} %get-tuple-element.26.inverse, ...), custom_call_target="tpu_custom_call" | custom-call | tf_op jit(solution)/shard_map/scores/pallas_call | solution.py:266
  31.6 1.5 %collective-permute-start.10 = (f32[32,128]{1,0:T(8,128)S(1)}, f32[32,128]{1,0:T(8,128)S(1)}, u32[]{:S(2)}, u32[]{:S(2)}) collective-permute-start(f32[32,128]{1,0:T(8,128)S(1)} %get-tuple-element.39), channel_id=1, source_target_pairs={{0,2},{1,3},{2,0},{3,1},{4,6},{5,7},{6,4},{7,5},{8,10},{9,11},{10,... | collective-permute-start | bytes 49160 | tf_op jit(solution)/shard_map/ppermute | solution.py:308
  33.2 0.5 %slabs.1 = (f32[32,80]{1,0:T(8,128)S(1)}, f32[32,80]{1,0:T(8,128)S(1)}) custom-call(f32[24,4096]{1,0:T(8,128)S(1)} %get-tuple-element.34.rows, bf16[320,4096]{1,0:T(8,128)(2,1)S(1)} %bitcast.11, f32[8,80]{1,0:T(8,128)S(1)} %get-tuple-element.35.refs_0_, f32[8,80]{1,0:T(8,128)S(1)} %get-tuple-element.36.refs_1_), custom_call_target="tpu_custom_call" | custom-call | tf_op jit(solution)/shard_map/slabs/pallas_call | solution.py:292
  33.7 0.7 %collective-permute-start.9 = (f32[32,80]{1,0:T(8,128)S(1)}, f32[32,80]{1,0:T(8,128)S(1)}, u32[]{:S(2)}, u32[]{:S(2)}) collective-permute-start(f32[32,80]{1,0:T(8,128)S(1)} %get-tuple-element.38), channel_id=1, source_target_pairs={{0,1},{1,0},{2,3},{3,2},{4,5},{5,4},{6,7},{7,6},{8,9},{9,8},{10,11... | collective-permute-start | bytes 30728 | tf_op jit(solution)/shard_map/ppermute | solution.py:308
  34.4 0.8 %collective-permute-done.9 = f32[32,80]{1,0:T(8,128)S(1)} collective-permute-done((f32[32,80]{1,0:T(8,128)S(1)}, f32[32,80]{1,0:T(8,128)S(1)}, u32[]{:S(2)}, u32[]{:S(2)}) %collective-permute-start.9) | collective-permute-done | bytes 10272 | tf_op jit(solution)/shard_map/ppermute | solution.py:308
  35.2 0.2 collective-permute-done.10
  35.4 0.9 %collective-permute-done.11 = f32[32,128]{1,0:T(8,128)S(1)} collective-permute-done((f32[32,128]{1,0:T(8,128)S(1)}, f32[32,128]{1,0:T(8,128)S(1)}, u32[]{:S(2)}, u32[]{:S(2)}) %collective-permute-start.11) | collective-permute-done | bytes 16416 | tf_op jit(solution)/shard_map/ppermute | solution.py:308
  36.3 0.6 %fusion = f32[80,32]{0,1:T(8,128)} fusion(f32[32,128]{1,0:T(8,128)S(1)} %collective-permute-done.11, f32[32,128]{1,0:T(8,128)S(1)} %collective-permute-done.10, f32[32,80]{1,0:T(8,128)S(1)} %get-tuple-element.37, f32[32,80]{1,0:T(8,128)S(1)} %collective-permute-done.9), kind=kLoop, calls=%fused_computation.1 | loop fusion | flops 7680 | bytes 51200 | tf_op jit(solution)/shard_map/transpose | solution.py:309
  (9 shorter events, 0.0 us)
Async XLA Ops:
  0.0 10.1 %collective-permute-start = (bf16[64,1024]{1,0:T(8,128)(2,1)}, bf16[64,1024]{1,0:T(8,128)(2,1)S(1)}, u32[]{:S(2)}, u32[]{:S(2)}) collective-permute-start(bf16[64,1024]{1,0:T(8,128)(2,1)} %bitcast.14), channel_id=1, source_target_pairs={{0,12},{4,8},{8,4},{12,0},{16,20},{20,16},{24,28},{28,24},{1,13},{... | collective-permute-start | bytes 393224 | tf_op jit(solution)/shard_map/ppermute | solution.py:198
  5.0 7.6 %collective-permute-start.2 = (bf16[64,1024]{1,0:T(8,128)(2,1)}, bf16[64,1024]{1,0:T(8,128)(2,1)S(1)}, u32[]{:S(2)}, u32[]{:S(2)}) collective-permute-start(bf16[64,1024]{1,0:T(8,128)(2,1)} %bitcast.17), channel_id=1, source_target_pairs={{0,4},{4,0},{8,12},{12,8},{16,28},{20,24},{24,20},{28,16},{1,5},{5... | collective-permute-start | bytes 393224 | tf_op jit(solution)/shard_map/ppermute | solution.py:198
  5.1 15.1 %collective-permute-start.4 = (bf16[64,1024]{1,0:T(8,128)(2,1)}, bf16[64,1024]{1,0:T(8,128)(2,1)S(1)}, u32[]{:S(2)}, u32[]{:S(2)}) collective-permute-start(bf16[64,1024]{1,0:T(8,128)(2,1)} %bitcast.15), channel_id=1, source_target_pairs={{0,8},{4,12},{8,0},{12,4},{1,9},{5,13},{9,1},{13,5},{2,10},{6,14},... | collective-permute-start | bytes 393224 | tf_op jit(solution)/shard_map/ppermute | solution.py:194
  5.6 16.3 %collective-permute-start.5 = (bf16[64,1024]{1,0:T(8,128)(2,1)}, bf16[64,1024]{1,0:T(8,128)(2,1)S(1)}, u32[]{:S(2)}, u32[]{:S(2)}) collective-permute-start(bf16[64,1024]{1,0:T(8,128)(2,1)} %bitcast.18), channel_id=1, source_target_pairs={{0,8},{4,12},{8,0},{12,4},{1,9},{5,13},{9,1},{13,5},{2,10},{6,14},... | collective-permute-start | bytes 393224 | tf_op jit(solution)/shard_map/ppermute | solution.py:194
  10.1 16.8 %copy-start = (bf16[320,1,4096]{2,0,1:T(8,128)(2,1)S(1)}, bf16[320,1,4096]{2,0,1:T(8,128)(2,1)}, u32[]{:S(2)}) copy-start(bf16[320,1,4096]{2,0,1:T(8,128)(2,1)} %param.15) | copy-start | bytes 7864324
  10.2 11.8 %collective-permute-start.1 = (bf16[64,1024]{1,0:T(8,128)(2,1)S(1)}, bf16[64,1024]{1,0:T(8,128)(2,1)S(1)}, u32[]{:S(2)}, u32[]{:S(2)}) collective-permute-start(bf16[64,1024]{1,0:T(8,128)(2,1)S(1)} %collective-permute-done.refs_0_), channel_id=1, source_target_pairs={{0,16},{16,0},{1,17},{17,1},{2,18},{18,2},{3,19},{19,3},{4,20},{20... | collective-permute-start | bytes 393224 | tf_op jit(solution)/shard_map/ppermute | solution.py:201
  12.7 9.3 %collective-permute-start.3 = (bf16[64,1024]{1,0:T(8,128)(2,1)S(1)}, bf16[64,1024]{1,0:T(8,128)(2,1)S(1)}, u32[]{:S(2)}, u32[]{:S(2)}) collective-permute-start(bf16[64,1024]{1,0:T(8,128)(2,1)S(1)} %collective-permute-done.2.refs_1_), channel_id=1, source_target_pairs={{0,16},{16,0},{1,17},{17,1},{2,18},{18,2},{3,19},{19,3},{4,20},{20... | collective-permute-start | bytes 393224 | tf_op jit(solution)/shard_map/ppermute | solution.py:201
  22.5 6.3 %collective-permute-start.6 = (bf16[128,128]{1,0:T(8,128)(2,1)S(1)}, bf16[128,128]{1,0:T(8,128)(2,1)S(1)}, u32[]{:S(2)}, u32[]{:S(2)}) collective-permute-start(bf16[128,128]{1,0:T(8,128)(2,1)S(1)} %sides.3.refs_0_), channel_id=1, source_target_pairs={{0,12},{4,8},{8,4},{12,0},{1,13},{5,9},{9,5},{13,1},{2,14},{6,10},... | collective-permute-start | bytes 98312 | tf_op jit(solution)/shard_map/ppermute | solution.py:194
  25.0 4.8 %collective-permute-start.7 = (bf16[128,128]{1,0:T(8,128)(2,1)S(1)}, bf16[128,128]{1,0:T(8,128)(2,1)S(1)}, u32[]{:S(2)}, u32[]{:S(2)}) collective-permute-start(bf16[128,128]{1,0:T(8,128)(2,1)S(1)} %sides.3.refs_0_), channel_id=1, source_target_pairs={{0,8},{4,12},{8,0},{12,4},{1,9},{5,13},{9,1},{13,5},{2,10},{6,14},... | collective-permute-start | bytes 98312 | tf_op jit(solution)/shard_map/ppermute | solution.py:194
  25.5 4.3 %collective-permute-start.8 = (bf16[128,128]{1,0:T(8,128)(2,1)S(1)}, bf16[128,128]{1,0:T(8,128)(2,1)S(1)}, u32[]{:S(2)}, u32[]{:S(2)}) collective-permute-start(bf16[128,128]{1,0:T(8,128)(2,1)S(1)} %sides.3.refs_0_), channel_id=1, source_target_pairs={{0,4},{4,0},{8,12},{12,8},{1,5},{5,1},{9,13},{13,9},{2,6},{6,2},{1... | collective-permute-start | bytes 98312 | tf_op jit(solution)/shard_map/ppermute | solution.py:194
  31.6 3.8 %collective-permute-start.10 = (f32[32,128]{1,0:T(8,128)S(1)}, f32[32,128]{1,0:T(8,128)S(1)}, u32[]{:S(2)}, u32[]{:S(2)}) collective-permute-start(f32[32,128]{1,0:T(8,128)S(1)} %get-tuple-element.39), channel_id=1, source_target_pairs={{0,2},{1,3},{2,0},{3,1},{4,6},{5,7},{6,4},{7,5},{8,10},{9,11},{10,... | collective-permute-start | bytes 49160 | tf_op jit(solution)/shard_map/ppermute | solution.py:308
  33.2 3.2 %collective-permute-start.11 = (f32[32,128]{1,0:T(8,128)S(1)}, f32[32,128]{1,0:T(8,128)S(1)}, u32[]{:S(2)}, u32[]{:S(2)}) collective-permute-start(f32[32,128]{1,0:T(8,128)S(1)} %get-tuple-element.40), channel_id=1, source_target_pairs={{0,3},{1,2},{2,1},{3,0},{4,7},{5,6},{6,5},{7,4},{8,11},{9,10},{10,... | collective-permute-start | bytes 49160 | tf_op jit(solution)/shard_map/ppermute | solution.py:308
  33.7 1.5 %collective-permute-start.9 = (f32[32,80]{1,0:T(8,128)S(1)}, f32[32,80]{1,0:T(8,128)S(1)}, u32[]{:S(2)}, u32[]{:S(2)}) collective-permute-start(f32[32,80]{1,0:T(8,128)S(1)} %get-tuple-element.38), channel_id=1, source_target_pairs={{0,1},{1,0},{2,3},{3,2},{4,5},{5,4},{6,7},{7,6},{8,9},{9,8},{10,11... | collective-permute-start | bytes 30728 | tf_op jit(solution)/shard_map/ppermute | solution.py:308

commit v5 on v4

--- a/solution.py
+++ b/solution.py
@@ -283,8 +283,10 @@
         second = lambda g, p: (p ^ jnp.where(g == 0, 1, 3)) * width
         mine = lambda g, p: (p ^ 2) * width + g * part
         other = lambda g, p: (p ^ 2) * width + (1 - g) * part
-        total = sides_call([(1, first), (0, second)], [near, near_out], [total], f32)
-        sides = sides_call([(1, second), (0, first), (1, direct), (0, direct)], [swapped(near), swapped(near_out), last, last_out], [total], bf16)
+        total = sides_call([(1, first), (0, second), (1, direct)], [near, near_out, last], [total], f32)
+        sides = sides_call(
+            [(1, second), (0, first), (0, direct)], [swapped(near), swapped(near_out), last_out], [total], bf16
+        )
         arrived = [far(sides, shift) for shift in (3, 2, 1)]
         own = scores_call((), tuple(range(layers)), [sides], [], 1)
         soon, later = tuple(range(layers // 2, layers)), tuple(range(layers // 2))

time: 37.1 us -> 36.9 us (level)
  no operation moved by 1% of the time
where the time goes in v5:
time: 36.9 us; the launch traced here: 36.8 us
  starting transfers between devices  18.5 us (50%)
  waiting for transfers between devices  10.5 us (28%)
  Pallas kernels  7.1 us (19%)
  other arithmetic  0.61 us (2%)
    ppermute x5, waiting for transfers between devices, far(): return lax.ppermute(x, 'corpus', [(i, i ^ shift) for i in range(places)])  8.11 us
    ppermute x5, starting transfers between devices, far(): return lax.ppermute(x, 'corpus', [(i, i ^ shift) for i in range(places)])  7.38 us
    ppermute x2, starting transfers between devices, mixed(): return lax.ppermute(x, ('groups', 'corpus'), pairs)  5.05 us
    ppermute x2, starting transfers between devices, swapped(): return lax.ppermute(x, 'groups', [(0, 1), (1, 0)])  3.87 us
    pallas_call x2, Pallas kernels, scores_call(): pl.pallas_call(functools.partial(scores_kernel, len(blocks), far, tokens,...  3.66 us
    ppermute x3, starting transfers between devices, body(): lax.ppermute(slabs[shift], 'layer', [(i, i ^ shift) for i in range(layers)])  2.19 us
    pallas_call x1, Pallas kernels, body(): pl.pallas_call(prepare_kernel, out_shape=[jax.ShapeDtypeStruct((queries_h...  2.14 us
    ppermute x3, waiting for transfers between devices, body(): lax.ppermute(slabs[shift], 'layer', [(i, i ^ shift) for i in range(layers)])  1.96 us
  transfers between devices with their start and end apart: 12, of which 7 were waited for; matrix products, arithmetic and copies ran while one was open for 0% of the time, Pallas kernels for 13%

profile of v5, /device:TPU:0, one launch (start us, length us, event | category | flops | bytes accessed | tf_op | source)
XLA Modules:
  0.0 36.8 jit_solution(13265437608935898717)
XLA Ops:
  0.0 5.0 %collective-permute-start = (bf16[64,1024]{1,0:T(8,128)(2,1)}, bf16[64,1024]{1,0:T(8,128)(2,1)S(1)}, u32[]{:S(2)}, u32[]{:S(2)}) collective-permute-start(bf16[64,1024]{1,0:T(8,128)(2,1)} %bitcast.14), channel_id=1, source_target_pairs={{0,12},{4,8},{8,4},{12,0},{16,20},{20,16},{24,28},{28,24},{1,13},{... | collective-permute-start | bytes 393224 | tf_op jit(solution)/shard_map/ppermute | solution.py:198
  5.1 0.6 %collective-permute-start.5 = (bf16[64,1024]{1,0:T(8,128)(2,1)}, bf16[64,1024]{1,0:T(8,128)(2,1)S(1)}, u32[]{:S(2)}, u32[]{:S(2)}) collective-permute-start(bf16[64,1024]{1,0:T(8,128)(2,1)} %bitcast.15), channel_id=1, source_target_pairs={{0,8},{4,12},{8,0},{12,4},{1,9},{5,13},{9,1},{13,5},{2,10},{6,14},... | collective-permute-start | bytes 393224 | tf_op jit(solution)/shard_map/ppermute | solution.py:194
  5.6 2.4 %collective-permute-start.4 = (bf16[64,1024]{1,0:T(8,128)(2,1)}, bf16[64,1024]{1,0:T(8,128)(2,1)S(1)}, u32[]{:S(2)}, u32[]{:S(2)}) collective-permute-start(bf16[64,1024]{1,0:T(8,128)(2,1)} %bitcast.18), channel_id=1, source_target_pairs={{0,8},{4,12},{8,0},{12,4},{1,9},{5,13},{9,1},{13,5},{2,10},{6,14},... | collective-permute-start | bytes 393224 | tf_op jit(solution)/shard_map/ppermute | solution.py:194
  8.0 2.1 %prepare.1 = (f32[128,128]{1,0:T(8,128)S(1)}, bf16[128,4096]{1,0:T(8,128)(2,1)S(1)}, bf16[128,4096]{1,0:T(8,128)(2,1)S(1)}, bf16[128,512]{1,0:T(8,128)(2,1)S(1)}...) custom-call(bf16[64,1024]{1,0:T(8,128)(2,1)} %bitcast.16, ...), custom_call_target="tpu_custom_call" | custom-call | tf_op jit(solution)/shard_map/prepare/pallas_call | solution.py:215
  10.2 2.0 %collective-permute-start.1 = (bf16[64,1024]{1,0:T(8,128)(2,1)S(1)}, bf16[64,1024]{1,0:T(8,128)(2,1)S(1)}, u32[]{:S(2)}, u32[]{:S(2)}) collective-permute-start(bf16[64,1024]{1,0:T(8,128)(2,1)S(1)} %collective-permute-done.refs_0_), channel_id=1, source_target_pairs={{0,16},{16,0},{1,17},{17,1},{2,18},{18,2},{3,19},{19,3},{4,20},{20... | collective-permute-start | bytes 393224 | tf_op jit(solution)/shard_map/ppermute | solution.py:201
  12.2 0.5 %collective-permute-done.2.refs_1_ = bf16[64,1024]{1,0:T(8,128)(2,1)S(1)} collective-permute-done((bf16[64,1024]{1,0:T(8,128)(2,1)}, bf16[64,1024]{1,0:T(8,128)(2,1)S(1)}, u32[]{:S(2)}, u32[]{:S(2)}) %collective-permute-start.2) | collective-permute-done | bytes 131104 | tf_op jit(solution)/shard_map/ppermute | solution.py:198
  12.7 1.8 %collective-permute-start.3 = (bf16[64,1024]{1,0:T(8,128)(2,1)S(1)}, bf16[64,1024]{1,0:T(8,128)(2,1)S(1)}, u32[]{:S(2)}, u32[]{:S(2)}) collective-permute-start(bf16[64,1024]{1,0:T(8,128)(2,1)S(1)} %collective-permute-done.2.refs_1_), channel_id=1, source_target_pairs={{0,16},{16,0},{1,17},{17,1},{2,18},{18,2},{3,19},{19,3},{4,20},{20... | collective-permute-start | bytes 393224 | tf_op jit(solution)/shard_map/ppermute | solution.py:201
  14.5 5.6 %collective-permute-done.5.refs_2_ = bf16[64,1024]{1,0:T(8,128)(2,1)S(1)} collective-permute-done((bf16[64,1024]{1,0:T(8,128)(2,1)}, bf16[64,1024]{1,0:T(8,128)(2,1)S(1)}, u32[]{:S(2)}, u32[]{:S(2)}) %collective-permute-start.5) | collective-permute-done | bytes 131104 | tf_op jit(solution)/shard_map/ppermute | solution.py:194
  20.1 0.4 %sides.2.refs_3_ = f32[128,128]{1,0:T(8,128)S(1)} custom-call(bf16[128,4096]{1,0:T(8,128)(2,1)S(1)} %get-tuple-element.27.acts, bf16[128,4096]{1,0:T(8,128)(2,1)S(1)} %get-tuple-element.28.outgrads, bf16[64,1024]{1,0:T(8,128)(2,1)S(1)} %collective-permute-done.refs_0_, bf16[64,1024]{1,0:T(8,128)(2,1)S(1)} %collective-permute-done.2.refs_1_, ...), custom_call_target="tpu_custom_call" | custom-call | tf_op jit(solution)/shard_map/sides/pallas_call | solution.py:204
  20.5 1.4 %collective-permute-done.4.refs_2_ = bf16[64,1024]{1,0:T(8,128)(2,1)S(1)} collective-permute-done((bf16[64,1024]{1,0:T(8,128)(2,1)}, bf16[64,1024]{1,0:T(8,128)(2,1)S(1)}, u32[]{:S(2)}, u32[]{:S(2)}) %collective-permute-start.4) | collective-permute-done | bytes 131104 | tf_op jit(solution)/shard_map/ppermute | solution.py:194
  22.0 0.4 sides.3.refs_0_
  22.3 2.5 %collective-permute-start.6 = (bf16[128,128]{1,0:T(8,128)(2,1)S(1)}, bf16[128,128]{1,0:T(8,128)(2,1)S(1)}, u32[]{:S(2)}, u32[]{:S(2)}) collective-permute-start(bf16[128,128]{1,0:T(8,128)(2,1)S(1)} %sides.3.refs_0_), channel_id=1, source_target_pairs={{0,12},{4,8},{8,4},{12,0},{1,13},{5,9},{9,5},{13,1},{2,14},{6,10},... | collective-permute-start | bytes 98312 | tf_op jit(solution)/shard_map/ppermute | solution.py:194
  24.9 0.5 %collective-permute-start.7 = (bf16[128,128]{1,0:T(8,128)(2,1)S(1)}, bf16[128,128]{1,0:T(8,128)(2,1)S(1)}, u32[]{:S(2)}, u32[]{:S(2)}) collective-permute-start(bf16[128,128]{1,0:T(8,128)(2,1)S(1)} %sides.3.refs_0_), channel_id=1, source_target_pairs={{0,8},{4,12},{8,0},{12,4},{1,9},{5,13},{9,1},{13,5},{2,10},{6,14},... | collective-permute-start | bytes 98312 | tf_op jit(solution)/shard_map/ppermute | solution.py:194
  25.3 1.5 %collective-permute-start.8 = (bf16[128,128]{1,0:T(8,128)(2,1)S(1)}, bf16[128,128]{1,0:T(8,128)(2,1)S(1)}, u32[]{:S(2)}, u32[]{:S(2)}) collective-permute-start(bf16[128,128]{1,0:T(8,128)(2,1)S(1)} %sides.3.refs_0_), channel_id=1, source_target_pairs={{0,4},{4,0},{8,12},{12,8},{1,5},{5,1},{9,13},{13,9},{2,6},{6,2},{1... | collective-permute-start | bytes 98312 | tf_op jit(solution)/shard_map/ppermute | solution.py:194
  26.8 1.8 %scores.2 = (f32[8,80]{1,0:T(8,128)S(1)}, f32[8,80]{1,0:T(8,128)S(1)}, f32[8,80]{1,0:T(8,128)S(1)}, f32[8,80]{1,0:T(8,128)S(1)}) custom-call(bf16[128,512]{1,0:T(8,128)(2,1)S(1)} %get-tuple-element.23.turn, bf16[64,192]{1,0:T(8,128)(2,1)S(1)} %get-tuple-element.24.back, bf16[512,256]{1,0:T(8,128)(2,1)S(1)} %get-tuple-element.25.turns, ...), custom_call_target="tpu_custom_call" | custom-call | tf_op jit(solution)/shard_map/scores/pallas_call | solution.py:266
  28.6 1.1 %collective-permute-done.7.refs_1_ = bf16[128,128]{1,0:T(8,128)(2,1)S(1)} collective-permute-done((bf16[128,128]{1,0:T(8,128)(2,1)S(1)}, bf16[128,128]{1,0:T(8,128)(2,1)S(1)}, u32[]{:S(2)}, u32[]{:S(2)}) %collective-permute-start.7) | collective-permute-done | bytes 32800 | tf_op jit(solution)/shard_map/ppermute | solution.py:194
  29.7 1.8 %scores.3 = (f32[32,128]{1,0:T(8,128)S(1)}, f32[32,128]{1,0:T(8,128)S(1)}, f32[24,4096]{1,0:T(8,128)S(1)}) custom-call(bf16[128,512]{1,0:T(8,128)(2,1)S(1)} %get-tuple-element.23.turn, bf16[64,192]{1,0:T(8,128)(2,1)S(1)} %get-tuple-element.24.back, bf16[512,256]{1,0:T(8,128)(2,1)S(1)} %get-tuple-element.25.turns, f32[64,256]{1,0:T(8,128)S(1)} %get-tuple-element.26.inverse, ...), custom_call_target="tpu_custom_call" | custom-call | tf_op jit(solution)/shard_map/scores/pallas_call | solution.py:266
  31.5 1.5 %collective-permute-start.10 = (f32[32,128]{1,0:T(8,128)S(1)}, f32[32,128]{1,0:T(8,128)S(1)}, u32[]{:S(2)}, u32[]{:S(2)}) collective-permute-start(f32[32,128]{1,0:T(8,128)S(1)} %get-tuple-element.39), channel_id=1, source_target_pairs={{0,2},{1,3},{2,0},{3,1},{4,6},{5,7},{6,4},{7,5},{8,10},{9,11},{10,... | collective-permute-start | bytes 49160 | tf_op jit(solution)/shard_map/ppermute | solution.py:310
  33.0 0.5 %slabs.1 = (f32[32,80]{1,0:T(8,128)S(1)}, f32[32,80]{1,0:T(8,128)S(1)}) custom-call(f32[24,4096]{1,0:T(8,128)S(1)} %get-tuple-element.34.rows, bf16[320,4096]{1,0:T(8,128)(2,1)S(1)} %bitcast.11, f32[8,80]{1,0:T(8,128)S(1)} %get-tuple-element.35.refs_0_, f32[8,80]{1,0:T(8,128)S(1)} %get-tuple-element.36.refs_1_), custom_call_target="tpu_custom_call" | custom-call | tf_op jit(solution)/shard_map/slabs/pallas_call | solution.py:294
  33.6 0.7 %collective-permute-start.9 = (f32[32,80]{1,0:T(8,128)S(1)}, f32[32,80]{1,0:T(8,128)S(1)}, u32[]{:S(2)}, u32[]{:S(2)}) collective-permute-start(f32[32,80]{1,0:T(8,128)S(1)} %get-tuple-element.38), channel_id=1, source_target_pairs={{0,1},{1,0},{2,3},{3,2},{4,5},{5,4},{6,7},{7,6},{8,9},{9,8},{10,11... | collective-permute-start | bytes 30728 | tf_op jit(solution)/shard_map/ppermute | solution.py:310
  34.2 0.8 %collective-permute-done.9 = f32[32,80]{1,0:T(8,128)S(1)} collective-permute-done((f32[32,80]{1,0:T(8,128)S(1)}, f32[32,80]{1,0:T(8,128)S(1)}, u32[]{:S(2)}, u32[]{:S(2)}) %collective-permute-start.9) | collective-permute-done | bytes 10272 | tf_op jit(solution)/shard_map/ppermute | solution.py:310
  35.1 0.2 collective-permute-done.10
  35.3 0.9 %collective-permute-done.11 = f32[32,128]{1,0:T(8,128)S(1)} collective-permute-done((f32[32,128]{1,0:T(8,128)S(1)}, f32[32,128]{1,0:T(8,128)S(1)}, u32[]{:S(2)}, u32[]{:S(2)}) %collective-permute-start.11) | collective-permute-done | bytes 16416 | tf_op jit(solution)/shard_map/ppermute | solution.py:310
  36.2 0.6 %fusion = f32[80,32]{0,1:T(8,128)} fusion(f32[32,128]{1,0:T(8,128)S(1)} %collective-permute-done.11, f32[32,128]{1,0:T(8,128)S(1)} %collective-permute-done.10, f32[32,80]{1,0:T(8,128)S(1)} %get-tuple-element.37, f32[32,80]{1,0:T(8,128)S(1)} %collective-permute-done.9), kind=kLoop, calls=%fused_computation.1 | loop fusion | flops 7680 | bytes 51200 | tf_op jit(solution)/shard_map/transpose | solution.py:311
  (9 shorter events, 0.0 us)
Async XLA Ops:
  0.0 10.1 %collective-permute-start = (bf16[64,1024]{1,0:T(8,128)(2,1)}, bf16[64,1024]{1,0:T(8,128)(2,1)S(1)}, u32[]{:S(2)}, u32[]{:S(2)}) collective-permute-start(bf16[64,1024]{1,0:T(8,128)(2,1)} %bitcast.14), channel_id=1, source_target_pairs={{0,12},{4,8},{8,4},{12,0},{16,20},{20,16},{24,28},{28,24},{1,13},{... | collective-permute-start | bytes 393224 | tf_op jit(solution)/shard_map/ppermute | solution.py:198
  5.0 7.6 %collective-permute-start.2 = (bf16[64,1024]{1,0:T(8,128)(2,1)}, bf16[64,1024]{1,0:T(8,128)(2,1)S(1)}, u32[]{:S(2)}, u32[]{:S(2)}) collective-permute-start(bf16[64,1024]{1,0:T(8,128)(2,1)} %bitcast.17), channel_id=1, source_target_pairs={{0,4},{4,0},{8,12},{12,8},{16,28},{20,24},{24,20},{28,16},{1,5},{5... | collective-permute-start | bytes 393224 | tf_op jit(solution)/shard_map/ppermute | solution.py:198
  5.1 15.1 %collective-permute-start.5 = (bf16[64,1024]{1,0:T(8,128)(2,1)}, bf16[64,1024]{1,0:T(8,128)(2,1)S(1)}, u32[]{:S(2)}, u32[]{:S(2)}) collective-permute-start(bf16[64,1024]{1,0:T(8,128)(2,1)} %bitcast.15), channel_id=1, source_target_pairs={{0,8},{4,12},{8,0},{12,4},{1,9},{5,13},{9,1},{13,5},{2,10},{6,14},... | collective-permute-start | bytes 393224 | tf_op jit(solution)/shard_map/ppermute | solution.py:194
  5.6 16.3 %collective-permute-start.4 = (bf16[64,1024]{1,0:T(8,128)(2,1)}, bf16[64,1024]{1,0:T(8,128)(2,1)S(1)}, u32[]{:S(2)}, u32[]{:S(2)}) collective-permute-start(bf16[64,1024]{1,0:T(8,128)(2,1)} %bitcast.18), channel_id=1, source_target_pairs={{0,8},{4,12},{8,0},{12,4},{1,9},{5,13},{9,1},{13,5},{2,10},{6,14},... | collective-permute-start | bytes 393224 | tf_op jit(solution)/shard_map/ppermute | solution.py:194
  10.1 16.6 %copy-start = (bf16[320,1,4096]{2,0,1:T(8,128)(2,1)S(1)}, bf16[320,1,4096]{2,0,1:T(8,128)(2,1)}, u32[]{:S(2)}) copy-start(bf16[320,1,4096]{2,0,1:T(8,128)(2,1)} %param.15) | copy-start | bytes 7864324
  10.2 11.8 %collective-permute-start.1 = (bf16[64,1024]{1,0:T(8,128)(2,1)S(1)}, bf16[64,1024]{1,0:T(8,128)(2,1)S(1)}, u32[]{:S(2)}, u32[]{:S(2)}) collective-permute-start(bf16[64,1024]{1,0:T(8,128)(2,1)S(1)} %collective-permute-done.refs_0_), channel_id=1, source_target_pairs={{0,16},{16,0},{1,17},{17,1},{2,18},{18,2},{3,19},{19,3},{4,20},{20... | collective-permute-start | bytes 393224 | tf_op jit(solution)/shard_map/ppermute | solution.py:201
  12.7 9.3 %collective-permute-start.3 = (bf16[64,1024]{1,0:T(8,128)(2,1)S(1)}, bf16[64,1024]{1,0:T(8,128)(2,1)S(1)}, u32[]{:S(2)}, u32[]{:S(2)}) collective-permute-start(bf16[64,1024]{1,0:T(8,128)(2,1)S(1)} %collective-permute-done.2.refs_1_), channel_id=1, source_target_pairs={{0,16},{16,0},{1,17},{17,1},{2,18},{18,2},{3,19},{19,3},{4,20},{20... | collective-permute-start | bytes 393224 | tf_op jit(solution)/shard_map/ppermute | solution.py:201
  22.3 6.3 %collective-permute-start.6 = (bf16[128,128]{1,0:T(8,128)(2,1)S(1)}, bf16[128,128]{1,0:T(8,128)(2,1)S(1)}, u32[]{:S(2)}, u32[]{:S(2)}) collective-permute-start(bf16[128,128]{1,0:T(8,128)(2,1)S(1)} %sides.3.refs_0_), channel_id=1, source_target_pairs={{0,12},{4,8},{8,4},{12,0},{1,13},{5,9},{9,5},{13,1},{2,14},{6,10},... | collective-permute-start | bytes 98312 | tf_op jit(solution)/shard_map/ppermute | solution.py:194
  24.9 4.8 %collective-permute-start.7 = (bf16[128,128]{1,0:T(8,128)(2,1)S(1)}, bf16[128,128]{1,0:T(8,128)(2,1)S(1)}, u32[]{:S(2)}, u32[]{:S(2)}) collective-permute-start(bf16[128,128]{1,0:T(8,128)(2,1)S(1)} %sides.3.refs_0_), channel_id=1, source_target_pairs={{0,8},{4,12},{8,0},{12,4},{1,9},{5,13},{9,1},{13,5},{2,10},{6,14},... | collective-permute-start | bytes 98312 | tf_op jit(solution)/shard_map/ppermute | solution.py:194
  25.3 4.4 %collective-permute-start.8 = (bf16[128,128]{1,0:T(8,128)(2,1)S(1)}, bf16[128,128]{1,0:T(8,128)(2,1)S(1)}, u32[]{:S(2)}, u32[]{:S(2)}) collective-permute-start(bf16[128,128]{1,0:T(8,128)(2,1)S(1)} %sides.3.refs_0_), channel_id=1, source_target_pairs={{0,4},{4,0},{8,12},{12,8},{1,5},{5,1},{9,13},{13,9},{2,6},{6,2},{1... | collective-permute-start | bytes 98312 | tf_op jit(solution)/shard_map/ppermute | solution.py:194
  31.5 3.8 %collective-permute-start.10 = (f32[32,128]{1,0:T(8,128)S(1)}, f32[32,128]{1,0:T(8,128)S(1)}, u32[]{:S(2)}, u32[]{:S(2)}) collective-permute-start(f32[32,128]{1,0:T(8,128)S(1)} %get-tuple-element.39), channel_id=1, source_target_pairs={{0,2},{1,3},{2,0},{3,1},{4,6},{5,7},{6,4},{7,5},{8,10},{9,11},{10,... | collective-permute-start | bytes 49160 | tf_op jit(solution)/shard_map/ppermute | solution.py:310
  33.0 3.2 %collective-permute-start.11 = (f32[32,128]{1,0:T(8,128)S(1)}, f32[32,128]{1,0:T(8,128)S(1)}, u32[]{:S(2)}, u32[]{:S(2)}) collective-permute-start(f32[32,128]{1,0:T(8,128)S(1)} %get-tuple-element.40), channel_id=1, source_target_pairs={{0,3},{1,2},{2,1},{3,0},{4,7},{5,6},{6,5},{7,4},{8,11},{9,10},{10,... | collective-permute-start | bytes 49160 | tf_op jit(solution)/shard_map/ppermute | solution.py:310
  33.6 1.5 %collective-permute-start.9 = (f32[32,80]{1,0:T(8,128)S(1)}, f32[32,80]{1,0:T(8,128)S(1)}, u32[]{:S(2)}, u32[]{:S(2)}) collective-permute-start(f32[32,80]{1,0:T(8,128)S(1)} %get-tuple-element.38), channel_id=1, source_target_pairs={{0,1},{1,0},{2,3},{3,2},{4,5},{5,4},{6,7},{7,6},{8,9},{9,8},{10,11... | collective-permute-start | bytes 30728 | tf_op jit(solution)/shard_map/ppermute | solution.py:310

commit v6 on v5

--- a/solution.py
+++ b/solution.py
@@ -86,9 +86,9 @@
     in_high, in_low = split(u_in)
     for at, (of_out, of_in) in enumerate(((out_high, in_high), (out_low, in_low))):
         zero = jnp.zeros_like(of_out)
-        top = jnp.concatenate([of_out, of_out, zero, zero], axis=1)
-        bottom = jnp.concatenate([zero, zero, of_in, of_in], axis=1)
-        turn[:, at * lanes : (at + 1) * lanes] = jnp.concatenate([top, bottom], axis=0)
+        top = jnp.concatenate([of_out, zero], axis=1)
+        bottom = jnp.concatenate([zero, of_in], axis=1)
+        turn[:, at * 2 * rank : (at + 1) * 2 * rank] = jnp.concatenate([top, bottom], axis=0)
     back[...] = jnp.concatenate([out_high, out_low, out_high], axis=1)
     for at, part in enumerate(split(tiled_diagonal(u_in.T, across))):
         turns[at * lanes : (at + 1) * lanes, :] = part
@@ -110,7 +110,7 @@
     parts = []
     for block in blocks:
         both = dot(block[...], turn[...])
-        parts.append(split(both[:, :lanes] + both[:, lanes:]))
+        parts.append(split(both[:, : 2 * rank] + both[:, 2 * rank :]))
     scaled = []
     for group in range(groups):
         high, low = [], []
@@ -122,7 +122,7 @@
         high, low = jnp.concatenate(high, axis=0), jnp.concatenate(low, axis=0)
         out_high, out_low = high[:, :rank], low[:, :rank]
         in_high, in_low = (
-            jnp.where(mask, jnp.concatenate([x[:, lanes // 2 :]] * 2, axis=1), jnp.zeros(mask.shape, bf16))
+            jnp.where(mask, jnp.concatenate([x[:, rank:]] * across, axis=1), jnp.zeros(mask.shape, bf16))
             for x in (high, low)
         )
         gradient = dot(
@@ -218,7 +218,7 @@
             jax.ShapeDtypeStruct((queries_here * tokens, 2 * rank), f32),
             jax.ShapeDtypeStruct(acts.shape, bf16),
             jax.ShapeDtypeStruct(acts.shape, bf16),
-            jax.ShapeDtypeStruct((2 * rank, 2 * lanes), bf16),
+            jax.ShapeDtypeStruct((2 * rank, 4 * rank), bf16),
             jax.ShapeDtypeStruct((rank, 3 * rank), bf16),
             jax.ShapeDtypeStruct((2 * lanes, lanes), bf16),
             jax.ShapeDtypeStruct((rank, lanes), f32),

time: 36.9 us -> 36.7 us (level)
  no operation moved by 1% of the time
where the time goes in v6:
time: 36.7 us; the launch traced here: 36.6 us
  starting transfers between devices  18.5 us (50%)
  waiting for transfers between devices  10.7 us (29%)
  Pallas kernels  6.74 us (18%)
  other arithmetic  0.61 us (2%)
    ppermute x5, waiting for transfers between devices, far(): return lax.ppermute(x, 'corpus', [(i, i ^ shift) for i in range(places)])  8.27 us
    ppermute x5, starting transfers between devices, far(): return lax.ppermute(x, 'corpus', [(i, i ^ shift) for i in range(places)])  7.38 us
    ppermute x2, starting transfers between devices, mixed(): return lax.ppermute(x, ('groups', 'corpus'), pairs)  5.05 us
    ppermute x2, starting transfers between devices, swapped(): return lax.ppermute(x, 'groups', [(0, 1), (1, 0)])  3.87 us
    pallas_call x2, Pallas kernels, scores_call(): pl.pallas_call(functools.partial(scores_kernel, len(blocks), far, tokens,...  3.31 us
    ppermute x3, starting transfers between devices, body(): lax.ppermute(slabs[shift], 'layer', [(i, i ^ shift) for i in range(layers)])  2.19 us
    pallas_call x1, Pallas kernels, body(): pl.pallas_call(prepare_kernel, out_shape=[jax.ShapeDtypeStruct((queries_h...  2.14 us
    ppermute x3, waiting for transfers between devices, body(): lax.ppermute(slabs[shift], 'layer', [(i, i ^ shift) for i in range(layers)])  1.95 us
  transfers between devices with their start and end apart: 12, of which 7 were waited for; matrix products, arithmetic and copies ran while one was open for 0% of the time, Pallas kernels for 13%

profile of v6, /device:TPU:0, one launch (start us, length us, event | category | flops | bytes accessed | tf_op | source)
XLA Modules:
  0.0 36.6 jit_solution(760444027547925031)
XLA Ops:
  0.0 5.0 %collective-permute-start = (bf16[64,1024]{1,0:T(8,128)(2,1)}, bf16[64,1024]{1,0:T(8,128)(2,1)S(1)}, u32[]{:S(2)}, u32[]{:S(2)}) collective-permute-start(bf16[64,1024]{1,0:T(8,128)(2,1)} %bitcast.14), channel_id=1, source_target_pairs={{0,12},{4,8},{8,4},{12,0},{16,20},{20,16},{24,28},{28,24},{1,13},{... | collective-permute-start | bytes 393224 | tf_op jit(solution)/shard_map/ppermute | solution.py:198
  5.1 0.6 %collective-permute-start.5 = (bf16[64,1024]{1,0:T(8,128)(2,1)}, bf16[64,1024]{1,0:T(8,128)(2,1)S(1)}, u32[]{:S(2)}, u32[]{:S(2)}) collective-permute-start(bf16[64,1024]{1,0:T(8,128)(2,1)} %bitcast.15), channel_id=1, source_target_pairs={{0,8},{4,12},{8,0},{12,4},{1,9},{5,13},{9,1},{13,5},{2,10},{6,14},... | collective-permute-start | bytes 393224 | tf_op jit(solution)/shard_map/ppermute | solution.py:194
  5.6 2.4 %collective-permute-start.4 = (bf16[64,1024]{1,0:T(8,128)(2,1)}, bf16[64,1024]{1,0:T(8,128)(2,1)S(1)}, u32[]{:S(2)}, u32[]{:S(2)}) collective-permute-start(bf16[64,1024]{1,0:T(8,128)(2,1)} %bitcast.18), channel_id=1, source_target_pairs={{0,8},{4,12},{8,0},{12,4},{1,9},{5,13},{9,1},{13,5},{2,10},{6,14},... | collective-permute-start | bytes 393224 | tf_op jit(solution)/shard_map/ppermute | solution.py:194
  8.0 2.1 %prepare.1 = (f32[128,128]{1,0:T(8,128)S(1)}, bf16[128,4096]{1,0:T(8,128)(2,1)S(1)}, bf16[128,4096]{1,0:T(8,128)(2,1)S(1)}, bf16[128,256]{1,0:T(8,128)(2,1)S(1)}...) custom-call(bf16[64,1024]{1,0:T(8,128)(2,1)} %bitcast.16, ...), custom_call_target="tpu_custom_call" | custom-call | tf_op jit(solution)/shard_map/prepare/pallas_call | solution.py:215
  10.2 2.0 %collective-permute-start.1 = (bf16[64,1024]{1,0:T(8,128)(2,1)S(1)}, bf16[64,1024]{1,0:T(8,128)(2,1)S(1)}, u32[]{:S(2)}, u32[]{:S(2)}) collective-permute-start(bf16[64,1024]{1,0:T(8,128)(2,1)S(1)} %collective-permute-done.refs_0_), channel_id=1, source_target_pairs={{0,16},{16,0},{1,17},{17,1},{2,18},{18,2},{3,19},{19,3},{4,20},{20... | collective-permute-start | bytes 393224 | tf_op jit(solution)/shard_map/ppermute | solution.py:201
  12.2 0.5 %collective-permute-done.2.refs_1_ = bf16[64,1024]{1,0:T(8,128)(2,1)S(1)} collective-permute-done((bf16[64,1024]{1,0:T(8,128)(2,1)}, bf16[64,1024]{1,0:T(8,128)(2,1)S(1)}, u32[]{:S(2)}, u32[]{:S(2)}) %collective-permute-start.2) | collective-permute-done | bytes 131104 | tf_op jit(solution)/shard_map/ppermute | solution.py:198
  12.7 1.8 %collective-permute-start.3 = (bf16[64,1024]{1,0:T(8,128)(2,1)S(1)}, bf16[64,1024]{1,0:T(8,128)(2,1)S(1)}, u32[]{:S(2)}, u32[]{:S(2)}) collective-permute-start(bf16[64,1024]{1,0:T(8,128)(2,1)S(1)} %collective-permute-done.2.refs_1_), channel_id=1, source_target_pairs={{0,16},{16,0},{1,17},{17,1},{2,18},{18,2},{3,19},{19,3},{4,20},{20... | collective-permute-start | bytes 393224 | tf_op jit(solution)/shard_map/ppermute | solution.py:201
  14.5 5.6 %collective-permute-done.5.refs_2_ = bf16[64,1024]{1,0:T(8,128)(2,1)S(1)} collective-permute-done((bf16[64,1024]{1,0:T(8,128)(2,1)}, bf16[64,1024]{1,0:T(8,128)(2,1)S(1)}, u32[]{:S(2)}, u32[]{:S(2)}) %collective-permute-start.5) | collective-permute-done | bytes 131104 | tf_op jit(solution)/shard_map/ppermute | solution.py:194
  20.1 0.4 %sides.2.refs_3_ = f32[128,128]{1,0:T(8,128)S(1)} custom-call(bf16[128,4096]{1,0:T(8,128)(2,1)S(1)} %get-tuple-element.27.acts, bf16[128,4096]{1,0:T(8,128)(2,1)S(1)} %get-tuple-element.28.outgrads, bf16[64,1024]{1,0:T(8,128)(2,1)S(1)} %collective-permute-done.refs_0_, bf16[64,1024]{1,0:T(8,128)(2,1)S(1)} %collective-permute-done.2.refs_1_, ...), custom_call_target="tpu_custom_call" | custom-call | tf_op jit(solution)/shard_map/sides/pallas_call | solution.py:204
  20.5 1.4 %collective-permute-done.4.refs_2_ = bf16[64,1024]{1,0:T(8,128)(2,1)S(1)} collective-permute-done((bf16[64,1024]{1,0:T(8,128)(2,1)}, bf16[64,1024]{1,0:T(8,128)(2,1)S(1)}, u32[]{:S(2)}, u32[]{:S(2)}) %collective-permute-start.4) | collective-permute-done | bytes 131104 | tf_op jit(solution)/shard_map/ppermute | solution.py:194
  22.0 0.4 sides.3.refs_0_
  22.3 2.5 %collective-permute-start.6 = (bf16[128,128]{1,0:T(8,128)(2,1)S(1)}, bf16[128,128]{1,0:T(8,128)(2,1)S(1)}, u32[]{:S(2)}, u32[]{:S(2)}) collective-permute-start(bf16[128,128]{1,0:T(8,128)(2,1)S(1)} %sides.3.refs_0_), channel_id=1, source_target_pairs={{0,12},{4,8},{8,4},{12,0},{1,13},{5,9},{9,5},{13,1},{2,14},{6,10},... | collective-permute-start | bytes 98312 | tf_op jit(solution)/shard_map/ppermute | solution.py:194
  24.9 0.5 %collective-permute-start.7 = (bf16[128,128]{1,0:T(8,128)(2,1)S(1)}, bf16[128,128]{1,0:T(8,128)(2,1)S(1)}, u32[]{:S(2)}, u32[]{:S(2)}) collective-permute-start(bf16[128,128]{1,0:T(8,128)(2,1)S(1)} %sides.3.refs_0_), channel_id=1, source_target_pairs={{0,8},{4,12},{8,0},{12,4},{1,9},{5,13},{9,1},{13,5},{2,10},{6,14},... | collective-permute-start | bytes 98312 | tf_op jit(solution)/shard_map/ppermute | solution.py:194
  25.3 1.5 %collective-permute-start.8 = (bf16[128,128]{1,0:T(8,128)(2,1)S(1)}, bf16[128,128]{1,0:T(8,128)(2,1)S(1)}, u32[]{:S(2)}, u32[]{:S(2)}) collective-permute-start(bf16[128,128]{1,0:T(8,128)(2,1)S(1)} %sides.3.refs_0_), channel_id=1, source_target_pairs={{0,4},{4,0},{8,12},{12,8},{1,5},{5,1},{9,13},{13,9},{2,6},{6,2},{1... | collective-permute-start | bytes 98312 | tf_op jit(solution)/shard_map/ppermute | solution.py:194
  26.8 1.7 %scores.2 = (f32[8,80]{1,0:T(8,128)S(1)}, f32[8,80]{1,0:T(8,128)S(1)}, f32[8,80]{1,0:T(8,128)S(1)}, f32[8,80]{1,0:T(8,128)S(1)}) custom-call(bf16[128,256]{1,0:T(8,128)(2,1)S(1)} %get-tuple-element.23.turn, bf16[64,192]{1,0:T(8,128)(2,1)S(1)} %get-tuple-element.24.back, bf16[512,256]{1,0:T(8,128)(2,1)S(1)} %get-tuple-element.25.turns, ...), custom_call_target="tpu_custom_call" | custom-call | tf_op jit(solution)/shard_map/scores/pallas_call | solution.py:266
  28.5 1.2 %collective-permute-done.7.refs_1_ = bf16[128,128]{1,0:T(8,128)(2,1)S(1)} collective-permute-done((bf16[128,128]{1,0:T(8,128)(2,1)S(1)}, bf16[128,128]{1,0:T(8,128)(2,1)S(1)}, u32[]{:S(2)}, u32[]{:S(2)}) %collective-permute-start.7) | collective-permute-done | bytes 32800 | tf_op jit(solution)/shard_map/ppermute | solution.py:194
  29.7 1.6 %scores.3 = (f32[32,128]{1,0:T(8,128)S(1)}, f32[32,128]{1,0:T(8,128)S(1)}, f32[24,4096]{1,0:T(8,128)S(1)}) custom-call(bf16[128,256]{1,0:T(8,128)(2,1)S(1)} %get-tuple-element.23.turn, bf16[64,192]{1,0:T(8,128)(2,1)S(1)} %get-tuple-element.24.back, bf16[512,256]{1,0:T(8,128)(2,1)S(1)} %get-tuple-element.25.turns, f32[64,256]{1,0:T(8,128)S(1)} %get-tuple-element.26.inverse, ...), custom_call_target="tpu_custom_call" | custom-call | tf_op jit(solution)/shard_map/scores/pallas_call | solution.py:266
  31.3 1.5 %collective-permute-start.10 = (f32[32,128]{1,0:T(8,128)S(1)}, f32[32,128]{1,0:T(8,128)S(1)}, u32[]{:S(2)}, u32[]{:S(2)}) collective-permute-start(f32[32,128]{1,0:T(8,128)S(1)} %get-tuple-element.39), channel_id=1, source_target_pairs={{0,2},{1,3},{2,0},{3,1},{4,6},{5,7},{6,4},{7,5},{8,10},{9,11},{10,... | collective-permute-start | bytes 49160 | tf_op jit(solution)/shard_map/ppermute | solution.py:310
  32.8 0.5 %slabs.1 = (f32[32,80]{1,0:T(8,128)S(1)}, f32[32,80]{1,0:T(8,128)S(1)}) custom-call(f32[24,4096]{1,0:T(8,128)S(1)} %get-tuple-element.34.rows, bf16[320,4096]{1,0:T(8,128)(2,1)S(1)} %bitcast.11, f32[8,80]{1,0:T(8,128)S(1)} %get-tuple-element.35.refs_0_, f32[8,80]{1,0:T(8,128)S(1)} %get-tuple-element.36.refs_1_), custom_call_target="tpu_custom_call" | custom-call | tf_op jit(solution)/shard_map/slabs/pallas_call | solution.py:294
  33.4 0.7 %collective-permute-start.9 = (f32[32,80]{1,0:T(8,128)S(1)}, f32[32,80]{1,0:T(8,128)S(1)}, u32[]{:S(2)}, u32[]{:S(2)}) collective-permute-start(f32[32,80]{1,0:T(8,128)S(1)} %get-tuple-element.38), channel_id=1, source_target_pairs={{0,1},{1,0},{2,3},{3,2},{4,5},{5,4},{6,7},{7,6},{8,9},{9,8},{10,11... | collective-permute-start | bytes 30728 | tf_op jit(solution)/shard_map/ppermute | solution.py:310
  34.0 0.8 %collective-permute-done.9 = f32[32,80]{1,0:T(8,128)S(1)} collective-permute-done((f32[32,80]{1,0:T(8,128)S(1)}, f32[32,80]{1,0:T(8,128)S(1)}, u32[]{:S(2)}, u32[]{:S(2)}) %collective-permute-start.9) | collective-permute-done | bytes 10272 | tf_op jit(solution)/shard_map/ppermute | solution.py:310
  34.9 0.2 collective-permute-done.10
  35.1 0.9 %collective-permute-done.11 = f32[32,128]{1,0:T(8,128)S(1)} collective-permute-done((f32[32,128]{1,0:T(8,128)S(1)}, f32[32,128]{1,0:T(8,128)S(1)}, u32[]{:S(2)}, u32[]{:S(2)}) %collective-permute-start.11) | collective-permute-done | bytes 16416 | tf_op jit(solution)/shard_map/ppermute | solution.py:310
  36.0 0.6 %fusion = f32[80,32]{0,1:T(8,128)} fusion(f32[32,128]{1,0:T(8,128)S(1)} %collective-permute-done.11, f32[32,128]{1,0:T(8,128)S(1)} %collective-permute-done.10, f32[32,80]{1,0:T(8,128)S(1)} %get-tuple-element.37, f32[32,80]{1,0:T(8,128)S(1)} %collective-permute-done.9), kind=kLoop, calls=%fused_computation.1 | loop fusion | flops 7680 | bytes 51200 | tf_op jit(solution)/shard_map/transpose | solution.py:311
  (9 shorter events, 0.0 us)
Async XLA Ops:
  0.0 10.1 %collective-permute-start = (bf16[64,1024]{1,0:T(8,128)(2,1)}, bf16[64,1024]{1,0:T(8,128)(2,1)S(1)}, u32[]{:S(2)}, u32[]{:S(2)}) collective-permute-start(bf16[64,1024]{1,0:T(8,128)(2,1)} %bitcast.14), channel_id=1, source_target_pairs={{0,12},{4,8},{8,4},{12,0},{16,20},{20,16},{24,28},{28,24},{1,13},{... | collective-permute-start | bytes 393224 | tf_op jit(solution)/shard_map/ppermute | solution.py:198
  5.0 7.6 %collective-permute-start.2 = (bf16[64,1024]{1,0:T(8,128)(2,1)}, bf16[64,1024]{1,0:T(8,128)(2,1)S(1)}, u32[]{:S(2)}, u32[]{:S(2)}) collective-permute-start(bf16[64,1024]{1,0:T(8,128)(2,1)} %bitcast.17), channel_id=1, source_target_pairs={{0,4},{4,0},{8,12},{12,8},{16,28},{20,24},{24,20},{28,16},{1,5},{5... | collective-permute-start | bytes 393224 | tf_op jit(solution)/shard_map/ppermute | solution.py:198
  5.1 15.1 %collective-permute-start.5 = (bf16[64,1024]{1,0:T(8,128)(2,1)}, bf16[64,1024]{1,0:T(8,128)(2,1)S(1)}, u32[]{:S(2)}, u32[]{:S(2)}) collective-permute-start(bf16[64,1024]{1,0:T(8,128)(2,1)} %bitcast.15), channel_id=1, source_target_pairs={{0,8},{4,12},{8,0},{12,4},{1,9},{5,13},{9,1},{13,5},{2,10},{6,14},... | collective-permute-start | bytes 393224 | tf_op jit(solution)/shard_map/ppermute | solution.py:194
  5.6 16.3 %collective-permute-start.4 = (bf16[64,1024]{1,0:T(8,128)(2,1)}, bf16[64,1024]{1,0:T(8,128)(2,1)S(1)}, u32[]{:S(2)}, u32[]{:S(2)}) collective-permute-start(bf16[64,1024]{1,0:T(8,128)(2,1)} %bitcast.18), channel_id=1, source_target_pairs={{0,8},{4,12},{8,0},{12,4},{1,9},{5,13},{9,1},{13,5},{2,10},{6,14},... | collective-permute-start | bytes 393224 | tf_op jit(solution)/shard_map/ppermute | solution.py:194
  10.1 16.6 %copy-start = (bf16[320,1,4096]{2,0,1:T(8,128)(2,1)S(1)}, bf16[320,1,4096]{2,0,1:T(8,128)(2,1)}, u32[]{:S(2)}) copy-start(bf16[320,1,4096]{2,0,1:T(8,128)(2,1)} %param.15) | copy-start | bytes 7864324
  10.2 11.8 %collective-permute-start.1 = (bf16[64,1024]{1,0:T(8,128)(2,1)S(1)}, bf16[64,1024]{1,0:T(8,128)(2,1)S(1)}, u32[]{:S(2)}, u32[]{:S(2)}) collective-permute-start(bf16[64,1024]{1,0:T(8,128)(2,1)S(1)} %collective-permute-done.refs_0_), channel_id=1, source_target_pairs={{0,16},{16,0},{1,17},{17,1},{2,18},{18,2},{3,19},{19,3},{4,20},{20... | collective-permute-start | bytes 393224 | tf_op jit(solution)/shard_map/ppermute | solution.py:201
  12.7 9.3 %collective-permute-start.3 = (bf16[64,1024]{1,0:T(8,128)(2,1)S(1)}, bf16[64,1024]{1,0:T(8,128)(2,1)S(1)}, u32[]{:S(2)}, u32[]{:S(2)}) collective-permute-start(bf16[64,1024]{1,0:T(8,128)(2,1)S(1)} %collective-permute-done.2.refs_1_), channel_id=1, source_target_pairs={{0,16},{16,0},{1,17},{17,1},{2,18},{18,2},{3,19},{19,3},{4,20},{20... | collective-permute-start | bytes 393224 | tf_op jit(solution)/shard_map/ppermute | solution.py:201
  22.3 6.1 %collective-permute-start.6 = (bf16[128,128]{1,0:T(8,128)(2,1)S(1)}, bf16[128,128]{1,0:T(8,128)(2,1)S(1)}, u32[]{:S(2)}, u32[]{:S(2)}) collective-permute-start(bf16[128,128]{1,0:T(8,128)(2,1)S(1)} %sides.3.refs_0_), channel_id=1, source_target_pairs={{0,12},{4,8},{8,4},{12,0},{1,13},{5,9},{9,5},{13,1},{2,14},{6,10},... | collective-permute-start | bytes 98312 | tf_op jit(solution)/shard_map/ppermute | solution.py:194
  24.9 4.8 %collective-permute-start.7 = (bf16[128,128]{1,0:T(8,128)(2,1)S(1)}, bf16[128,128]{1,0:T(8,128)(2,1)S(1)}, u32[]{:S(2)}, u32[]{:S(2)}) collective-permute-start(bf16[128,128]{1,0:T(8,128)(2,1)S(1)} %sides.3.refs_0_), channel_id=1, source_target_pairs={{0,8},{4,12},{8,0},{12,4},{1,9},{5,13},{9,1},{13,5},{2,10},{6,14},... | collective-permute-start | bytes 98312 | tf_op jit(solution)/shard_map/ppermute | solution.py:194
  25.3 4.4 %collective-permute-start.8 = (bf16[128,128]{1,0:T(8,128)(2,1)S(1)}, bf16[128,128]{1,0:T(8,128)(2,1)S(1)}, u32[]{:S(2)}, u32[]{:S(2)}) collective-permute-start(bf16[128,128]{1,0:T(8,128)(2,1)S(1)} %sides.3.refs_0_), channel_id=1, source_target_pairs={{0,4},{4,0},{8,12},{12,8},{1,5},{5,1},{9,13},{13,9},{2,6},{6,2},{1... | collective-permute-start | bytes 98312 | tf_op jit(solution)/shard_map/ppermute | solution.py:194
  31.3 3.8 %collective-permute-start.10 = (f32[32,128]{1,0:T(8,128)S(1)}, f32[32,128]{1,0:T(8,128)S(1)}, u32[]{:S(2)}, u32[]{:S(2)}) collective-permute-start(f32[32,128]{1,0:T(8,128)S(1)} %get-tuple-element.39), channel_id=1, source_target_pairs={{0,2},{1,3},{2,0},{3,1},{4,6},{5,7},{6,4},{7,5},{8,10},{9,11},{10,... | collective-permute-start | bytes 49160 | tf_op jit(solution)/shard_map/ppermute | solution.py:310
  32.8 3.2 %collective-permute-start.11 = (f32[32,128]{1,0:T(8,128)S(1)}, f32[32,128]{1,0:T(8,128)S(1)}, u32[]{:S(2)}, u32[]{:S(2)}) collective-permute-start(f32[32,128]{1,0:T(8,128)S(1)} %get-tuple-element.40), channel_id=1, source_target_pairs={{0,3},{1,2},{2,1},{3,0},{4,7},{5,6},{6,5},{7,4},{8,11},{9,10},{10,... | collective-permute-start | bytes 49160 | tf_op jit(solution)/shard_map/ppermute | solution.py:310
  33.4 1.5 %collective-permute-start.9 = (f32[32,80]{1,0:T(8,128)S(1)}, f32[32,80]{1,0:T(8,128)S(1)}, u32[]{:S(2)}, u32[]{:S(2)}) collective-permute-start(f32[32,80]{1,0:T(8,128)S(1)} %get-tuple-element.38), channel_id=1, source_target_pairs={{0,1},{1,0},{2,3},{3,2},{4,5},{5,4},{6,7},{7,6},{8,9},{9,8},{10,11... | collective-permute-start | bytes 30728 | tf_op jit(solution)/shard_map/ppermute | solution.py:310

commit v7 on v6

--- a/solution.py
+++ b/solution.py
@@ -283,10 +283,10 @@
         second = lambda g, p: (p ^ jnp.where(g == 0, 1, 3)) * width
         mine = lambda g, p: (p ^ 2) * width + g * part
         other = lambda g, p: (p ^ 2) * width + (1 - g) * part
-        total = sides_call([(1, first), (0, second), (1, direct)], [near, near_out, last], [total], f32)
-        sides = sides_call(
-            [(1, second), (0, first), (0, direct)], [swapped(near), swapped(near_out), last_out], [total], bf16
+        total = sides_call(
+            [(1, first), (0, second), (1, direct), (1, second)], [near, near_out, last, swapped(near)], [total], f32
         )
+        sides = sides_call([(0, first), (0, direct)], [swapped(near_out), last_out], [total], bf16)
         arrived = [far(sides, shift) for shift in (3, 2, 1)]
         own = scores_call((), tuple(range(layers)), [sides], [], 1)
         soon, later = tuple(range(layers // 2, layers)), tuple(range(layers // 2))

time: 36.7 us -> 36.7 us (level)
  starting transfers between devices: 18.5 us -> 17.7 us
  waiting for transfers between devices: 10.7 us -> 11.4 us
    ppermute x2, starting transfers between devices: 3.87 us -> 2.03 us  [swapped(): return lax.ppermute(x, 'groups', [(0, 1), (1, 0)])]
    ppermute x2, waiting for transfers between devices: 0.48 us -> 1.85 us  [mixed(): return lax.ppermute(x, ('groups', 'corpus'), pairs)]
    ppermute x5, starting transfers between devices: 7.38 us -> 8.47 us  [far(): return lax.ppermute(x, 'corpus', [(i, i ^ shift) for i in range(places)])]
    ppermute x5, waiting for transfers between devices: 8.27 us -> 7.55 us  [far(): return lax.ppermute(x, 'corpus', [(i, i ^ shift) for i in range(places)])]
where the time goes in v7:
time: 36.7 us; the launch traced here: 36.5 us
  starting transfers between devices  17.7 us (48%)
  waiting for transfers between devices  11.4 us (31%)
  Pallas kernels  6.76 us (18%)
  other arithmetic  0.61 us (2%)
    ppermute x5, starting transfers between devices, far(): return lax.ppermute(x, 'corpus', [(i, i ^ shift) for i in range(places)])  8.47 us
    ppermute x5, waiting for transfers between devices, far(): return lax.ppermute(x, 'corpus', [(i, i ^ shift) for i in range(places)])  7.55 us
    ppermute x2, starting transfers between devices, mixed(): return lax.ppermute(x, ('groups', 'corpus'), pairs)  5.05 us
    pallas_call x2, Pallas kernels, scores_call(): pl.pallas_call(functools.partial(scores_kernel, len(blocks), far, tokens,...  3.31 us
    ppermute x3, starting transfers between devices, body(): lax.ppermute(slabs[shift], 'layer', [(i, i ^ shift) for i in range(layers)])  2.19 us
    pallas_call x1, Pallas kernels, body(): pl.pallas_call(prepare_kernel, out_shape=[jax.ShapeDtypeStruct((queries_h...  2.14 us
    ppermute x2, starting transfers between devices, swapped(): return lax.ppermute(x, 'groups', [(0, 1), (1, 0)])  2.03 us
    ppermute x3, waiting for transfers between devices, body(): lax.ppermute(slabs[shift], 'layer', [(i, i ^ shift) for i in range(layers)])  1.96 us
  transfers between devices with their start and end apart: 12, of which 7 were waited for; matrix products, arithmetic and copies ran while one was open for 0% of the time, Pallas kernels for 13%

profile of v7, /device:TPU:0, one launch (start us, length us, event | category | flops | bytes accessed | tf_op | source)
XLA Modules:
  0.0 36.5 jit_solution(1974072500013090599)
XLA Ops:
  0.0 5.0 %collective-permute-start.3 = (bf16[64,1024]{1,0:T(8,128)(2,1)}, bf16[64,1024]{1,0:T(8,128)(2,1)S(1)}, u32[]{:S(2)}, u32[]{:S(2)}) collective-permute-start(bf16[64,1024]{1,0:T(8,128)(2,1)} %bitcast.14), channel_id=1, source_target_pairs={{0,12},{4,8},{8,4},{12,0},{16,20},{20,16},{24,28},{28,24},{1,13},{... | collective-permute-start | bytes 393224 | tf_op jit(solution)/shard_map/ppermute | solution.py:198
  5.1 0.6 %collective-permute-start.4 = (bf16[64,1024]{1,0:T(8,128)(2,1)}, bf16[64,1024]{1,0:T(8,128)(2,1)S(1)}, u32[]{:S(2)}, u32[]{:S(2)}) collective-permute-start(bf16[64,1024]{1,0:T(8,128)(2,1)} %bitcast.15), channel_id=1, source_target_pairs={{0,8},{4,12},{8,0},{12,4},{1,9},{5,13},{9,1},{13,5},{2,10},{6,14},... | collective-permute-start | bytes 393224 | tf_op jit(solution)/shard_map/ppermute | solution.py:194
  5.6 2.1 %prepare.1 = (f32[128,128]{1,0:T(8,128)S(1)}, bf16[128,4096]{1,0:T(8,128)(2,1)S(1)}, bf16[128,4096]{1,0:T(8,128)(2,1)S(1)}, bf16[128,256]{1,0:T(8,128)(2,1)S(1)}...) custom-call(bf16[64,1024]{1,0:T(8,128)(2,1)} %bitcast.16, ...), custom_call_target="tpu_custom_call" | custom-call | tf_op jit(solution)/shard_map/prepare/pallas_call | solution.py:215
  7.8 0.0 copy-start
  7.8 1.9 %collective-permute-done.3.refs_0_ = bf16[64,1024]{1,0:T(8,128)(2,1)S(1)} collective-permute-done((bf16[64,1024]{1,0:T(8,128)(2,1)}, bf16[64,1024]{1,0:T(8,128)(2,1)S(1)}, u32[]{:S(2)}, u32[]{:S(2)}) %collective-permute-start.3) | collective-permute-done | bytes 131104 | tf_op jit(solution)/shard_map/ppermute | solution.py:198
  9.6 3.5 %collective-permute-start.2 = (bf16[64,1024]{1,0:T(8,128)(2,1)}, bf16[64,1024]{1,0:T(8,128)(2,1)S(1)}, u32[]{:S(2)}, u32[]{:S(2)}) collective-permute-start(bf16[64,1024]{1,0:T(8,128)(2,1)} %bitcast.19), channel_id=1, source_target_pairs={{0,8},{4,12},{8,0},{12,4},{1,9},{5,13},{9,1},{13,5},{2,10},{6,14},... | collective-permute-start | bytes 393224 | tf_op jit(solution)/shard_map/ppermute | solution.py:194
  13.1 2.0 %collective-permute-start.1 = (bf16[64,1024]{1,0:T(8,128)(2,1)S(1)}, bf16[64,1024]{1,0:T(8,128)(2,1)S(1)}, u32[]{:S(2)}, u32[]{:S(2)}) collective-permute-start(bf16[64,1024]{1,0:T(8,128)(2,1)S(1)} %collective-permute-done.refs_1_), channel_id=1, source_target_pairs={{0,16},{16,0},{1,17},{17,1},{2,18},{18,2},{3,19},{19,3},{4,20},{20... | collective-permute-start | bytes 393224 | tf_op jit(solution)/shard_map/ppermute | solution.py:201
  15.1 5.0 %collective-permute-done.4.refs_2_ = bf16[64,1024]{1,0:T(8,128)(2,1)S(1)} collective-permute-done((bf16[64,1024]{1,0:T(8,128)(2,1)}, bf16[64,1024]{1,0:T(8,128)(2,1)S(1)}, u32[]{:S(2)}, u32[]{:S(2)}) %collective-permute-start.4) | collective-permute-done | bytes 131104 | tf_op jit(solution)/shard_map/ppermute | solution.py:194
  20.1 0.5 %sides.2.refs_2_ = f32[128,128]{1,0:T(8,128)S(1)} custom-call(bf16[128,4096]{1,0:T(8,128)(2,1)S(1)} %get-tuple-element.27.acts, bf16[128,4096]{1,0:T(8,128)(2,1)S(1)} %get-tuple-element.28.outgrads, bf16[64,1024]{1,0:T(8,128)(2,1)S(1)} %collective-permute-done.3.refs_0_, bf16[64,1024]{1,0:T(8,128)(2,1)S(1)} %collective-permute-done.refs_1_, ...), custom_call_target="tpu_custom_call" | custom-call | tf_op jit(solution)/shard_map/sides/pallas_call | solution.py:204
  20.6 1.3 %collective-permute-done.2.refs_1_ = bf16[64,1024]{1,0:T(8,128)(2,1)S(1)} collective-permute-done((bf16[64,1024]{1,0:T(8,128)(2,1)}, bf16[64,1024]{1,0:T(8,128)(2,1)S(1)}, u32[]{:S(2)}, u32[]{:S(2)}) %collective-permute-start.2) | collective-permute-done | bytes 131104 | tf_op jit(solution)/shard_map/ppermute | solution.py:194
  22.0 0.3 sides.3.refs_0_
  22.2 2.5 %collective-permute-start.6 = (bf16[128,128]{1,0:T(8,128)(2,1)S(1)}, bf16[128,128]{1,0:T(8,128)(2,1)S(1)}, u32[]{:S(2)}, u32[]{:S(2)}) collective-permute-start(bf16[128,128]{1,0:T(8,128)(2,1)S(1)} %sides.3.refs_0_), channel_id=1, source_target_pairs={{0,12},{4,8},{8,4},{12,0},{1,13},{5,9},{9,5},{13,1},{2,14},{6,10},... | collective-permute-start | bytes 98312 | tf_op jit(solution)/shard_map/ppermute | solution.py:194
  24.8 0.5 %collective-permute-start.7 = (bf16[128,128]{1,0:T(8,128)(2,1)S(1)}, bf16[128,128]{1,0:T(8,128)(2,1)S(1)}, u32[]{:S(2)}, u32[]{:S(2)}) collective-permute-start(bf16[128,128]{1,0:T(8,128)(2,1)S(1)} %sides.3.refs_0_), channel_id=1, source_target_pairs={{0,8},{4,12},{8,0},{12,4},{1,9},{5,13},{9,1},{13,5},{2,10},{6,14},... | collective-permute-start | bytes 98312 | tf_op jit(solution)/shard_map/ppermute | solution.py:194
  25.3 1.4 %collective-permute-start.8 = (bf16[128,128]{1,0:T(8,128)(2,1)S(1)}, bf16[128,128]{1,0:T(8,128)(2,1)S(1)}, u32[]{:S(2)}, u32[]{:S(2)}) collective-permute-start(bf16[128,128]{1,0:T(8,128)(2,1)S(1)} %sides.3.refs_0_), channel_id=1, source_target_pairs={{0,4},{4,0},{8,12},{12,8},{1,5},{5,1},{9,13},{13,9},{2,6},{6,2},{1... | collective-permute-start | bytes 98312 | tf_op jit(solution)/shard_map/ppermute | solution.py:194
  26.7 1.7 %scores.2 = (f32[8,80]{1,0:T(8,128)S(1)}, f32[8,80]{1,0:T(8,128)S(1)}, f32[8,80]{1,0:T(8,128)S(1)}, f32[8,80]{1,0:T(8,128)S(1)}) custom-call(bf16[128,256]{1,0:T(8,128)(2,1)S(1)} %get-tuple-element.23.turn, bf16[64,192]{1,0:T(8,128)(2,1)S(1)} %get-tuple-element.24.back, bf16[512,256]{1,0:T(8,128)(2,1)S(1)} %get-tuple-element.25.turns, ...), custom_call_target="tpu_custom_call" | custom-call | tf_op jit(solution)/shard_map/scores/pallas_call | solution.py:266
  28.4 1.2 %collective-permute-done.7.refs_1_ = bf16[128,128]{1,0:T(8,128)(2,1)S(1)} collective-permute-done((bf16[128,128]{1,0:T(8,128)(2,1)S(1)}, bf16[128,128]{1,0:T(8,128)(2,1)S(1)}, u32[]{:S(2)}, u32[]{:S(2)}) %collective-permute-start.7) | collective-permute-done | bytes 32800 | tf_op jit(solution)/shard_map/ppermute | solution.py:194
  29.6 1.6 %scores.3 = (f32[32,128]{1,0:T(8,128)S(1)}, f32[32,128]{1,0:T(8,128)S(1)}, f32[24,4096]{1,0:T(8,128)S(1)}) custom-call(bf16[128,256]{1,0:T(8,128)(2,1)S(1)} %get-tuple-element.23.turn, bf16[64,192]{1,0:T(8,128)(2,1)S(1)} %get-tuple-element.24.back, bf16[512,256]{1,0:T(8,128)(2,1)S(1)} %get-tuple-element.25.turns, f32[64,256]{1,0:T(8,128)S(1)} %get-tuple-element.26.inverse, ...), custom_call_target="tpu_custom_call" | custom-call | tf_op jit(solution)/shard_map/scores/pallas_call | solution.py:266
  31.2 1.5 %collective-permute-start.10 = (f32[32,128]{1,0:T(8,128)S(1)}, f32[32,128]{1,0:T(8,128)S(1)}, u32[]{:S(2)}, u32[]{:S(2)}) collective-permute-start(f32[32,128]{1,0:T(8,128)S(1)} %get-tuple-element.39), channel_id=1, source_target_pairs={{0,2},{1,3},{2,0},{3,1},{4,6},{5,7},{6,4},{7,5},{8,10},{9,11},{10,... | collective-permute-start | bytes 49160 | tf_op jit(solution)/shard_map/ppermute | solution.py:310
  32.8 0.5 %slabs.1 = (f32[32,80]{1,0:T(8,128)S(1)}, f32[32,80]{1,0:T(8,128)S(1)}) custom-call(f32[24,4096]{1,0:T(8,128)S(1)} %get-tuple-element.34.rows, bf16[320,4096]{1,0:T(8,128)(2,1)S(1)} %bitcast.11, f32[8,80]{1,0:T(8,128)S(1)} %get-tuple-element.35.refs_0_, f32[8,80]{1,0:T(8,128)S(1)} %get-tuple-element.36.refs_1_), custom_call_target="tpu_custom_call" | custom-call | tf_op jit(solution)/shard_map/slabs/pallas_call | solution.py:294
  33.3 0.7 %collective-permute-start.9 = (f32[32,80]{1,0:T(8,128)S(1)}, f32[32,80]{1,0:T(8,128)S(1)}, u32[]{:S(2)}, u32[]{:S(2)}) collective-permute-start(f32[32,80]{1,0:T(8,128)S(1)} %get-tuple-element.38), channel_id=1, source_target_pairs={{0,1},{1,0},{2,3},{3,2},{4,5},{5,4},{6,7},{7,6},{8,9},{9,8},{10,11... | collective-permute-start | bytes 30728 | tf_op jit(solution)/shard_map/ppermute | solution.py:310
  34.0 0.8 %collective-permute-done.9 = f32[32,80]{1,0:T(8,128)S(1)} collective-permute-done((f32[32,80]{1,0:T(8,128)S(1)}, f32[32,80]{1,0:T(8,128)S(1)}, u32[]{:S(2)}, u32[]{:S(2)}) %collective-permute-start.9) | collective-permute-done | bytes 10272 | tf_op jit(solution)/shard_map/ppermute | solution.py:310
  34.8 0.2 collective-permute-done.10
  35.0 0.9 %collective-permute-done.11 = f32[32,128]{1,0:T(8,128)S(1)} collective-permute-done((f32[32,128]{1,0:T(8,128)S(1)}, f32[32,128]{1,0:T(8,128)S(1)}, u32[]{:S(2)}, u32[]{:S(2)}) %collective-permute-start.11) | collective-permute-done | bytes 16416 | tf_op jit(solution)/shard_map/ppermute | solution.py:310
  35.9 0.6 %fusion = f32[80,32]{0,1:T(8,128)} fusion(f32[32,128]{1,0:T(8,128)S(1)} %collective-permute-done.11, f32[32,128]{1,0:T(8,128)S(1)} %collective-permute-done.10, f32[32,80]{1,0:T(8,128)S(1)} %get-tuple-element.37, f32[32,80]{1,0:T(8,128)S(1)} %collective-permute-done.9), kind=kLoop, calls=%fused_computation.1 | loop fusion | flops 7680 | bytes 51200 | tf_op jit(solution)/shard_map/transpose | solution.py:311
  (9 shorter events, 0.0 us)
Async XLA Ops:
  0.0 9.6 %collective-permute-start.3 = (bf16[64,1024]{1,0:T(8,128)(2,1)}, bf16[64,1024]{1,0:T(8,128)(2,1)S(1)}, u32[]{:S(2)}, u32[]{:S(2)}) collective-permute-start(bf16[64,1024]{1,0:T(8,128)(2,1)} %bitcast.14), channel_id=1, source_target_pairs={{0,12},{4,8},{8,4},{12,0},{16,20},{20,16},{24,28},{28,24},{1,13},{... | collective-permute-start | bytes 393224 | tf_op jit(solution)/shard_map/ppermute | solution.py:198
  5.0 8.0 %collective-permute-start = (bf16[64,1024]{1,0:T(8,128)(2,1)}, bf16[64,1024]{1,0:T(8,128)(2,1)S(1)}, u32[]{:S(2)}, u32[]{:S(2)}) collective-permute-start(bf16[64,1024]{1,0:T(8,128)(2,1)} %bitcast.17), channel_id=1, source_target_pairs={{0,4},{4,0},{8,12},{12,8},{16,28},{20,24},{24,20},{28,16},{1,5},{5... | collective-permute-start | bytes 393224 | tf_op jit(solution)/shard_map/ppermute | solution.py:198
  5.1 15.1 %collective-permute-start.4 = (bf16[64,1024]{1,0:T(8,128)(2,1)}, bf16[64,1024]{1,0:T(8,128)(2,1)S(1)}, u32[]{:S(2)}, u32[]{:S(2)}) collective-permute-start(bf16[64,1024]{1,0:T(8,128)(2,1)} %bitcast.15), channel_id=1, source_target_pairs={{0,8},{4,12},{8,0},{12,4},{1,9},{5,13},{9,1},{13,5},{2,10},{6,14},... | collective-permute-start | bytes 393224 | tf_op jit(solution)/shard_map/ppermute | solution.py:194
  7.8 18.9 %copy-start = (bf16[320,1,4096]{2,0,1:T(8,128)(2,1)S(1)}, bf16[320,1,4096]{2,0,1:T(8,128)(2,1)}, u32[]{:S(2)}) copy-start(bf16[320,1,4096]{2,0,1:T(8,128)(2,1)} %param.15) | copy-start | bytes 7864324
  9.6 10.5 %collective-permute-start.5 = (bf16[64,1024]{1,0:T(8,128)(2,1)S(1)}, bf16[64,1024]{1,0:T(8,128)(2,1)S(1)}, u32[]{:S(2)}, u32[]{:S(2)}) collective-permute-start(bf16[64,1024]{1,0:T(8,128)(2,1)S(1)} %collective-permute-done.3.refs_0_), channel_id=1, source_target_pairs={{0,16},{16,0},{1,17},{17,1},{2,18},{18,2},{3,19},{19,3},{4,20},{20... | collective-permute-start | bytes 393224 | tf_op jit(solution)/shard_map/ppermute | solution.py:201
  9.6 12.3 %collective-permute-start.2 = (bf16[64,1024]{1,0:T(8,128)(2,1)}, bf16[64,1024]{1,0:T(8,128)(2,1)S(1)}, u32[]{:S(2)}, u32[]{:S(2)}) collective-permute-start(bf16[64,1024]{1,0:T(8,128)(2,1)} %bitcast.19), channel_id=1, source_target_pairs={{0,8},{4,12},{8,0},{12,4},{1,9},{5,13},{9,1},{13,5},{2,10},{6,14},... | collective-permute-start | bytes 393224 | tf_op jit(solution)/shard_map/ppermute | solution.py:194
  13.1 8.9 %collective-permute-start.1 = (bf16[64,1024]{1,0:T(8,128)(2,1)S(1)}, bf16[64,1024]{1,0:T(8,128)(2,1)S(1)}, u32[]{:S(2)}, u32[]{:S(2)}) collective-permute-start(bf16[64,1024]{1,0:T(8,128)(2,1)S(1)} %collective-permute-done.refs_1_), channel_id=1, source_target_pairs={{0,16},{16,0},{1,17},{17,1},{2,18},{18,2},{3,19},{19,3},{4,20},{20... | collective-permute-start | bytes 393224 | tf_op jit(solution)/shard_map/ppermute | solution.py:201
  22.2 6.1 %collective-permute-start.6 = (bf16[128,128]{1,0:T(8,128)(2,1)S(1)}, bf16[128,128]{1,0:T(8,128)(2,1)S(1)}, u32[]{:S(2)}, u32[]{:S(2)}) collective-permute-start(bf16[128,128]{1,0:T(8,128)(2,1)S(1)} %sides.3.refs_0_), channel_id=1, source_target_pairs={{0,12},{4,8},{8,4},{12,0},{1,13},{5,9},{9,5},{13,1},{2,14},{6,10},... | collective-permute-start | bytes 98312 | tf_op jit(solution)/shard_map/ppermute | solution.py:194
  24.8 4.8 %collective-permute-start.7 = (bf16[128,128]{1,0:T(8,128)(2,1)S(1)}, bf16[128,128]{1,0:T(8,128)(2,1)S(1)}, u32[]{:S(2)}, u32[]{:S(2)}) collective-permute-start(bf16[128,128]{1,0:T(8,128)(2,1)S(1)} %sides.3.refs_0_), channel_id=1, source_target_pairs={{0,8},{4,12},{8,0},{12,4},{1,9},{5,13},{9,1},{13,5},{2,10},{6,14},... | collective-permute-start | bytes 98312 | tf_op jit(solution)/shard_map/ppermute | solution.py:194
  25.3 4.3 %collective-permute-start.8 = (bf16[128,128]{1,0:T(8,128)(2,1)S(1)}, bf16[128,128]{1,0:T(8,128)(2,1)S(1)}, u32[]{:S(2)}, u32[]{:S(2)}) collective-permute-start(bf16[128,128]{1,0:T(8,128)(2,1)S(1)} %sides.3.refs_0_), channel_id=1, source_target_pairs={{0,4},{4,0},{8,12},{12,8},{1,5},{5,1},{9,13},{13,9},{2,6},{6,2},{1... | collective-permute-start | bytes 98312 | tf_op jit(solution)/shard_map/ppermute | solution.py:194
  31.2 3.8 %collective-permute-start.10 = (f32[32,128]{1,0:T(8,128)S(1)}, f32[32,128]{1,0:T(8,128)S(1)}, u32[]{:S(2)}, u32[]{:S(2)}) collective-permute-start(f32[32,128]{1,0:T(8,128)S(1)} %get-tuple-element.39), channel_id=1, source_target_pairs={{0,2},{1,3},{2,0},{3,1},{4,6},{5,7},{6,4},{7,5},{8,10},{9,11},{10,... | collective-permute-start | bytes 49160 | tf_op jit(solution)/shard_map/ppermute | solution.py:310
  32.8 3.2 %collective-permute-start.11 = (f32[32,128]{1,0:T(8,128)S(1)}, f32[32,128]{1,0:T(8,128)S(1)}, u32[]{:S(2)}, u32[]{:S(2)}) collective-permute-start(f32[32,128]{1,0:T(8,128)S(1)} %get-tuple-element.40), channel_id=1, source_target_pairs={{0,3},{1,2},{2,1},{3,0},{4,7},{5,6},{6,5},{7,4},{8,11},{9,10},{10,... | collective-permute-start | bytes 49160 | tf_op jit(solution)/shard_map/ppermute | solution.py:310
  33.3 1.5 %collective-permute-start.9 = (f32[32,80]{1,0:T(8,128)S(1)}, f32[32,80]{1,0:T(8,128)S(1)}, u32[]{:S(2)}, u32[]{:S(2)}) collective-permute-start(f32[32,80]{1,0:T(8,128)S(1)} %get-tuple-element.38), channel_id=1, source_target_pairs={{0,1},{1,0},{2,3},{3,2},{4,5},{5,4},{6,7},{7,6},{8,9},{9,8},{10,11... | collective-permute-start | bytes 30728 | tf_op jit(solution)/shard_map/ppermute | solution.py:310
